TPU v7x, 256 devices: a whole 4x4x8 slice. The times are simulated.
256 devices in a mesh: section: 8 (over y, z_lo), dp: 32 (over z_hi, x, core).
Axes of the slice: x: 4, y: 4, z: 8 (z_hi: 4, z_lo: 2; z = z_hi * 2 + z_lo), core: 2. Of those that a mesh axis runs over, the one named last changes fastest.
Arguments:
- pre_norm: bfloat16 [2, 32, 48, 4096], P(None, 'dp'), may hold values from -12 to 12
- norm_gain: float32 [4096], replicated, may hold values from 0.3 to 3
- queries: bfloat16 [8, 2, 32, 128, 2048], P('section', None, 'dp'), may hold values from -24 to 24
- keys: bfloat16 [8, 2, 32, 48, 2048], P('section', None, 'dp'), may hold values from -6 to 6
- values: bfloat16 [8, 2, 32, 48, 2048], P('section', None, 'dp'), may hold values from -6 to 6
- head_grad: bfloat16 [8, 2, 32, 128, 2048], P('section', None, 'dp'), may hold values from -2 to 2
- key_weight: bfloat16 [8, 4096, 2048], P('section', 'dp'), may hold values from -0.09375 to 0.09375
- value_weight: bfloat16 [8, 4096, 2048], P('section', 'dp'), may hold values from -0.09375 to 0.09375
Outputs:
- query_grad: bfloat16 [8, 2, 32, 128, 2048], P('section', None, 'dp')
- key_weight_grad: bfloat16 [8, 4096, 2048], P('section', 'dp')
- value_weight_grad: bfloat16 [8, 4096, 2048], P('section', 'dp')
- encoder_grad: bfloat16 [2, 32, 48, 4096], P(None, 'dp')
- gain_grad: float32 [4096], replicated
All inputs are finite; a program needn't handle non-finite values.
Results may differ from a plain program's by a relative error of at most 0.02.
Values may be sent and summed in bfloat16 or wider, within the bound.
No kernel may reach another device: no remote copies, remote signals or barrier semaphores. Data moves between devices by JAX's collectives and lax.ppermute only.
A program may use at most 128 MiB of HBM per device.

v0:
```python
import functools

import jax
import jax.numpy as jnp
from jax import lax
from jax.experimental import pallas as pl
from jax.experimental.pallas import tpu as pltpu
from jax.sharding import Mesh, PartitionSpec as P

EPS = 1e-06
BF = jnp.bfloat16
F32 = jnp.float32
SEC = ("y", "zlo")
ZC = ("zhi", "core")
SRC = 48
D = 4096
HD = 2048
COLS = 512
PIECE = 6
VMEM = pl.BlockSpec(memory_space=pltpu.VMEM)
HBM = pl.BlockSpec(memory_space=pl.ANY)
SMEM = pl.BlockSpec(memory_space=pltpu.SMEM)


def shape(dims, dtype=BF):
    return jax.ShapeDtypeStruct(dims, dtype)


def params(mib=60):
    return pltpu.CompilerParams(vmem_limit_bytes=mib * 2**20)


def cost():
    return pl.CostEstimate(flops=0, bytes_accessed=0, transcendentals=0)


def rows_dot(a, b):
    return lax.dot_general(a, b, (((1,), (1,)), ((), ())), preferred_element_type=F32)


def columns_dot(a, b):
    return lax.dot_general(a, b, (((0,), (0,)), ((), ())), preferred_element_type=F32)


def heads_kernel(first, q_ref, k_ref, v_ref, g_ref, *refs):
    if first:
        key_w, value_w, local_ref, grads_ref, stack_ref, sems = refs
        key_out = grads_ref.at[:, pl.ds(0, HD)]
        value_out = grads_ref.at[:, pl.ds(HD, HD)]
        stacked = [
            pltpu.make_async_copy(w.at[0], stack_ref.at[i], sems.at[i])
            for i, w in enumerate((key_w, value_w))
        ]
        for copy in stacked:
            copy.start()
    else:
        _, local_ref, grads_ref = refs
        key_out, value_out = grads_ref.at[0], grads_ref.at[1]
    src = k_ref.shape[0]
    lane = lax.broadcasted_iota(jnp.int32, (src, 256), 1) // 64
    masks = [lane == h for h in range(4)]

    def spread(block):
        zero = jnp.zeros_like(block)
        return jnp.concatenate([jnp.where(m, block, zero) for m in masks], axis=0)

    def diagonal(wide):
        out = wide[:src]
        for h in range(1, 4):
            out = jnp.where(masks[h], wide[h * src : (h + 1) * src], out)
        return out

    for part in range(HD // 256):
        at = pl.ds(part * 256, 256)
        q, g = q_ref[:, at], g_ref[:, at]
        k, v = spread(k_ref[:, at]), spread(v_ref[:, at])
        scores = rows_dot(k, q).reshape(4, src, -1)
        exponent = jnp.exp(scores - jnp.max(scores, axis=1, keepdims=True))
        probs = exponent * (1.0 / jnp.sum(exponent, axis=1, keepdims=True))
        slopes = rows_dot(v, g).reshape(4, src, -1)
        center = jnp.sum(probs * slopes, axis=1, keepdims=True)
        score_grad = (probs * (slopes - center)).astype(BF).reshape(4 * src, -1)
        probs = probs.astype(BF).reshape(4 * src, -1)
        value = jnp.dot(probs, g, preferred_element_type=F32)
        key = jnp.dot(score_grad, q, preferred_element_type=F32)
        key_out[:, at] = diagonal(key).astype(BF)
        value_out[:, at] = diagonal(value).astype(BF)
        local_ref[:, at] = columns_dot(score_grad, k).astype(BF)
    if first:
        for copy in stacked:
            copy.wait()


def heads(q, k, v, g, m, *others):
    tgt = q.shape[3]

    def row(n):
        return pl.BlockSpec((None, None, None, n, HD), lambda i: (0, m, 0, 0, 0))

    if m == 0:
        grads = pl.BlockSpec((SRC, D), lambda i: (0, 0))
        outs = [(grads, shape((SRC, D))), (HBM, shape((2, 128, HD)))]
        scratch = [pltpu.SemaphoreType.DMA((2,))]
    else:
        grads = pl.BlockSpec((2, SRC, HD), lambda i: (0, 0, 0))
        outs, scratch = [(grads, shape((2, SRC, HD)))], []
    return pl.pallas_call(
        functools.partial(heads_kernel, m == 0),
        grid=(1,),
        in_specs=[row(tgt), row(SRC), row(SRC), row(tgt)] + [HBM] * len(others),
        out_specs=[row(tgt)] + [spec for spec, _ in outs],
        out_shape=[shape(q.shape)] + [struct for _, struct in outs],
        input_output_aliases={} if m == 0 else {4: 0},
        scratch_shapes=scratch,
        compiler_params=params(),
        cost_estimate=cost(),
        name="heads",
    )(q, k, v, g, *others)


def memory_kernel(place_ref, pre_ref, gain_ref, out_ref):
    rows, features = pre_ref.shape
    squares = jnp.zeros((rows, 128), F32)
    for n in range(features // 128):
        part = pre_ref[:, pl.ds(n * 128, 128)].astype(F32)
        squares += part * part
    inverse = lax.rsqrt(jnp.sum(squares, axis=-1, keepdims=True) / features + EPS)
    for z in range(4):
        for c in range(2):
            at = pl.ds(pl.multiple_of(((z * 4 + place_ref[4]) * 2 + c) * 128, 128), 128)
            hidden = pre_ref[:, at].astype(F32)
            out_ref[z * 2 + c] = (hidden * inverse * gain_ref[:, at]).astype(BF)


def memory_blocks(place, pre, gain):
    rows = pre.shape[0]
    return pl.pallas_call(
        memory_kernel,
        in_specs=[SMEM, VMEM, VMEM],
        out_specs=VMEM,
        out_shape=shape((8, rows, 128)),
        compiler_params=params(),
        cost_estimate=cost(),
        name="memory",
    )(place, pre, gain)


def token_blocks(place_ref):
    z, c = place_ref[0], place_ref[1]
    index = []
    for core in (c, 1 - c):
        for step in (0, 3, 1, 2):
            index.append(lax.rem(z + step, 4) * 2 + core)
    return index


def start_all(pairs, sems, first=0):
    copies = [pltpu.make_async_copy(a, b, sems.at[first + i]) for i, (a, b) in enumerate(pairs)]
    for copy in copies:
        copy.start()
    return copies


def wait_all(copies):
    for copy in copies:
        copy.wait()


def lanes(index):
    return pl.ds(pl.multiple_of(index * 128, 128), 128)


def part(ref, where):
    kind, index = where
    if kind == "pair":
        return ref.at[index]
    if kind == "half":
        return ref.at[:, pl.ds(index * HD, HD)]
    return ref


def return_kernel(m, wheres, place_ref, *refs):
    weights, cols, grads = refs[:8], refs[8:12], refs[12:28]
    out_ref, gain_ref, grad_s, weight_s, cols_s, acc_s, out_s, sems = refs[-8:]
    x, y = place_ref[2], place_ref[4]
    place = token_blocks(place_ref)
    pairs = []
    for i, (ref, where) in enumerate(zip(grads, wheres)):
        half, zc = i // 8, place[i % 8]
        pairs.append((part(ref, where), grad_s.at[zc, :, pl.ds(half * HD, HD)]))
    for r in range(4):
        for half in range(2):
            ref = weights[2 * r + half]
            ref = ref.at[half] if len(ref.shape) == 3 else ref
            pairs.append((ref, weight_s.at[r, :, pl.ds(half * HD, HD)]))
    for r in range(4):
        at = lanes(lax.rem(y + r + 4 - x, 4))
        pairs.append((cols[r].at[:, m], cols_s.at[:, :, at]))
    copies = start_all(pairs, sems)
    wait_all(copies[:20])
    grad = grad_s[...].reshape(8 * SRC, D)
    for n in range(2):
        if n == 1:
            wait_all(copies[20:])
        weight = weight_s[pl.ds(2 * n, 2)].reshape(256, D)
        acc_s[:, pl.ds(256 * n, 256)] = rows_dot(grad, weight)
    result = acc_s[...]
    columns = cols_s[...].reshape(8 * SRC, COLS).astype(F32)
    gain = jnp.sum(result * columns, axis=0, keepdims=True)
    for r in range(4):
        block = gain[:, r * 128 : (r + 1) * 128]
        gain_ref[:, lanes(lax.rem(x + r, 4))] = jnp.broadcast_to(block, (8, 128))
    rows = 8 * SRC
    target = lax.broadcasted_iota(jnp.int32, (rows, rows), 0)
    source = lax.broadcasted_iota(jnp.int32, (rows, rows), 1)
    rank, rest = target // SRC, target % SRC
    wanted = (rest // PIECE) * SRC + rank * PIECE + rest % PIECE
    move = (source == wanted).astype(F32).astype(BF)
    moved = jnp.dot(move, result.astype(BF), preferred_element_type=F32)
    out_s[...] = moved.astype(BF).reshape(8, SRC, COLS)
    wait_all(start_all([(out_s, out_ref.at[:, m])], sems))


def return_blocks(m, place, weights, columns, grads, *before):
    refs, wheres = zip(*grads)
    return pl.pallas_call(
        functools.partial(return_kernel, m, wheres),
        in_specs=[SMEM] + [HBM] * (28 + len(before)),
        out_specs=[HBM, VMEM],
        out_shape=[shape((8, 2, SRC, COLS)), shape((8, COLS), F32)],
        input_output_aliases={29: 0} if before else {},
        scratch_shapes=[
            pltpu.VMEM((8, SRC, D), BF),
            pltpu.VMEM((4, 128, D), BF),
            pltpu.VMEM((8, SRC, COLS), BF),
            pltpu.VMEM((8 * SRC, COLS), F32),
            pltpu.VMEM((8, SRC, COLS), BF),
            pltpu.SemaphoreType.DMA((28,)),
        ],
        compiler_params=params(),
        cost_estimate=cost(),
        name="returned",
    )(place, *weights, *columns, *refs, *before)


def weight_kernel(wheres, place_ref, *refs):
    cols, grads, outs = refs[:4], refs[4:20], refs[20:24]
    grad_s, cols_s, sems = refs[24:]
    x, y = place_ref[2], place_ref[4]
    place = token_blocks(place_ref)
    pairs = []
    for r in range(4):
        at = lanes(lax.rem(y + r + 4 - x, 4))
        for m in range(2):
            pairs.append((cols[r].at[:, m], cols_s.at[m, :, :, at]))
    for i, (ref, where) in enumerate(zip(grads, wheres)):
        pairs.append((part(ref, where), grad_s.at[i // 8, place[i % 8]]))
    wait_all(start_all(pairs, sems))
    columns = cols_s[...].reshape(16 * SRC, COLS)
    for n in range(HD // 512):
        at = pl.ds(n * 512, 512)
        grad = grad_s[:, :, :, at].reshape(16 * SRC, 512)
        partial = columns_dot(columns, grad).astype(BF)
        for r in range(4):
            outs[r][:, at] = partial[r * 128 : (r + 1) * 128]


def weight_blocks(place, columns, grads):
    refs, wheres = zip(*grads)
    return pl.pallas_call(
        functools.partial(weight_kernel, wheres),
        in_specs=[SMEM] + [HBM] * 20,
        out_specs=[VMEM] * 4,
        out_shape=[shape((128, HD))] * 4,
        scratch_shapes=[
            pltpu.VMEM((2, 8, SRC, HD), BF),
            pltpu.VMEM((2, 8, SRC, COLS), BF),
            pltpu.SemaphoreType.DMA((24,)),
        ],
        compiler_params=params(),
        cost_estimate=cost(),
        name="weights",
    )(place, *columns, *refs)


def pick_rows(rows, cols, wanted, keep):
    target = lax.broadcasted_iota(jnp.int32, (rows, cols), 0)
    source = lax.broadcasted_iota(jnp.int32, (rows, cols), 1)
    return ((source == wanted(target)) & keep(target)).astype(F32).astype(BF)


def sum_kernel(place_ref, layers_ref, gain0_ref, gain1_ref, out_ref):
    moved = jnp.zeros((128, COLS), F32)
    for m in range(2):
        total = jnp.sum(layers_ref[:, m].astype(F32), axis=0).astype(BF)
        move = pick_rows(
            128,
            SRC,
            lambda t: (t // 16) * PIECE + t % 16 - m * PIECE,
            lambda t: (t % 16 >= m * PIECE) & (t % 16 < (m + 1) * PIECE),
        )
        moved += jnp.dot(move, total, preferred_element_type=F32)
    blocks = [lanes(lax.rem(place_ref[2] + r, 4)) for r in range(4)]
    gain = jnp.concatenate([(gain0_ref[:, at] + gain1_ref[:, at])[:1] for at in blocks], axis=1)
    high = gain.astype(BF).astype(F32)
    row = lax.broadcasted_iota(jnp.int32, (128, COLS), 0) % 16
    moved = jnp.where(row == 12, high, jnp.where(row == 13, gain - high, moved))
    out_ref[...] = moved.astype(BF).reshape(8, 16, COLS)


def sum_layers(place, layers, gains):
    return pl.pallas_call(
        sum_kernel,
        in_specs=[SMEM] + [VMEM] * 3,
        out_specs=VMEM,
        out_shape=shape((8, 16, COLS)),
        compiler_params=params(),
        cost_estimate=cost(),
        name="layers",
    )(place, layers, *gains)


def encoder_kernel(
    place_ref, own_ref, pre_ref, gain_ref, query_ref, out_ref, query_out, full_s, sems
):
    handed = start_all([(query_ref, query_out)], sems)
    for z in range(4):
        for c in range(2):
            for x in range(4):
                at = (z * 4 + lax.rem(place_ref[2] + x, 4)) * 2 + c
                full_s[:, lanes(at)] = own_ref[z * 2 + c, :, x * 128 : (x + 1) * 128]
    own = full_s[...].astype(F32)
    rank = place_ref[3]
    pick = pick_rows(
        16,
        2 * SRC,
        lambda t: (t // PIECE) * SRC + rank * PIECE + t % PIECE,
        lambda t: t < 2 * PIECE,
    )
    hidden = jnp.dot(pick, pre_ref[...], preferred_element_type=F32)
    inverse = lax.rsqrt(jnp.mean(hidden * hidden, axis=-1, keepdims=True) + EPS)
    scaled = own * gain_ref[...]
    row_mean = jnp.mean(hidden * scaled, axis=-1, keepdims=True)
    mine = inverse * scaled - hidden * (inverse * inverse * inverse * row_mean)
    row = lax.broadcasted_iota(jnp.int32, (16, D), 0)
    packed = jnp.where(row < 2 * PIECE, mine, own).astype(BF)
    for s in range(8):
        out_ref[s] = packed
    wait_all(handed)


def encoder_rows(place, own, pre, gain, query):
    return pl.pallas_call(
        encoder_kernel,
        in_specs=[SMEM, VMEM, VMEM, VMEM, HBM],
        out_specs=[VMEM, HBM],
        out_shape=[shape((8, 16, D)), shape(query.shape)],
        scratch_shapes=[pltpu.VMEM((16, D), BF), pltpu.SemaphoreType.DMA((1,))],
        compiler_params=params(),
        cost_estimate=cost(),
        name="encoder",
    )(place, own, pre, gain, query)


def finish_kernel(packed_ref, gain_ref, out_ref, gain_out_ref):
    packed = packed_ref[...].reshape(128, D)
    move = pick_rows(
        2 * SRC,
        128,
        lambda t: ((t % SRC) // PIECE) * 16 + (t // SRC) * PIECE + t % PIECE,
        lambda t: t >= 0,
    )
    out_ref[...] = jnp.dot(move, packed, preferred_element_type=F32).astype(BF)
    target = lax.broadcasted_iota(jnp.int32, (16, 128), 1) % 16
    ones = ((target == 12) | (target == 13)).astype(F32).astype(BF)
    gain = jnp.dot(ones, packed, preferred_element_type=F32)
    gain_out_ref[...] = gain[:1] / gain_ref[...]


def finish(packed, gain):
    return pl.pallas_call(
        finish_kernel,
        in_specs=[VMEM] * 2,
        out_specs=[VMEM, VMEM],
        out_shape=[shape((2 * SRC, D)), shape((1, D), F32)],
        compiler_params=params(),
        cost_estimate=cost(),
        name="finish",
    )(packed, gain)


def add_kernel(a_ref, b_ref, c_ref, d_ref, out_ref, terms_s, sems):
    refs = (a_ref, b_ref, c_ref, d_ref)
    wait_all(start_all([(ref, terms_s.at[i]) for i, ref in enumerate(refs)], sems))
    total = terms_s[0].astype(F32) + terms_s[1].astype(F32)
    total += terms_s[2].astype(F32) + terms_s[3].astype(F32)
    out_ref[...] = total.astype(BF)


def add_blocks(*terms):
    dims = terms[0].shape
    return pl.pallas_call(
        add_kernel,
        in_specs=[HBM] * 4,
        out_specs=VMEM,
        out_shape=shape(dims),
        scratch_shapes=[pltpu.VMEM((4,) + dims, BF), pltpu.SemaphoreType.DMA((4,))],
        compiler_params=params(),
        cost_estimate=cost(),
        name="add",
    )(*terms)


def shift(value, axis, step):
    return lax.ppermute(value, axis, [(i, (i + step) % 4) for i in range(4)])


def swap(value):
    return lax.ppermute(value, "core", [(0, 1), (1, 0)])


def after(value, *others):
    return lax.optimization_barrier((value,) + others)[0]


def exchange(value, axes):
    return lax.all_to_all(value, axes, split_axis=0, concat_axis=0, tiled=True)


class Chain:
    def __init__(self):
        self.last = ()

    def __call__(self, value, move, *others):
        result = move(after(value, *self.last, *others))
        self.last = (result,)
        return result


def body(pre_norm, norm_gain, queries, keys, values, head_grad, key_weight, value_weight):
    batches, _, source_n, features = pre_norm.shape
    rows = batches * source_n
    place = jnp.stack(
        [lax.axis_index(name) for name in ("zhi", "core", "x", SEC, "y")]
    ).astype(jnp.int32)
    gain = norm_gain.reshape(1, features)
    hidden = pre_norm.reshape(rows, features)
    side = Chain()

    local, own0, stacked = heads(queries, keys, values, head_grad, 0, key_weight, value_weight)
    minus0, plus0 = shift(own0, "zhi", 1), shift(own0, "zhi", -1)
    weight_m, weight_p = shift(stacked, "x", 1), shift(stacked, "x", -1)
    own0_s = side(own0, swap)
    local, own1 = heads(after(queries, own0), keys, values, head_grad, 1, local)
    own1_s = side(own1, swap)
    blocks = memory_blocks(place, after(hidden, own1), gain)
    quarter = exchange(blocks, ZC).reshape(8, batches, source_n, 128)
    minus0, plus0, weight_m, weight_p, own1, own1_s, quarter = lax.optimization_barrier(
        (minus0, plus0, weight_m, weight_p, own1, own1_s, quarter)
    )

    far0 = shift(minus0, "zhi", 1)
    plus1 = shift(own1, "zhi", -1)
    key_2, value_2 = shift(weight_m[0], "x", 1), shift(weight_p[1], "x", -1)
    minus0_s = side(minus0, swap)
    quarter = after(quarter, key_2, value_2)
    quarter_p, quarter_2, quarter_m = (shift(quarter, "y", -r) for r in (1, 2, 3))
    far0, plus0, plus1, minus0_s, quarter_p, quarter_2, quarter_m = lax.optimization_barrier(
        (far0, plus0, plus1, minus0_s, quarter_p, quarter_2, quarter_m)
    )
    columns = (quarter, quarter_p, quarter_2, quarter_m)
    weights = (stacked, stacked, weight_p, weight_p, key_2, value_2, weight_m, weight_m)

    value1m = shift(after(own1[1], far0), "zhi", 1)
    value1f = shift(plus1[1], "zhi", -1)
    far0_s, plus0_s, plus1_s = swap(far0), swap(plus0), swap(plus1)
    blocks0 = (own0, minus0, plus0, far0, own0_s, minus0_s, plus0_s, far0_s)
    keys0, values0 = ([(b, ("half", i)) for b in blocks0] for i in range(2))
    returned, gain0 = return_blocks(0, place, weights, columns, keys0 + values0)
    value1m, value1f, returned, plus1_s = lax.optimization_barrier(
        (value1m, value1f, returned, plus1_s)
    )

    key1m = shift(after(own1[0], value1m), "zhi", 1)
    key1f = shift(after(plus1[0], value1f), "zhi", -1)
    value1m_s, value1f_s = swap(value1m), swap(value1f)
    whole = ("whole", 0)

    def second(i, minus, far, minus_s, far_s):
        at = ("pair", i)
        first = [(own1, at), (minus, whole), (plus1, at), (far, whole)]
        return first + [(own1_s, at), (minus_s, whole), (plus1_s, at), (far_s, whole)]

    values1 = second(1, value1m, value1f, value1m_s, value1f_s)
    value_part = weight_blocks(place, columns, values0 + values1)
    value_in = [shift(value_part[r], "x", r) for r in (2, 1, 3)]
    key1m, key1f = lax.optimization_barrier((key1m, key1f, value_part[0]))[:2]

    key1m_s, key1f_s = swap(key1m), swap(key1f)
    keys1 = second(0, key1m, key1f, key1m_s, key1f_s)
    returned, gain1 = return_blocks(1, place, weights, columns, keys1 + values1, returned)
    layers = exchange(returned, SEC)
    query_in = lax.ppermute(
        after(local, key1m_s, key1f_s), SEC, [(s, s - 1) for s in range(1, 8)]
    )
    gain_part = gain0 + gain1
    gain_part += lax.ppermute(gain_part, "x", [(0, 1), (1, 0), (2, 3), (3, 2)])
    gain_other = lax.ppermute(gain_part, "x", [(0, 2), (2, 0), (1, 3), (3, 1)])
    columns = lax.optimization_barrier((*columns, returned))[:4]
    key_part = weight_blocks(place, columns, keys0 + keys1)
    sums = sum_layers(place, after(layers, key_part[0], *value_in), [gain_part, gain_other])
    own = exchange(sums, ZC)
    key_from = lax.optimization_barrier((*key_part, sums, *value_in))[:4]
    key_in = [shift(key_from[r], "x", r) for r in (2, 1, 3)]
    packed, query_grad = encoder_rows(place, own, hidden, gain, query_in)
    packed = exchange(packed, SEC)

    grad_value = add_blocks(value_part[0], *value_in)
    grad_key = add_blocks(key_part[0], *key_in)
    encoder_grad, gain_grad = finish(after(packed, *key_in), gain)
    return (
        query_grad,
        grad_key[None],
        grad_value[None],
        encoder_grad.reshape(pre_norm.shape),
        gain_grad.reshape(features),
    )


def solution(mesh):
    grid = Mesh(mesh.devices.reshape(4, 2, 4, 4, 2), ("y", "zlo", "zhi", "x", "core"))
    dp = ("zhi", "x", "core")
    return jax.shard_map(
        body,
        mesh=grid,
        in_specs=(
            P(None, dp, None, None),
            P(),
            P(SEC, None, dp, None, None),
            P(SEC, None, dp, None, None),
            P(SEC, None, dp, None, None),
            P(SEC, None, dp, None, None),
            P(SEC, dp, None),
            P(SEC, dp, None),
        ),
        out_specs=(
            P(SEC, None, dp, None, None),
            P(SEC, dp, None),
            P(SEC, dp, None),
            P(None, dp, None, None),
            P(),
        ),
        check_vma=False,
    )
```

profile of v0, /device:TPU:8, one launch (start us, length us, event | category | flops | bytes accessed | tf_op | source)
XLA Modules:
  0.0 285.0 jit_solution(12829843093317665323)
XLA Ops:
  0.6 35.2 %heads.2 = (bf16[1,2,1,128,2048]{4,3,2,1,0:T(8,128)(2,1)}, bf16[48,4096]{1,0:T(8,128)(2,1)}, bf16[2,128,2048]{2,1,0:T(8,128)(2,1)}) custom-call(bf16[1,2,1,128,2048]{4,3,2,1,0:T(8,128)(2,1)} %q_ref.2, bf16[1,2,1,48,2048]{4,3,2,1,0:T(8,128)(2,1)} %k_ref.3, bf16[1,2,1,48,2048]{4,3,2,1,0:T(8,128)(2,1)} %v_ref.3, bf16[1,2,1,128,2048]{4,3,2,1,0:T(8,128)(2,1)} %g_ref.3, ...), custom_call_target="tpu_custom_call" | custom-call | tf_op jit(solution)/shard_map/heads/pallas_call | solution.py:107
  35.8 2.8 collective-permute-start.3
  38.7 6.3 %collective-permute-start.1 = (bf16[48,4096]{1,0:T(8,128)(2,1)}, bf16[48,4096]{1,0:T(8,128)(2,1)S(1)}, u32[]{:S(2)}, u32[]{:S(2)}) collective-permute-start(bf16[48,4096]{1,0:T(8,128)(2,1)} %get-tuple-element.65.refs_12_.refs_20_.refs_4_), channel_id=1, source_target_pairs={{0,24},{8,0},{16,8},{24,16},{1,25},{9,1},{17,9},{25,17},{2,26},{10... | collective-permute-start | bytes 1179656 | tf_op jit(solution)/shard_map/ppermute | solution.py:415
  45.0 4.6 %heads.3 = (bf16[1,2,1,128,2048]{4,3,2,1,0:T(8,128)(2,1)}, bf16[2,48,2048]{2,1,0:T(8,128)(2,1)}) custom-call(bf16[1,2,1,128,2048]{4,3,2,1,0:T(8,128)(2,1)} %q_ref.2, bf16[1,2,1,48,2048]{4,3,2,1,0:T(8,128)(2,1)} %k_ref.3, bf16[1,2,1,48,2048]{4,3,2,1,0:T(8,128)(2,1)} %v_ref.3, bf16[1,2,1,128,2048]{4,3,2,1,0:T(8,128)(2,1)} %g_ref.3, ...), custom_call_target="tpu_custom_call", output_to_operand_aliasing={{0}: (4, {})} | custom-call | tf_op jit(solution)/shard_map/heads/pallas_call | solution.py:107
  52.5 19.1 %all_to_all.20 = bf16[8,96,128]{2,1,0:T(8,128)(2,1)S(1)} all-to-all(bf16[8,96,128]{2,1,0:T(8,128)(2,1)} %memory.1), channel_id=1, replica_groups=mesh['y'=4,'zlo'=2,'zhi'=4,'x'=4,'core'=2] {'zhi','core'}, dimensions={0} | all-to-all | bytes 393216 | tf_op jit(solution)/shard_map/all_to_all | solution.py:427
  73.9 2.5 collective-permute-start.7
  77.1 3.6 %collective-permute-start.9 = (bf16[2,48,2048]{2,1,0:T(8,128)(2,1)S(1)}, bf16[2,48,2048]{2,1,0:T(8,128)(2,1)S(1)}, u32[]{:S(2)}, u32[]{:S(2)}) collective-permute-start(bf16[2,48,2048]{2,1,0:T(8,128)(2,1)S(1)} %copy-done.2), channel_id=1, source_target_pairs={{0,24},{8,0},{16,8},{24,16},{1,25},{9,1},{17,9},{25,17},{2,26},{10... | collective-permute-start | bytes 1179656 | tf_op jit(solution)/shard_map/ppermute | solution.py:415
  80.7 6.9 %collective-permute-done.6.refs_4_ = bf16[128,2048]{1,0:T(8,128)(2,1)S(1)} collective-permute-done((bf16[128,2048]{1,0:T(8,128)(2,1)S(1)}, bf16[128,2048]{1,0:T(8,128)(2,1)S(1)}, u32[]{:S(2)}, u32[]{:S(2)}) %collective-permute-start.6) | collective-permute-done | bytes 524320 | tf_op jit(solution)/shard_map/ppermute | solution.py:415
  90.3 2.5 collective-permute-start.11
  93.5 2.1 collective-permute-done.8.refs_15_.refs_23_.refs_7_
  96.0 2.3 collective-permute-done.12.refs_10_.refs_2_
  103.5 2.1 collective-permute-start.15
  107.1 8.8 %returned.2 = (bf16[8,2,48,512]{3,2,1,0:T(8,128)(2,1)}, f32[8,512]{1,0:T(8,128)}) custom-call(s32[5]{0:T(128)} %stack.23.place_ref, bf16[2,128,2048]{2,1,0:T(8,128)(2,1)} %get-tuple-element.64.refs_0_.refs_1_, bf16[2,128,2048]{2,1,0:T(8,128)(2,1)} %get-tuple-element.64.refs_0_.refs_1_, bf16[2,128,2048]{2,1,0:T(8,128)(2,1)} %copy-done, ...), custom_call_target="tpu_custom_call" | custom-call | tf_op jit(solution)/shard_map/returned/pallas_call | solution.py:226
  116.6 2.2 collective-permute-start.20
  120.9 6.1 %weights.2 = (bf16[128,2048]{1,0:T(8,128)(2,1)}, bf16[128,2048]{1,0:T(8,128)(2,1)}, bf16[128,2048]{1,0:T(8,128)(2,1)}, bf16[128,2048]{1,0:T(8,128)(2,1)}) custom-call(s32[5]{0:T(128)} %stack.23.place_ref, bf16[8,2,48,128]{3,2,1,0:T(8,128)(2,1)} %bitcast.30, bf16[8,2,48,128]{3,2,1,0:T(8,128)(2,1)} %copy-done.17, bf16[8,2,48,128]{3,2,1,0:T(8,128)(2,1)} %copy-done.16, ...), custom_call_target="tpu_custom_call" | custom-call | tf_op jit(solution)/shard_map/weights/pallas_call | solution.py:270
  128.2 8.7 %collective-permute-start.23 = (bf16[48,2048]{1,0:T(8,128)(2,1)S(1)}, bf16[48,2048]{1,0:T(8,128)(2,1)S(1)}, u32[]{:S(2)}, u32[]{:S(2)}) collective-permute-start(bf16[48,2048]{1,0:T(8,128)(2,1)S(1)} %collective-permute-done.19.refs_13_), channel_id=1, source_target_pairs={{0,1},{1,0},{2,3},{3,2},{4,5},{5,4},{6,7},{7,6},{8,9},{9,8},{10,11... | collective-permute-start | bytes 589832 | tf_op jit(solution)/shard_map/ppermute | solution.py:419
  139.6 8.8 %returned.3 = (bf16[8,2,48,512]{3,2,1,0:T(8,128)(2,1)}, f32[8,512]{1,0:T(8,128)}) custom-call(s32[5]{0:T(128)} %stack.23.place_ref, bf16[2,128,2048]{2,1,0:T(8,128)(2,1)} %get-tuple-element.64.refs_0_.refs_1_, bf16[2,128,2048]{2,1,0:T(8,128)(2,1)} %get-tuple-element.64.refs_0_.refs_1_, ...), custom_call_target="tpu_custom_call", output_to_operand_aliasing={{0}: (29, {})} | custom-call | tf_op jit(solution)/shard_map/returned/pallas_call | solution.py:226
  148.5 7.3 %all-to-all-start.1 = ((bf16[8,2,48,512]{3,2,1,0:T(8,128)(2,1)}), bf16[8,2,48,512]{3,2,1,0:T(8,128)(2,1)S(1)}, u32[]{:S(2)}, u32[]{:S(2)}) async-start(bf16[8,2,48,512]{3,2,1,0:T(8,128)(2,1)} %get-tuple-element.98), calls=%async_computation.1 | async-start | bytes 1572864 | tf_op jit(solution)/shard_map/all_to_all | solution.py:427
  155.8 3.4 %collective-permute-start.30 = (bf16[1,2,1,128,2048]{4,3,2,1,0:T(8,128)(2,1)S(1)}, bf16[1,2,1,128,2048]{4,3,2,1,0:T(8,128)(2,1)S(1)}, u32[]{:S(2)}, u32[]{:S(2)}) collective-permute-start(bf16[1,2,1,128,2048]{4,3,2,1,0:T(8,128)(2,1)S(1)} %copy-done.22), channel_id=1, source_target_pairs={{32,0},{64,32},{96,64},{128,96},{160,128},{192,160},{224,192},{33,... | collective-permute-start | bytes 3145736 | tf_op jit(solution)/shard_map/ppermute | solution.py:503
  164.2 20.8 %collective-permute-done.28 = f32[8,512]{1,0:T(8,128)S(1)} collective-permute-done((f32[8,512]{1,0:T(8,128)S(1)}, f32[8,512]{1,0:T(8,128)S(1)}, u32[]{:S(2)}, u32[]{:S(2)}) %collective-permute-start.28) | collective-permute-done | bytes 16416 | tf_op jit(solution)/shard_map/ppermute | solution.py:507
  185.9 6.1 %weights.3 = (bf16[128,2048]{1,0:T(8,128)(2,1)}, bf16[128,2048]{1,0:T(8,128)(2,1)}, bf16[128,2048]{1,0:T(8,128)(2,1)}, bf16[128,2048]{1,0:T(8,128)(2,1)}) custom-call(s32[5]{0:T(128)} %stack.23.place_ref, bf16[8,2,48,128]{3,2,1,0:T(8,128)(2,1)} %bitcast.32, bf16[8,2,48,128]{3,2,1,0:T(8,128)(2,1)} %copy-done.17, bf16[8,2,48,128]{3,2,1,0:T(8,128)(2,1)} %copy-done.16, ...), custom_call_target="tpu_custom_call" | custom-call | tf_op jit(solution)/shard_map/weights/pallas_call | solution.py:270
  194.4 2.1 layers.1
  196.5 4.8 %all-to-all-start.2 = ((bf16[8,16,512]{2,1,0:T(8,128)(2,1)}), bf16[8,16,512]{2,1,0:T(8,128)(2,1)S(1)}, u32[]{:S(2)}, u32[]{:S(2)}) async-start(bf16[8,16,512]{2,1,0:T(8,128)(2,1)} %layers.1), calls=%async_computation.2 | async-start | bytes 262144 | tf_op jit(solution)/shard_map/all_to_all | solution.py:427
  201.3 8.9 %all-to-all-done.2.own_ref = bf16[8,16,512]{2,1,0:T(8,128)(2,1)S(1)} async-done(((bf16[8,16,512]{2,1,0:T(8,128)(2,1)}), bf16[8,16,512]{2,1,0:T(8,128)(2,1)S(1)}, u32[]{:S(2)}, u32[]{:S(2)}) %all-to-all-start.2) | async-done | bytes 131104 | tf_op jit(solution)/shard_map/all_to_all | solution.py:427
  210.8 35.0 %encoder.1 = (bf16[8,16,4096]{2,1,0:T(8,128)(2,1)}, bf16[1,2,1,128,2048]{4,3,2,1,0:T(8,128)(2,1)}) custom-call(s32[5]{0:T(128)} %stack.23.place_ref, bf16[8,16,512]{2,1,0:T(8,128)(2,1)} %copy-done.35, bf16[96,4096]{1,0:T(8,128)(2,1)} %bitcast.34, f32[1,4096]{1,0:T(1,128)} %bitcast.38, bf16[1,2,1,128,2048]{4,3,2,1,0:T(8,128)(2,1)} %copy-done.21), custom_call_target="tpu_custom_call" | custom-call | tf_op jit(solution)/shard_map/encoder/pallas_call | solution.py:353
  245.8 6.0 %all-to-all-start.3 = ((bf16[8,16,4096]{2,1,0:T(8,128)(2,1)}), bf16[8,16,4096]{2,1,0:T(8,128)(2,1)S(1)}, u32[]{:S(2)}, u32[]{:S(2)}) async-start(bf16[8,16,4096]{2,1,0:T(8,128)(2,1)} %get-tuple-element.119), calls=%async_computation.3 | async-start | bytes 2097152 | tf_op jit(solution)/shard_map/all_to_all | solution.py:427
  254.7 2.4 collective-permute-start.33
  257.1 2.6 add.15
  259.7 8.7 %collective-permute-done.31.b_ref = bf16[128,2048]{1,0:T(8,128)(2,1)S(1)} collective-permute-done((bf16[128,2048]{1,0:T(8,128)(2,1)}, bf16[128,2048]{1,0:T(8,128)(2,1)S(1)}, u32[]{:S(2)}, u32[]{:S(2)}) %collective-permute-start.31) | collective-permute-done | bytes 524320 | tf_op jit(solution)/shard_map/ppermute | solution.py:415
  268.4 8.6 %collective-permute-done.32.c_ref = bf16[128,2048]{1,0:T(8,128)(2,1)S(1)} collective-permute-done((bf16[128,2048]{1,0:T(8,128)(2,1)S(1)}, bf16[128,2048]{1,0:T(8,128)(2,1)S(1)}, u32[]{:S(2)}, u32[]{:S(2)}) %collective-permute-start.32) | collective-permute-done | bytes 524320 | tf_op jit(solution)/shard_map/ppermute | solution.py:415
  278.7 2.6 add.14
  282.2 2.5 finish.1
  (146 shorter events, 37.3 us)
Async XLA Ops:
  35.8 35.8 %collective-permute-start.3 = (bf16[2,128,2048]{2,1,0:T(8,128)(2,1)}, bf16[2,128,2048]{2,1,0:T(8,128)(2,1)S(1)}, u32[]{:S(2)}, u32[]{:S(2)}) collective-permute-start(bf16[2,128,2048]{2,1,0:T(8,128)(2,1)} %get-tuple-element.64.refs_0_.refs_1_), channel_id=1, source_target_pairs={{0,6},{2,0},{4,2},{6,4},{1,7},{3,1},{5,3},{7,5},{8,14},{10,8},{12,... | collective-permute-start | bytes 3145736 | tf_op jit(solution)/shard_map/ppermute | solution.py:415
  38.7 33.0 %collective-permute-start.2 = (bf16[2,128,2048]{2,1,0:T(8,128)(2,1)}, bf16[2,128,2048]{2,1,0:T(8,128)(2,1)S(1)}, u32[]{:S(2)}, u32[]{:S(2)}) collective-permute-start(bf16[2,128,2048]{2,1,0:T(8,128)(2,1)} %get-tuple-element.64.refs_0_.refs_1_), channel_id=1, source_target_pairs={{0,2},{2,4},{4,6},{6,0},{1,3},{3,5},{5,7},{7,1},{8,10},{10,12},{12... | collective-permute-start | bytes 3145736 | tf_op jit(solution)/shard_map/ppermute | solution.py:415
  38.7 10.9 %collective-permute-start.4 = (bf16[48,4096]{1,0:T(8,128)(2,1)}, bf16[48,4096]{1,0:T(8,128)(2,1)S(1)}, u32[]{:S(2)}, u32[]{:S(2)}) collective-permute-start(bf16[48,4096]{1,0:T(8,128)(2,1)} %get-tuple-element.65.refs_12_.refs_20_.refs_4_), channel_id=1, source_target_pairs={{0,1},{1,0},{2,3},{3,2},{4,5},{5,4},{6,7},{7,6},{8,9},{9,8},{10,11... | collective-permute-start | bytes 1179656 | tf_op jit(solution)/shard_map/ppermute | solution.py:419
  38.7 33.0 %collective-permute-start.1 = (bf16[48,4096]{1,0:T(8,128)(2,1)}, bf16[48,4096]{1,0:T(8,128)(2,1)S(1)}, u32[]{:S(2)}, u32[]{:S(2)}) collective-permute-start(bf16[48,4096]{1,0:T(8,128)(2,1)} %get-tuple-element.65.refs_12_.refs_20_.refs_4_), channel_id=1, source_target_pairs={{0,24},{8,0},{16,8},{24,16},{1,25},{9,1},{17,9},{25,17},{2,26},{10... | collective-permute-start | bytes 1179656 | tf_op jit(solution)/shard_map/ppermute | solution.py:415
  45.0 26.7 %collective-permute-start = (bf16[48,4096]{1,0:T(8,128)(2,1)}, bf16[48,4096]{1,0:T(8,128)(2,1)S(1)}, u32[]{:S(2)}, u32[]{:S(2)}) collective-permute-start(bf16[48,4096]{1,0:T(8,128)(2,1)} %get-tuple-element.65.refs_12_.refs_20_.refs_4_), channel_id=1, source_target_pairs={{0,8},{8,16},{16,24},{24,0},{1,9},{9,17},{17,25},{25,1},{2,10},{10... | collective-permute-start | bytes 1179656 | tf_op jit(solution)/shard_map/ppermute | solution.py:415
  49.5 22.1 %collective-permute-start.5 = (bf16[2,48,2048]{2,1,0:T(8,128)(2,1)}, bf16[2,48,2048]{2,1,0:T(8,128)(2,1)}, u32[]{:S(2)}, u32[]{:S(2)}) collective-permute-start(bf16[2,48,2048]{2,1,0:T(8,128)(2,1)} %get-tuple-element.77.refs_12_.refs_20_), channel_id=1, source_target_pairs={{0,1},{1,0},{2,3},{3,2},{4,5},{5,4},{6,7},{7,6},{8,9},{9,8},{10,11... | collective-permute-start | bytes 1179656 | tf_op jit(solution)/shard_map/ppermute | solution.py:419
  73.1 14.5 %collective-permute-start.6 = (bf16[128,2048]{1,0:T(8,128)(2,1)S(1)}, bf16[128,2048]{1,0:T(8,128)(2,1)S(1)}, u32[]{:S(2)}, u32[]{:S(2)}) collective-permute-start(bf16[128,2048]{1,0:T(8,128)(2,1)S(1)} %slice_bitcast_fusion.1), channel_id=1, source_target_pairs={{0,2},{2,4},{4,6},{6,0},{1,3},{3,5},{5,7},{7,1},{8,10},{10,12},{12... | collective-permute-start | bytes 1572872 | tf_op jit(solution)/shard_map/ppermute | solution.py:415
  73.9 13.8 %collective-permute-start.7 = (bf16[128,2048]{1,0:T(8,128)(2,1)S(1)}, bf16[128,2048]{1,0:T(8,128)(2,1)S(1)}, u32[]{:S(2)}, u32[]{:S(2)}) collective-permute-start(bf16[128,2048]{1,0:T(8,128)(2,1)S(1)} %slice_bitcast_fusion), channel_id=1, source_target_pairs={{0,6},{2,0},{4,2},{6,4},{1,7},{3,1},{5,3},{7,5},{8,14},{10,8},{12,... | collective-permute-start | bytes 1572872 | tf_op jit(solution)/shard_map/ppermute | solution.py:415
  76.4 13.9 %collective-permute-start.10 = (bf16[48,4096]{1,0:T(8,128)(2,1)S(1)}, bf16[48,4096]{1,0:T(8,128)(2,1)S(1)}, u32[]{:S(2)}, u32[]{:S(2)}) collective-permute-start(bf16[48,4096]{1,0:T(8,128)(2,1)S(1)} %copy-done.7), channel_id=1, source_target_pairs={{0,1},{1,0},{2,3},{3,2},{4,5},{5,4},{6,7},{7,6},{8,9},{9,8},{10,11... | collective-permute-start | bytes 1179656 | tf_op jit(solution)/shard_map/ppermute | solution.py:419
  76.4 19.2 %collective-permute-start.8 = (bf16[48,4096]{1,0:T(8,128)(2,1)S(1)}, bf16[48,4096]{1,0:T(8,128)(2,1)S(1)}, u32[]{:S(2)}, u32[]{:S(2)}) collective-permute-start(bf16[48,4096]{1,0:T(8,128)(2,1)S(1)} %copy-done.7), channel_id=1, source_target_pairs={{0,8},{8,16},{16,24},{24,0},{1,9},{9,17},{17,25},{25,1},{2,10},{10... | collective-permute-start | bytes 1179656 | tf_op jit(solution)/shard_map/ppermute | solution.py:415
  77.1 18.8 %collective-permute-start.9 = (bf16[2,48,2048]{2,1,0:T(8,128)(2,1)S(1)}, bf16[2,48,2048]{2,1,0:T(8,128)(2,1)S(1)}, u32[]{:S(2)}, u32[]{:S(2)}) collective-permute-start(bf16[2,48,2048]{2,1,0:T(8,128)(2,1)S(1)} %copy-done.2), channel_id=1, source_target_pairs={{0,24},{8,0},{16,8},{24,16},{1,25},{9,1},{17,9},{25,17},{2,26},{10... | collective-permute-start | bytes 1179656 | tf_op jit(solution)/shard_map/ppermute | solution.py:415
  87.7 8.3 %collective-permute-start.13 = (bf16[8,2,48,128]{3,2,1,0:T(8,128)(2,1)S(1)}, bf16[8,2,48,128]{3,2,1,0:T(8,128)(2,1)S(1)}, u32[]{:S(2)}, u32[]{:S(2)}) collective-permute-start(bf16[8,2,48,128]{3,2,1,0:T(8,128)(2,1)S(1)} %bitcast.26), channel_id=1, source_target_pairs={{0,64},{64,128},{128,192},{192,0},{1,65},{65,129},{129,193},{193,1... | collective-permute-start | bytes 589832 | tf_op jit(solution)/shard_map/ppermute | solution.py:415
  89.3 8.9 %collective-permute-start.12 = (bf16[8,2,48,128]{3,2,1,0:T(8,128)(2,1)S(1)}, bf16[8,2,48,128]{3,2,1,0:T(8,128)(2,1)S(1)}, u32[]{:S(2)}, u32[]{:S(2)}) collective-permute-start(bf16[8,2,48,128]{3,2,1,0:T(8,128)(2,1)S(1)} %bitcast.27), channel_id=1, source_target_pairs={{0,128},{64,192},{128,0},{192,64},{1,129},{65,193},{129,1},{193,65... | collective-permute-start | bytes 589832 | tf_op jit(solution)/shard_map/ppermute | solution.py:415
  90.3 9.3 %collective-permute-start.11 = (bf16[8,2,48,128]{3,2,1,0:T(8,128)(2,1)S(1)}, bf16[8,2,48,128]{3,2,1,0:T(8,128)(2,1)S(1)}, u32[]{:S(2)}, u32[]{:S(2)}) collective-permute-start(bf16[8,2,48,128]{3,2,1,0:T(8,128)(2,1)S(1)} %bitcast.28), channel_id=1, source_target_pairs={{0,192},{64,0},{128,64},{192,128},{1,193},{65,1},{129,65},{193,129... | collective-permute-start | bytes 589832 | tf_op jit(solution)/shard_map/ppermute | solution.py:415
  100.7 15.2 %collective-permute-start.18 = (bf16[2,48,2048]{2,1,0:T(8,128)(2,1)S(1)}, bf16[2,48,2048]{2,1,0:T(8,128)(2,1)S(1)}, u32[]{:S(2)}, u32[]{:S(2)}) collective-permute-start(bf16[2,48,2048]{2,1,0:T(8,128)(2,1)S(1)} %collective-permute-done.9.refs_14_.refs_22_), channel_id=1, source_target_pairs={{0,1},{1,0},{2,3},{3,2},{4,5},{5,4},{6,7},{7,6},{8,9},{9,8},{10,11... | collective-permute-start | bytes 1179656 | tf_op jit(solution)/shard_map/ppermute | solution.py:419
  101.5 14.5 %collective-permute-start.14 = (bf16[48,2048]{1,0:T(8,128)(2,1)}, bf16[48,2048]{1,0:T(8,128)(2,1)S(1)}, u32[]{:S(2)}, u32[]{:S(2)}) collective-permute-start(bf16[48,2048]{1,0:T(8,128)(2,1)} %get-tuple-element.83), channel_id=1, source_target_pairs={{0,8},{8,16},{16,24},{24,0},{1,9},{9,17},{17,25},{25,1},{2,10},{10... | collective-permute-start | bytes 589832 | tf_op jit(solution)/shard_map/ppermute | solution.py:415
  103.5 12.5 %collective-permute-start.15 = (bf16[48,2048]{1,0:T(8,128)(2,1)}, bf16[48,2048]{1,0:T(8,128)(2,1)}, u32[]{:S(2)}, u32[]{:S(2)}) collective-permute-start(bf16[48,2048]{1,0:T(8,128)(2,1)} %get-tuple-element.129), channel_id=1, source_target_pairs={{0,24},{8,0},{16,8},{24,16},{1,25},{9,1},{17,9},{25,17},{2,26},{10... | collective-permute-start | bytes 589832 | tf_op jit(solution)/shard_map/ppermute | solution.py:415
  116.6 10.4 %collective-permute-start.20 = (bf16[48,2048]{1,0:T(8,128)(2,1)S(1)}, bf16[48,2048]{1,0:T(8,128)(2,1)S(1)}, u32[]{:S(2)}, u32[]{:S(2)}) collective-permute-start(bf16[48,2048]{1,0:T(8,128)(2,1)S(1)} %get-tuple-element.91), channel_id=1, source_target_pairs={{0,24},{8,0},{16,8},{24,16},{1,25},{9,1},{17,9},{25,17},{2,26},{10... | collective-permute-start | bytes 589832 | tf_op jit(solution)/shard_map/ppermute | solution.py:415
  118.8 9.4 %collective-permute-start.19 = (bf16[48,2048]{1,0:T(8,128)(2,1)S(1)}, bf16[48,2048]{1,0:T(8,128)(2,1)S(1)}, u32[]{:S(2)}, u32[]{:S(2)}) collective-permute-start(bf16[48,2048]{1,0:T(8,128)(2,1)S(1)} %get-tuple-element.89), channel_id=1, source_target_pairs={{0,8},{8,16},{16,24},{24,0},{1,9},{9,17},{17,25},{25,1},{2,10},{10... | collective-permute-start | bytes 589832 | tf_op jit(solution)/shard_map/ppermute | solution.py:415
  128.2 10.1 %collective-permute-start.23 = (bf16[48,2048]{1,0:T(8,128)(2,1)S(1)}, bf16[48,2048]{1,0:T(8,128)(2,1)S(1)}, u32[]{:S(2)}, u32[]{:S(2)}) collective-permute-start(bf16[48,2048]{1,0:T(8,128)(2,1)S(1)} %collective-permute-done.19.refs_13_), channel_id=1, source_target_pairs={{0,1},{1,0},{2,3},{3,2},{4,5},{5,4},{6,7},{7,6},{8,9},{9,8},{10,11... | collective-permute-start | bytes 589832 | tf_op jit(solution)/shard_map/ppermute | solution.py:419
  148.5 44.4 %all-to-all-start.1 = ((bf16[8,2,48,512]{3,2,1,0:T(8,128)(2,1)}), bf16[8,2,48,512]{3,2,1,0:T(8,128)(2,1)S(1)}, u32[]{:S(2)}, u32[]{:S(2)}) async-start(bf16[8,2,48,512]{3,2,1,0:T(8,128)(2,1)} %get-tuple-element.98), calls=%async_computation.1 | async-start | bytes 1572864 | tf_op jit(solution)/shard_map/all_to_all | solution.py:427
  155.8 45.4 %collective-permute-start.30 = (bf16[1,2,1,128,2048]{4,3,2,1,0:T(8,128)(2,1)S(1)}, bf16[1,2,1,128,2048]{4,3,2,1,0:T(8,128)(2,1)S(1)}, u32[]{:S(2)}, u32[]{:S(2)}) collective-permute-start(bf16[1,2,1,128,2048]{4,3,2,1,0:T(8,128)(2,1)S(1)} %copy-done.22), channel_id=1, source_target_pairs={{32,0},{64,32},{96,64},{128,96},{160,128},{192,160},{224,192},{33,... | collective-permute-start | bytes 3145736 | tf_op jit(solution)/shard_map/ppermute | solution.py:503
  159.2 32.8 %collective-permute-start.25 = (bf16[128,2048]{1,0:T(8,128)(2,1)}, bf16[128,2048]{1,0:T(8,128)(2,1)S(1)}, u32[]{:S(2)}, u32[]{:S(2)}) collective-permute-start(bf16[128,2048]{1,0:T(8,128)(2,1)} %get-tuple-element.104), channel_id=1, source_target_pairs={{0,4},{2,6},{4,0},{6,2},{1,5},{3,7},{5,1},{7,3},{8,12},{10,14},{12... | collective-permute-start | bytes 1572872 | tf_op jit(solution)/shard_map/ppermute | solution.py:415
  160.1 31.9 %collective-permute-start.26 = (bf16[128,2048]{1,0:T(8,128)(2,1)}, bf16[128,2048]{1,0:T(8,128)(2,1)S(1)}, u32[]{:S(2)}, u32[]{:S(2)}) collective-permute-start(bf16[128,2048]{1,0:T(8,128)(2,1)} %get-tuple-element.105), channel_id=1, source_target_pairs={{0,2},{2,4},{4,6},{6,0},{1,3},{3,5},{5,7},{7,1},{8,10},{10,12},{12... | collective-permute-start | bytes 1572872 | tf_op jit(solution)/shard_map/ppermute | solution.py:415
  162.1 30.8 %collective-permute-start.27 = (bf16[128,2048]{1,0:T(8,128)(2,1)}, bf16[128,2048]{1,0:T(8,128)(2,1)}, u32[]{:S(2)}, u32[]{:S(2)}) collective-permute-start(bf16[128,2048]{1,0:T(8,128)(2,1)} %get-tuple-element.106), channel_id=1, source_target_pairs={{0,6},{2,0},{4,2},{6,4},{1,7},{3,1},{5,3},{7,5},{8,14},{10,8},{12,... | collective-permute-start | bytes 1572872 | tf_op jit(solution)/shard_map/ppermute | solution.py:415
  163.4 21.6 %collective-permute-start.28 = (f32[8,512]{1,0:T(8,128)S(1)}, f32[8,512]{1,0:T(8,128)S(1)}, u32[]{:S(2)}, u32[]{:S(2)}) collective-permute-start(f32[8,512]{1,0:T(8,128)S(1)} %add.12), channel_id=1, source_target_pairs={{0,2},{2,0},{4,6},{6,4},{1,3},{3,1},{5,7},{7,5},{8,10},{10,8},{12,... | collective-permute-start | bytes 49160 | tf_op jit(solution)/shard_map/ppermute | solution.py:507
  185.0 7.9 %collective-permute-start.29 = (f32[8,512]{1,0:T(8,128)S(1)}, f32[8,512]{1,0:T(8,128)S(1)}, u32[]{:S(2)}, u32[]{:S(2)}) collective-permute-start(f32[8,512]{1,0:T(8,128)S(1)} %add.13.gain0_ref), channel_id=1, source_target_pairs={{0,4},{4,0},{2,6},{6,2},{1,5},{5,1},{3,7},{7,3},{8,12},{12,8},{10,... | collective-permute-start | bytes 49160 | tf_op jit(solution)/shard_map/ppermute | solution.py:508
  196.5 13.7 %all-to-all-start.2 = ((bf16[8,16,512]{2,1,0:T(8,128)(2,1)}), bf16[8,16,512]{2,1,0:T(8,128)(2,1)S(1)}, u32[]{:S(2)}, u32[]{:S(2)}) async-start(bf16[8,16,512]{2,1,0:T(8,128)(2,1)} %layers.1), calls=%async_computation.2 | async-start | bytes 262144 | tf_op jit(solution)/shard_map/all_to_all | solution.py:427
  245.8 35.5 %all-to-all-start.3 = ((bf16[8,16,4096]{2,1,0:T(8,128)(2,1)}), bf16[8,16,4096]{2,1,0:T(8,128)(2,1)S(1)}, u32[]{:S(2)}, u32[]{:S(2)}) async-start(bf16[8,16,4096]{2,1,0:T(8,128)(2,1)} %get-tuple-element.119), calls=%async_computation.3 | async-start | bytes 2097152 | tf_op jit(solution)/shard_map/all_to_all | solution.py:427
  251.8 16.6 %collective-permute-start.31 = (bf16[128,2048]{1,0:T(8,128)(2,1)}, bf16[128,2048]{1,0:T(8,128)(2,1)S(1)}, u32[]{:S(2)}, u32[]{:S(2)}) collective-permute-start(bf16[128,2048]{1,0:T(8,128)(2,1)} %get-tuple-element.116), channel_id=1, source_target_pairs={{0,4},{2,6},{4,0},{6,2},{1,5},{3,7},{5,1},{7,3},{8,12},{10,14},{12... | collective-permute-start | bytes 1572872 | tf_op jit(solution)/shard_map/ppermute | solution.py:415
  253.9 23.2 %collective-permute-start.32 = (bf16[128,2048]{1,0:T(8,128)(2,1)S(1)}, bf16[128,2048]{1,0:T(8,128)(2,1)S(1)}, u32[]{:S(2)}, u32[]{:S(2)}) collective-permute-start(bf16[128,2048]{1,0:T(8,128)(2,1)S(1)} %copy-done.41), channel_id=1, source_target_pairs={{0,2},{2,4},{4,6},{6,0},{1,3},{3,5},{5,7},{7,1},{8,10},{10,12},{12... | collective-permute-start | bytes 1572872 | tf_op jit(solution)/shard_map/ppermute | solution.py:415
  254.7 22.4 %collective-permute-start.33 = (bf16[128,2048]{1,0:T(8,128)(2,1)S(1)}, bf16[128,2048]{1,0:T(8,128)(2,1)S(1)}, u32[]{:S(2)}, u32[]{:S(2)}) collective-permute-start(bf16[128,2048]{1,0:T(8,128)(2,1)S(1)} %copy-done.40), channel_id=1, source_target_pairs={{0,6},{2,0},{4,2},{6,4},{1,7},{3,1},{5,3},{7,5},{8,14},{10,8},{12,... | collective-permute-start | bytes 1572872 | tf_op jit(solution)/shard_map/ppermute | solution.py:415
  (47 other events, 320.3 us)
where the time goes:
time: 291 us; the launch traced here: 285 us
  Pallas kernels  116 us (40%)
  starting transfers between devices  72.1 us (25%)
  waiting for transfers between devices  62.5 us (21%)
  blocking collectives  19.1 us (7%)
  local copies, waits for them, and re-layouts  13.5 us (5%)
    pallas_call x2, Pallas kernels, heads(): pl.pallas_call(functools.partial(heads_kernel, m == 0), grid=(1,), in_spe...  39.7 us
    ppermute x21, starting transfers between devices, shift(): return lax.ppermute(value, axis, [(i, (i + step) % 4) for i in range(4)])  38.3 us
    pallas_call x1, Pallas kernels, encoder_rows(): pl.pallas_call(encoder_kernel, in_specs=[SMEM, VMEM, VMEM, VMEM, HBM], ou...  35 us
    ppermute x21, waiting for transfers between devices, shift(): return lax.ppermute(value, axis, [(i, (i + step) % 4) for i in range(4)])  31.5 us
    ppermute x1, waiting for transfers between devices, body(): gain_part += lax.ppermute(gain_part, 'x', [(0, 1), (1, 0), (2, 3), (3, 2)])  20.8 us
    all_to_all x1, blocking collectives, exchange(): return lax.all_to_all(value, axes, split_axis=0, concat_axis=0, tiled=True)  19.1 us
    all_to_all x3, starting transfers between devices, exchange(): return lax.all_to_all(value, axes, split_axis=0, concat_axis=0, tiled=True)  18.1 us
    pallas_call x2, Pallas kernels, return_blocks(): pl.pallas_call(functools.partial(return_kernel, m, wheres), in_specs=[SME...  17.7 us
  transfers between devices with their start and end apart: 37, of which 12 were waited for; matrix products, arithmetic and copies ran while one was open for 1% of the time, Pallas kernels for 12%

commit v1 on v0

v1 whole, which is shorter than its diff:
```python
import functools

import jax
import jax.numpy as jnp
from jax import lax
from jax.experimental import pallas as pl
from jax.experimental.pallas import tpu as pltpu
from jax.sharding import Mesh, PartitionSpec as P

EPS = 1e-06
BF = jnp.bfloat16
F32 = jnp.float32
SEC = ("y", "zlo")
ZC = ("zhi", "core")
SRC = 48
D = 4096
HD = 2048
COLS = 512
PIECE = 6
VMEM = pl.BlockSpec(memory_space=pltpu.VMEM)
HBM = pl.BlockSpec(memory_space=pl.ANY)
PIN = pl.BlockSpec(memory_space=pltpu.HBM)


def shape(dims, dtype=BF):
    return jax.ShapeDtypeStruct(dims, dtype)


def pinned(dims, dtype=BF):
    return pltpu.HBM(dims, dtype)


def hold(*values):
    return [pltpu.with_memory_space_constraint(v, pltpu.HBM) for v in values]


def params(mib=16):
    return pltpu.CompilerParams(vmem_limit_bytes=mib * 2**20)


def cost(megabytes=0):
    return pl.CostEstimate(flops=0, bytes_accessed=megabytes * 2**20, transcendentals=0)


def rows_dot(a, b):
    return lax.dot_general(a, b, (((1,), (1,)), ((), ())), preferred_element_type=F32)


def columns_dot(a, b):
    return lax.dot_general(a, b, (((0,), (0,)), ((), ())), preferred_element_type=F32)


def heads_kernel(first, q_ref, k_ref, v_ref, g_ref, *refs):
    if first:
        key_w, value_w, local_ref, grads_ref, stack_ref = refs
        stack_ref[0], stack_ref[1] = key_w[0], value_w[0]
    else:
        _, local_ref, grads_ref = refs
    key_out = grads_ref.at[:, pl.ds(0, HD)]
    value_out = grads_ref.at[:, pl.ds(HD, HD)]
    src = k_ref.shape[0]
    lane = lax.broadcasted_iota(jnp.int32, (src, 256), 1) // 64
    masks = [lane == h for h in range(4)]

    def spread(block):
        zero = jnp.zeros_like(block)
        return jnp.concatenate([jnp.where(m, block, zero) for m in masks], axis=0)

    def diagonal(wide):
        out = wide[:src]
        for h in range(1, 4):
            out = jnp.where(masks[h], wide[h * src : (h + 1) * src], out)
        return out

    for part in range(HD // 256):
        at = pl.ds(part * 256, 256)
        q, g = q_ref[:, at], g_ref[:, at]
        k, v = spread(k_ref[:, at]), spread(v_ref[:, at])
        scores = rows_dot(k, q).reshape(4, src, -1)
        exponent = jnp.exp(scores - jnp.max(scores, axis=1, keepdims=True))
        probs = exponent * (1.0 / jnp.sum(exponent, axis=1, keepdims=True))
        slopes = rows_dot(v, g).reshape(4, src, -1)
        center = jnp.sum(probs * slopes, axis=1, keepdims=True)
        score_grad = (probs * (slopes - center)).astype(BF).reshape(4 * src, -1)
        probs = probs.astype(BF).reshape(4 * src, -1)
        value = jnp.dot(probs, g, preferred_element_type=F32)
        key = jnp.dot(score_grad, q, preferred_element_type=F32)
        key_out[:, at] = diagonal(key).astype(BF)
        value_out[:, at] = diagonal(value).astype(BF)
        local_ref[:, at] = columns_dot(score_grad, k).astype(BF)


def heads(q, k, v, g, m, *others):
    tgt = q.shape[3]

    def row(n):
        return pl.BlockSpec((None, None, None, n, HD), lambda i: (0, m, 0, 0, 0))

    def whole(*dims):
        return pl.BlockSpec(dims, lambda i: (0,) * len(dims))

    if m == 0:
        outs, more = [(SRC, D), (2, 128, HD)], [whole(1, 128, HD)] * 2
    else:
        outs, more = [(SRC, D)], [HBM]
    return pl.pallas_call(
        functools.partial(heads_kernel, m == 0),
        grid=(1,),
        in_specs=[row(tgt), row(SRC), row(SRC), row(tgt)] + more,
        out_specs=[row(tgt)] + [whole(*dims) for dims in outs],
        out_shape=[shape(q.shape)] + [shape(dims) for dims in outs],
        input_output_aliases={} if m == 0 else {4: 0},
        compiler_params=params(60),
        cost_estimate=cost(40),
        name="heads",
    )(q, k, v, g, *others)


def memory_kernel(pre_ref, gain_ref, out_ref):
    rows, features = pre_ref.shape
    squares = jnp.zeros((rows, 128), F32)
    for n in range(features // 128):
        part = pre_ref[:, pl.ds(n * 128, 128)].astype(F32)
        squares += part * part
    inverse = lax.rsqrt(jnp.sum(squares, axis=-1, keepdims=True) / features + EPS)
    for z in range(4):
        for c in range(2):
            at = pl.ds(pl.multiple_of(((z * 4 + lax.axis_index("y")) * 2 + c) * 128, 128), 128)
            hidden = pre_ref[:, at].astype(F32)
            out_ref[z * 2 + c] = (hidden * inverse * gain_ref[:, at]).astype(BF)


def memory_blocks(pre, gain):
    rows = pre.shape[0]
    return pl.pallas_call(
        memory_kernel,
        in_specs=[VMEM, VMEM],
        out_specs=VMEM,
        out_shape=shape((8, rows, 128)),
        compiler_params=params(60),
        cost_estimate=cost(),
        name="memory",
    )(pre, gain)


def token_blocks():
    z, c = lax.axis_index("zhi"), lax.axis_index("core")
    index = []
    for core in (c, 1 - c):
        for step in (0, 3, 1, 2):
            index.append(lax.rem(z + step, 4) * 2 + core)
    return index


def start_all(pairs, sems, first=0):
    copies = [pltpu.make_async_copy(a, b, sems.at[first + i]) for i, (a, b) in enumerate(pairs)]
    for copy in copies:
        copy.start()
    return copies


def wait_all(copies):
    for copy in copies:
        copy.wait()


def lanes(index):
    return pl.ds(pl.multiple_of(index * 128, 128), 128)


def columns_kernel(*refs):
    cols, out_ref, flip_ref, cols_s, flip_s, sems = refs[:4], *refs[4:]
    x, y = lax.axis_index("x"), lax.axis_index("y")
    pairs = []
    for r in range(4):
        at = lanes(lax.rem(y + r + 4 - x, 4))
        for m in range(2):
            pairs.append((cols[r].at[:, m], cols_s.at[m, :, :, at]))
    wait_all(start_all(pairs, sems))
    columns = cols_s[...].reshape(16 * SRC, COLS)
    kept = start_all([(cols_s, out_ref)], sems)
    for n in range(6):
        at = slice(n * 128, (n + 1) * 128)
        flip_s[:, at] = columns[at].T
    wait_all(kept + start_all([(flip_s, flip_ref)], sems, 1))


def gather_columns(*columns):
    return pl.pallas_call(
        columns_kernel,
        in_specs=[HBM] * 4,
        out_specs=[PIN, PIN],
        out_shape=[pinned((2, 8, SRC, COLS)), pinned((COLS, 16 * SRC))],
        scratch_shapes=[
            pltpu.VMEM((2, 8, SRC, COLS), BF),
            pltpu.VMEM((COLS, 16 * SRC), BF),
            pltpu.SemaphoreType.DMA((8,)),
        ],
        compiler_params=params(),
        cost_estimate=cost(),
        name="columns",
    )(*columns)


def return_kernel(m, *refs):
    weights, grads, refs = refs[:4], refs[4:12], refs[12:]
    if m == 0:
        out_ref, plain_ref, all_ref, grad_s, weight_s, out_s, plain_s, sems = refs
    else:
        cols_ref, before_ref, _, out_ref, gain_ref, all_ref = refs[:6]
        grad_s, weight_s, out_s, plain_s, cols_s, sems = refs[6:]
    x = lax.axis_index("x")
    place = token_blocks()
    pairs = []
    for half in range(2):
        for i, ref in enumerate(grads):
            pairs.append((ref.at[:, pl.ds(half * HD, HD)], grad_s.at[half, place[i]]))
        for r, ref in enumerate(weights):
            pairs.append((ref.at[half], weight_s.at[half, pl.ds(r * 128, 128)]))
    if m == 1:
        pairs += [(cols_ref, cols_s), (before_ref, plain_s)]
    copies = start_all(pairs, sems)
    wait_all(copies[:12])
    result = rows_dot(grad_s[0].reshape(8 * SRC, HD), weight_s[0])
    wait_all(copies[12:])
    kept = start_all([(grad_s, all_ref)], sems)
    result += rows_dot(grad_s[1].reshape(8 * SRC, HD), weight_s[1])
    rounded = result.astype(BF)
    if m == 0:
        plain_s[...] = rounded
        kept += start_all([(plain_s, plain_ref)], sems, 1)
    else:
        first, second = (cols_s[i].reshape(8 * SRC, COLS).astype(F32) for i in range(2))
        gain = jnp.sum(plain_s[...].astype(F32) * first + result * second, axis=0, keepdims=True)
        for r in range(4):
            block = gain[:, r * 128 : (r + 1) * 128]
            gain_ref[:, lanes(lax.rem(x + r, 4))] = jnp.broadcast_to(block, (8, 128))
    rows = 8 * SRC
    target = lax.broadcasted_iota(jnp.int32, (rows, rows), 0)
    source = lax.broadcasted_iota(jnp.int32, (rows, rows), 1)
    rank, rest = target // SRC, target % SRC
    wanted = (rest // PIECE) * SRC + rank * PIECE + rest % PIECE
    move = (source == wanted).astype(F32).astype(BF)
    moved = jnp.dot(move, rounded, preferred_element_type=F32)
    out_s[...] = moved.astype(BF).reshape(8, SRC, COLS)
    wait_all(kept + start_all([(out_s, out_ref.at[:, m])], sems, 2))


def return_blocks(m, weights, grads, *more):
    outs = [pinned((8, 2, SRC, COLS)), pinned((8 * SRC, COLS)), pinned((2, 8, SRC, HD))]
    scratch = [
        pltpu.VMEM((2, 8, SRC, HD), BF),
        pltpu.VMEM((2, COLS, HD), BF),
        pltpu.VMEM((8, SRC, COLS), BF),
        pltpu.VMEM((8 * SRC, COLS), BF),
    ]
    if m == 1:
        outs[1] = shape((8, COLS), F32)
        scratch.append(pltpu.VMEM((2, 8, SRC, COLS), BF))
    return pl.pallas_call(
        functools.partial(return_kernel, m),
        in_specs=[HBM] * 12 + [PIN] * len(more),
        out_specs=[PIN, VMEM if m == 1 else PIN, PIN],
        out_shape=outs,
        input_output_aliases={14: 0} if m == 1 else {},
        scratch_shapes=scratch + [pltpu.SemaphoreType.DMA((26,))],
        compiler_params=params(),
        cost_estimate=cost(),
        name="returned",
    )(*weights, *grads, *hold(*more))


def weight_kernel(flip_ref, first_ref, second_ref, *refs):
    outs, far_p, far_m, grad_s, flip_s, outs_s, sems = refs[:3], *refs[3:]
    kept = []
    pairs = [(flip_ref, flip_s)]
    for half in (1, 0):
        for m, ref in enumerate((first_ref, second_ref)):
            pairs.append((ref.at[half], grad_s.at[half, m]))
    copies = start_all(pairs, sems)
    for half in (1, 0):
        wait_all(copies[:3] if half == 1 else copies[3:])
        for n in range(HD // 512):
            at = pl.ds(n * 512, 512)
            grad = grad_s[half, :, :, :, at].reshape(16 * SRC, 512)
            partial = jnp.dot(flip_s[...], grad, preferred_element_type=F32).astype(BF)
            outs_s[0, half, :, at] = partial[:128]
            outs_s[1, half, :, at] = partial[128:256]
            far_p[half, :, at] = partial[256:320]
            far_m[half, :, at] = partial[320:384]
            outs_s[2, half, :, at] = partial[384:]
        pairs = [(outs_s.at[i, half], out.at[half]) for i, out in enumerate(outs)]
        kept += start_all(pairs, sems, 5 + 3 * half)
    wait_all(kept)


def weight_blocks(flipped, first, second):
    return pl.pallas_call(
        weight_kernel,
        in_specs=[PIN] * 3,
        out_specs=[PIN] * 3 + [VMEM] * 2,
        out_shape=[pinned((2, 128, HD))] * 3 + [shape((2, 64, HD))] * 2,
        scratch_shapes=[
            pltpu.VMEM((2, 2, 8, SRC, HD), BF),
            pltpu.VMEM((COLS, 16 * SRC), BF),
            pltpu.VMEM((3, 2, 128, HD), BF),
            pltpu.SemaphoreType.DMA((11,)),
        ],
        compiler_params=params(),
        cost_estimate=cost(),
        name="weights",
    )(*hold(flipped, first, second))


def relay_kernel(near_p, near_m, far_p, far_m, out_p, out_m, near_s, far_s, sems):
    pairs = [(near_p, near_s.at[0]), (near_m, near_s.at[1])]
    pairs += [(far_p, far_s.at[0]), (far_m, far_s.at[1])]
    wait_all(start_all(pairs, sems))
    first, second = pl.ds(0, 64), pl.ds(64, 64)
    for half in range(2):
        added = near_s[0, half, first].astype(F32) + far_s[0, half].astype(F32)
        out_p[half, first] = added.astype(BF)
        out_p[half, second] = near_s[0, half, second]
        out_m[half, first] = near_s[1, half, first]
        added = near_s[1, half, second].astype(F32) + far_s[1, half].astype(F32)
        out_m[half, second] = added.astype(BF)


def relay_blocks(near_p, near_m, far_p, far_m):
    return pl.pallas_call(
        relay_kernel,
        in_specs=[PIN, PIN, HBM, HBM],
        out_specs=[VMEM] * 2,
        out_shape=[shape(near_p.shape)] * 2,
        scratch_shapes=[
            pltpu.VMEM((2, 2, 128, HD), BF),
            pltpu.VMEM((2, 2, 64, HD), BF),
            pltpu.SemaphoreType.DMA((4,)),
        ],
        compiler_params=params(),
        cost_estimate=cost(),
        name="relay",
    )(*hold(near_p, near_m), far_p, far_m)


def pick_rows(rows, cols, wanted, keep):
    target = lax.broadcasted_iota(jnp.int32, (rows, cols), 0)
    source = lax.broadcasted_iota(jnp.int32, (rows, cols), 1)
    return ((source == wanted(target)) & keep(target)).astype(F32).astype(BF)


def sum_kernel(layers_ref, gain0_ref, gain1_ref, gain2_ref, gain3_ref, out_ref):
    moved = jnp.zeros((128, COLS), F32)
    for m in range(2):
        total = jnp.sum(layers_ref[:, m].astype(F32), axis=0).astype(BF)
        move = pick_rows(
            128,
            SRC,
            lambda t: (t // 16) * PIECE + t % 16 - m * PIECE,
            lambda t: (t % 16 >= m * PIECE) & (t % 16 < (m + 1) * PIECE),
        )
        moved += jnp.dot(move, total, preferred_element_type=F32)
    blocks = [lanes(lax.rem(lax.axis_index("x") + r, 4)) for r in range(4)]
    gains = (gain0_ref, gain1_ref, gain2_ref, gain3_ref)
    gain = jnp.concatenate([sum(ref[:, at] for ref in gains)[:1] for at in blocks], axis=1)
    high = gain.astype(BF).astype(F32)
    row = lax.broadcasted_iota(jnp.int32, (128, COLS), 0) % 16
    moved = jnp.where(row == 12, high, jnp.where(row == 13, gain - high, moved))
    out_ref[...] = moved.astype(BF).reshape(8, 16, COLS)


def sum_layers(layers, gains):
    return pl.pallas_call(
        sum_kernel,
        in_specs=[VMEM] * 5,
        out_specs=VMEM,
        out_shape=shape((8, 16, COLS)),
        compiler_params=params(),
        cost_estimate=cost(),
        name="layers",
    )(layers, *gains)


def encoder_kernel(
    own_ref, pre_ref, gain_ref, out_ref, full_s
):
    for z in range(4):
        for c in range(2):
            for x in range(4):
                at = (z * 4 + lax.rem(lax.axis_index("x") + x, 4)) * 2 + c
                full_s[:, lanes(at)] = own_ref[z * 2 + c, :, x * 128 : (x + 1) * 128]
    own = full_s[...].astype(F32)
    rank = (lax.axis_index("y") * 2 + lax.axis_index("zlo"))
    pick = pick_rows(
        16,
        2 * SRC,
        lambda t: (t // PIECE) * SRC + rank * PIECE + t % PIECE,
        lambda t: t < 2 * PIECE,
    )
    hidden = jnp.dot(pick, pre_ref[...], preferred_element_type=F32)
    inverse = lax.rsqrt(jnp.mean(hidden * hidden, axis=-1, keepdims=True) + EPS)
    scaled = own * gain_ref[...]
    row_mean = jnp.mean(hidden * scaled, axis=-1, keepdims=True)
    mine = inverse * scaled - hidden * (inverse * inverse * inverse * row_mean)
    row = lax.broadcasted_iota(jnp.int32, (16, D), 0)
    packed = jnp.where(row < 2 * PIECE, mine, own).astype(BF)
    for s in range(8):
        out_ref[s] = packed


def encoder_rows(own, pre, gain):
    return pl.pallas_call(
        encoder_kernel,
        in_specs=[VMEM, VMEM, VMEM],
        out_specs=VMEM,
        out_shape=shape((8, 16, D)),
        scratch_shapes=[pltpu.VMEM((16, D), BF)],
        compiler_params=params(),
        cost_estimate=cost(),
        name="encoder",
    )(own, pre, gain)


def finish_kernel(packed_ref, gain_ref, out_ref, gain_out_ref):
    packed = packed_ref[...].reshape(128, D)
    move = pick_rows(
        2 * SRC,
        128,
        lambda t: ((t % SRC) // PIECE) * 16 + (t // SRC) * PIECE + t % PIECE,
        lambda t: t >= 0,
    )
    out_ref[...] = jnp.dot(move, packed, preferred_element_type=F32).astype(BF)
    target = lax.broadcasted_iota(jnp.int32, (16, 128), 1) % 16
    ones = ((target == 12) | (target == 13)).astype(F32).astype(BF)
    gain = jnp.dot(ones, packed, preferred_element_type=F32)
    gain_out_ref[...] = gain[:1] / gain_ref[...]


def finish(packed, gain):
    return pl.pallas_call(
        finish_kernel,
        in_specs=[VMEM, VMEM],
        out_specs=[VMEM, VMEM],
        out_shape=[shape((2 * SRC, D)), shape((1, D), F32)],
        compiler_params=params(),
        cost_estimate=cost(),
        name="finish",
    )(packed, gain)


def add_kernel(*refs):
    terms, (key_out, value_out), (terms_s, sems) = refs[:3], refs[3:5], refs[5:]
    wait_all(start_all([(ref, terms_s.at[i]) for i, ref in enumerate(terms)], sems))
    for half, out in enumerate((key_out, value_out)):
        total = terms_s[0, half].astype(F32) + terms_s[1, half].astype(F32)
        out[...] = (total + terms_s[2, half].astype(F32)).astype(BF)


def add_blocks(*terms):
    dims = terms[0].shape
    return pl.pallas_call(
        add_kernel,
        in_specs=[PIN, HBM, HBM],
        out_specs=[VMEM] * 2,
        out_shape=[shape(dims[1:])] * 2,
        scratch_shapes=[pltpu.VMEM((3,) + dims, BF), pltpu.SemaphoreType.DMA((3,))],
        compiler_params=params(),
        cost_estimate=cost(60),
        name="add",
    )(*hold(terms[0]), *terms[1:])


def hand_kernel(in_ref, out_ref, held_s, sems):
    wait_all(start_all([(in_ref, held_s)], sems))
    wait_all(start_all([(held_s, out_ref)], sems))


def hand_on(value):
    return pl.pallas_call(
        hand_kernel,
        in_specs=[HBM],
        out_specs=PIN,
        out_shape=pinned(value.shape),
        scratch_shapes=[pltpu.VMEM(value.shape, BF), pltpu.SemaphoreType.DMA((1,))],
        compiler_params=params(),
        cost_estimate=cost(80),
        name="hand",
    )(value)


def shift(value, axis, step):
    return lax.ppermute(value, axis, [(i, (i + step) % 4) for i in range(4)])


def swap(value):
    return lax.ppermute(value, "core", [(0, 1), (1, 0)])


def after(value, *others):
    return lax.optimization_barrier((value,) + others)[0]


def exchange(value, axes):
    return lax.all_to_all(value, axes, split_axis=0, concat_axis=0, tiled=True)


class Chain:
    def __init__(self):
        self.last = ()

    def __call__(self, value, move, *others):
        result = move(after(value, *self.last, *others))
        self.last = (result,)
        return result


def body(pre_norm, norm_gain, queries, keys, values, head_grad, key_weight, value_weight):
    batches, _, source_n, features = pre_norm.shape
    rows = batches * source_n
    gain = norm_gain.reshape(1, features)
    hidden = pre_norm.reshape(rows, features)
    side = Chain()

    blocks = memory_blocks(hidden, gain)
    quarter = exchange(blocks, ZC).reshape(8, batches, source_n, 128)
    queries = after(queries, blocks)
    local, own0, stacked = heads(queries, keys, values, head_grad, 0, key_weight, value_weight)
    minus0, plus0 = shift(own0, "zhi", 1), shift(own0, "zhi", -1)
    own0_s = side(own0, swap)
    stacked = after(stacked, own0_s)
    weight_m, weight_p = shift(stacked, "x", 1), shift(stacked, "x", -1)
    local, own1 = heads(after(queries, own0), keys, values, head_grad, 1, local)
    own1_s = side(own1, swap)
    minus0, plus0, weight_m, weight_p, own1, own1_s, quarter = lax.optimization_barrier(
        (minus0, plus0, weight_m, weight_p, own1, own1_s, quarter)
    )

    far0 = shift(minus0, "zhi", 1)
    plus1 = shift(own1, "zhi", -1)
    weight_2 = shift(after(stacked, weight_m), "x", 2)
    minus0_s, plus0_s = swap(minus0), swap(plus0)
    far0, plus1, quarter = lax.optimization_barrier((far0, plus1, quarter))

    minus1 = shift(after(own1, far0), "zhi", 1)
    far1 = shift(plus1, "zhi", -1)
    far0_s, plus1_s = swap(far0), swap(plus1)
    quarters = [quarter] + [shift(quarter, "y", -r) for r in (1, 2, 3)]
    weights = (stacked, weight_p, weight_2, weight_m)
    blocks0 = (own0, minus0, plus0, far0, own0_s, minus0_s, plus0_s, far0_s)
    returned, plain, all0 = return_blocks(0, weights, blocks0)
    columns, flipped = gather_columns(after(quarters[0], returned), *quarters[1:])
    minus1, far1, columns, flipped = lax.optimization_barrier((minus1, far1, columns, flipped))

    minus1_s, far1_s = swap(minus1), swap(far1)
    blocks1 = (own1, minus1, plus1, far1, own1_s, minus1_s, plus1_s, far1_s)
    returned, gain_part, all1 = return_blocks(1, weights, blocks1, columns, plain, returned)
    layers = exchange(returned, SEC)
    query_in = lax.ppermute(
        after(local, layers), SEC, [(s, s - 1) for s in range(1, 8)]
    )
    gains = [gain_part] + [shift(gain_part, "x", r) for r in (1, 2, 3)]
    part = weight_blocks(after(flipped, returned), all0, all1)
    sums = sum_layers(after(layers, part[0]), gains)
    own = exchange(sums, ZC)
    far_p, far_m = lax.optimization_barrier((part[3], part[4], *gains))[:2]
    far_p, far_m = shift(far_p, "x", 1), shift(far_m, "x", -1)
    near_p, near_m = relay_blocks(part[1], part[2], far_p, far_m)
    packed = encoder_rows(after(own, near_p), hidden, gain)
    near_p, near_m = shift(near_p, "x", 1), shift(near_m, "x", -1)
    packed = exchange(packed, SEC)
    grad_key, grad_value = add_blocks(part[0], near_p, near_m)
    query_grad = hand_on(query_in)
    encoder_grad, gain_grad = finish(after(packed, grad_key, query_grad), gain)
    return (
        query_grad,
        grad_key[None],
        grad_value[None],
        encoder_grad.reshape(pre_norm.shape),
        gain_grad.reshape(features),
    )


def solution(mesh):
    grid = Mesh(mesh.devices.reshape(4, 2, 4, 4, 2), ("y", "zlo", "zhi", "x", "core"))
    dp = ("zhi", "x", "core")
    return jax.shard_map(
        body,
        mesh=grid,
        in_specs=(
            P(None, dp, None, None),
            P(),
            P(SEC, None, dp, None, None),
            P(SEC, None, dp, None, None),
            P(SEC, None, dp, None, None),
            P(SEC, None, dp, None, None),
            P(SEC, dp, None),
            P(SEC, dp, None),
        ),
        out_specs=(
            P(SEC, None, dp, None, None),
            P(SEC, dp, None),
            P(SEC, dp, None),
            P(None, dp, None, None),
            P(),
        ),
        check_vma=False,
    )
```

time: 291 us -> 178 us (0.61); the launches traced: 285 us -> 177 us
  Pallas kernels: 116 us -> 40.5 us
  starting transfers between devices: 72.1 us -> 56.7 us
  local copies, waits for them, and re-layouts: 13.5 us -> 1.97 us
  waiting for transfers between devices: 62.5 us -> 56.3 us
    pallas_call x10 -> x11, Pallas kernels: 76.8 us -> 30.7 us  [the longest x2 10.4 us: return_blocks(): pl.pallas_call(functools.partial(return_kernel, m), in_specs=[HBM] * 12 +...]
    pallas_call x2, Pallas kernels: 39.7 us -> 9.8 us  [heads(): pl.pallas_call(functools.partial(heads_kernel, m == 0), grid=(1,), in_spe...]
    ppermute x3 -> x1, waiting for transfers between devices: 20.8 us -> 7.52 us  [body(): lax.ppermute(after(local, layers), SEC, [(s, s - 1) for s in range(1, 8)])]
    ppermute x21 -> x19, waiting for transfers between devices: 31.5 us -> 43.8 us  [shift(): return lax.ppermute(value, axis, [(i, (i + step) % 4) for i in range(4)])]
    unnamed x84 -> x18, local copies, waits for them, and re-layouts: 11.4 us -> 1.97 us
    ppermute x10 -> x8, starting transfers between devices: 10.6 us -> 1.21 us  [swap(): return lax.ppermute(value, 'core', [(0, 1), (1, 0)])]
    all_to_all x3, waiting for transfers between devices: 8.89 us -> 1.23 us  [exchange(): return lax.all_to_all(value, axes, split_axis=0, concat_axis=0, tiled=True)]
    all_to_all x3, starting transfers between devices: 18.1 us -> 15 us  [exchange(): return lax.all_to_all(value, axes, split_axis=0, concat_axis=0, tiled=True)]
  transfers between devices with their start and end apart: 37 -> 31, of which waited for: 12 -> 13; matrix products, arithmetic and copies ran while one was open for 1% -> 0% of each run, Pallas kernels for 12% -> 14%
where the time goes in v1:
time: 178 us; the launch traced here: 177 us
  starting transfers between devices  56.7 us (32%)
  waiting for transfers between devices  56.3 us (32%)
  Pallas kernels  40.5 us (23%)
  blocking collectives  21 us (12%)
  local copies, waits for them, and re-layouts  1.97 us (1%)
    ppermute x19, waiting for transfers between devices, shift(): return lax.ppermute(value, axis, [(i, (i + step) % 4) for i in range(4)])  43.8 us
    ppermute x19, starting transfers between devices, shift(): return lax.ppermute(value, axis, [(i, (i + step) % 4) for i in range(4)])  37.2 us
    all_to_all x1, blocking collectives, exchange(): return lax.all_to_all(value, axes, split_axis=0, concat_axis=0, tiled=True)  21 us
    all_to_all x3, starting transfers between devices, exchange(): return lax.all_to_all(value, axes, split_axis=0, concat_axis=0, tiled=True)  15 us
    pallas_call x2, Pallas kernels, return_blocks(): pl.pallas_call(functools.partial(return_kernel, m), in_specs=[HBM] * 12 +...  10.4 us
    pallas_call x2, Pallas kernels, heads(): pl.pallas_call(functools.partial(heads_kernel, m == 0), grid=(1,), in_spe...  9.8 us
    pallas_call x1, Pallas kernels, weight_blocks(): pl.pallas_call(weight_kernel, in_specs=[PIN] * 3, out_specs=[PIN] * 3 + [...  7.94 us
    ppermute x1, waiting for transfers between devices, body(): lax.ppermute(after(local, layers), SEC, [(s, s - 1) for s in range(1, 8)])  7.52 us
  transfers between devices with their start and end apart: 31, of which 13 were waited for; matrix products, arithmetic and copies ran while one was open for 0% of the time, Pallas kernels for 14%

profile of v1, /device:TPU:8, one launch (start us, length us, event | category | flops | bytes accessed | tf_op | source)
XLA Modules:
  0.0 177.3 jit_solution(6917064962342749114)
XLA Ops:
  0.6 2.1 %memory.1 = bf16[8,96,128]{2,1,0:T(8,128)(2,1)} custom-call(bf16[96,4096]{1,0:T(8,128)(2,1)} %bitcast.9, f32[1,4096]{1,0:T(1,128)} %bitcast.15), custom_call_target="tpu_custom_call" | custom-call | tf_op jit(solution)/shard_map/memory/pallas_call | solution.py:135
  2.7 5.2 %heads.2 = (bf16[1,2,1,128,2048]{4,3,2,1,0:T(8,128)(2,1)}, bf16[48,4096]{1,0:T(8,128)(2,1)}, bf16[2,128,2048]{2,1,0:T(8,128)(2,1)}) custom-call(bf16[1,2,1,128,2048]{4,3,2,1,0:T(8,128)(2,1)} %q_ref.1, bf16[1,2,1,48,2048]{4,3,2,1,0:T(8,128)(2,1)} %k_ref.3, bf16[1,2,1,48,2048]{4,3,2,1,0:T(8,128)(2,1)} %v_ref.3, bf16[1,2,1,128,2048]{4,3,2,1,0:T(8,128)(2,1)} %g_ref.3, ...), custom_call_target="tpu_custom_call" | custom-call | bytes 41943040 | tf_op jit(solution)/shard_map/heads/pallas_call | solution.py:106
  8.0 1.9 %collective-permute-done.refs_8_ = bf16[48,4096]{1,0:T(8,128)(2,1)S(1)} collective-permute-done((bf16[48,4096]{1,0:T(8,128)(2,1)}, bf16[48,4096]{1,0:T(8,128)(2,1)S(1)}, u32[]{:S(2)}, u32[]{:S(2)}) %collective-permute-start) | collective-permute-done | bytes 393248 | tf_op jit(solution)/shard_map/ppermute | solution.py:496
  10.0 2.8 %collective-permute-start.4 = (bf16[2,128,2048]{2,1,0:T(8,128)(2,1)}, bf16[2,128,2048]{2,1,0:T(8,128)(2,1)S(1)}, u32[]{:S(2)}, u32[]{:S(2)}) collective-permute-start(bf16[2,128,2048]{2,1,0:T(8,128)(2,1)} %get-tuple-element.68.refs_0_), channel_id=1, source_target_pairs={{0,6},{2,0},{4,2},{6,4},{1,7},{3,1},{5,3},{7,5},{8,14},{10,8},{12,... | collective-permute-start | bytes 3145736 | tf_op jit(solution)/shard_map/ppermute | solution.py:492
  12.7 6.3 %collective-permute-start.2 = (bf16[48,4096]{1,0:T(8,128)(2,1)}, bf16[48,4096]{1,0:T(8,128)(2,1)}, u32[]{:S(2)}, u32[]{:S(2)}) collective-permute-start(bf16[48,4096]{1,0:T(8,128)(2,1)} %get-tuple-element.58.refs_4_), channel_id=1, source_target_pairs={{0,24},{8,0},{16,8},{24,16},{1,25},{9,1},{17,9},{25,17},{2,26},{10... | collective-permute-start | bytes 1179656 | tf_op jit(solution)/shard_map/ppermute | solution.py:492
  19.0 4.6 %heads.3 = (bf16[1,2,1,128,2048]{4,3,2,1,0:T(8,128)(2,1)}, bf16[48,4096]{1,0:T(8,128)(2,1)}) custom-call(bf16[1,2,1,128,2048]{4,3,2,1,0:T(8,128)(2,1)} %q_ref.1, bf16[1,2,1,48,2048]{4,3,2,1,0:T(8,128)(2,1)} %k_ref.3, bf16[1,2,1,48,2048]{4,3,2,1,0:T(8,128)(2,1)} %v_ref.3, bf16[1,2,1,128,2048]{4,3,2,1,0:T(8,128)(2,1)} %g_ref.3, ...), custom_call_target="tpu_custom_call", output_to_operand_aliasing={{0}: (4, {})} | custom-call | bytes 41943040 | tf_op jit(solution)/shard_map/heads/pallas_call | solution.py:106
  23.6 21.0 %all_to_all.20 = bf16[8,96,128]{2,1,0:T(8,128)(2,1)S(1)} all-to-all(bf16[8,96,128]{2,1,0:T(8,128)(2,1)S(1)} %copy-done.8), channel_id=1, replica_groups=mesh['y'=4,'zlo'=2,'zhi'=4,'x'=4,'core'=2] {'zhi','core'}, dimensions={0} | all-to-all | bytes 393216 | tf_op jit(solution)/shard_map/all_to_all | solution.py:504
  44.6 2.0 %collective-permute-start.6 = (bf16[2,128,2048]{2,1,0:T(8,128)(2,1)S(1)}, bf16[2,128,2048]{2,1,0:T(8,128)(2,1)S(1)}, u32[]{:S(2)}, u32[]{:S(2)}) collective-permute-start(bf16[2,128,2048]{2,1,0:T(8,128)(2,1)S(1)} %copy-done), channel_id=1, source_target_pairs={{0,4},{2,6},{4,0},{6,2},{1,5},{3,7},{5,1},{7,3},{8,12},{10,14},{12... | collective-permute-start | bytes 3145736 | tf_op jit(solution)/shard_map/ppermute | solution.py:492
  46.6 1.9 %collective-permute-start.8 = (bf16[48,4096]{1,0:T(8,128)(2,1)}, bf16[48,4096]{1,0:T(8,128)(2,1)S(1)}, u32[]{:S(2)}, u32[]{:S(2)}) collective-permute-start(bf16[48,4096]{1,0:T(8,128)(2,1)} %get-tuple-element.73.refs_4_), channel_id=1, source_target_pairs={{0,24},{8,0},{16,8},{24,16},{1,25},{9,1},{17,9},{25,17},{2,26},{10... | collective-permute-start | bytes 1179656 | tf_op jit(solution)/shard_map/ppermute | solution.py:492
  50.0 15.9 %collective-permute-done.8.refs_6_ = bf16[48,4096]{1,0:T(8,128)(2,1)S(1)} collective-permute-done((bf16[48,4096]{1,0:T(8,128)(2,1)}, bf16[48,4096]{1,0:T(8,128)(2,1)S(1)}, u32[]{:S(2)}, u32[]{:S(2)}) %collective-permute-start.8) | collective-permute-done | bytes 393248 | tf_op jit(solution)/shard_map/ppermute | solution.py:492
  66.8 1.8 %collective-permute-start.9 = (bf16[48,4096]{1,0:T(8,128)(2,1)}, bf16[48,4096]{1,0:T(8,128)(2,1)S(1)}, u32[]{:S(2)}, u32[]{:S(2)}) collective-permute-start(bf16[48,4096]{1,0:T(8,128)(2,1)} %get-tuple-element.73.refs_4_), channel_id=1, source_target_pairs={{0,8},{8,16},{16,24},{24,0},{1,9},{9,17},{17,25},{25,1},{2,10},{10... | collective-permute-start | bytes 1179656 | tf_op jit(solution)/shard_map/ppermute | solution.py:492
  68.7 2.3 %collective-permute-start.10 = (bf16[48,4096]{1,0:T(8,128)(2,1)S(1)}, bf16[48,4096]{1,0:T(8,128)(2,1)S(1)}, u32[]{:S(2)}, u32[]{:S(2)}) collective-permute-start(bf16[48,4096]{1,0:T(8,128)(2,1)S(1)} %collective-permute-done.8.refs_6_), channel_id=1, source_target_pairs={{0,24},{8,0},{16,8},{24,16},{1,25},{9,1},{17,9},{25,17},{2,26},{10... | collective-permute-start | bytes 1179656 | tf_op jit(solution)/shard_map/ppermute | solution.py:492
  71.0 1.6 collective-permute-start.16
  73.5 2.4 %collective-permute-start.14 = (bf16[8,2,48,128]{3,2,1,0:T(8,128)(2,1)S(1)}, bf16[8,2,48,128]{3,2,1,0:T(8,128)(2,1)S(1)}, u32[]{:S(2)}, u32[]{:S(2)}) collective-permute-start(bf16[8,2,48,128]{3,2,1,0:T(8,128)(2,1)S(1)} %bitcast.13), channel_id=1, source_target_pairs={{0,192},{64,0},{128,64},{192,128},{1,193},{65,1},{129,65},{193,129... | collective-permute-start | bytes 589832 | tf_op jit(solution)/shard_map/ppermute | solution.py:492
  75.9 4.8 %returned.2 = (bf16[8,2,48,512]{3,2,1,0:T(8,128)(2,1)}, bf16[384,512]{1,0:T(8,128)(2,1)}, bf16[2,8,48,2048]{3,2,1,0:T(8,128)(2,1)}) custom-call(bf16[2,128,2048]{2,1,0:T(8,128)(2,1)S(1)} %copy-done, bf16[2,128,2048]{2,1,0:T(8,128)(2,1)S(1)} %collective-permute-done.4.refs_1_, bf16[2,128,2048]{2,1,0:T(8,128)(2,1)S(1)} %collective-permute-done.6.refs_2_, ...), custom_call_target="tpu_custom_call" | custom-call | tf_op jit(solution)/shard_map/returned/pallas_call | solution.py:260
  81.9 2.1 %collective-permute-done.14.refs_1_ = bf16[8,2,48,128]{3,2,1,0:T(8,128)(2,1)S(1)} collective-permute-done((bf16[8,2,48,128]{3,2,1,0:T(8,128)(2,1)S(1)}, bf16[8,2,48,128]{3,2,1,0:T(8,128)(2,1)S(1)}, u32[]{:S(2)}, u32[]{:S(2)}) %collective-permute-start.14) | collective-permute-done | bytes 196640 | tf_op jit(solution)/shard_map/ppermute | solution.py:492
  87.9 5.6 %returned.3 = (bf16[8,2,48,512]{3,2,1,0:T(8,128)(2,1)}, f32[8,512]{1,0:T(8,128)S(1)}, bf16[2,8,48,2048]{3,2,1,0:T(8,128)(2,1)}) custom-call(bf16[2,128,2048]{2,1,0:T(8,128)(2,1)S(1)} %copy-done, bf16[2,128,2048]{2,1,0:T(8,128)(2,1)S(1)} %collective-permute-done.4.refs_1_, ...), custom_call_target="tpu_custom_call", output_to_operand_aliasing={{0}: (14, {})} | custom-call | tf_op jit(solution)/shard_map/returned/pallas_call | solution.py:260
  93.5 5.0 %all-to-all-start.1 = ((bf16[8,2,48,512]{3,2,1,0:T(8,128)(2,1)}), bf16[8,2,48,512]{3,2,1,0:T(8,128)(2,1)S(1)}, u32[]{:S(2)}, u32[]{:S(2)}) async-start(bf16[8,2,48,512]{3,2,1,0:T(8,128)(2,1)} %get-tuple-element.86), calls=%async_computation.1 | async-start | bytes 1572864 | tf_op jit(solution)/shard_map/all_to_all | solution.py:504
  99.7 5.0 %collective-permute-start.22 = (f32[8,512]{1,0:T(8,128)S(1)}, f32[8,512]{1,0:T(8,128)S(1)}, u32[]{:S(2)}, u32[]{:S(2)}) collective-permute-start(f32[8,512]{1,0:T(8,128)S(1)} %get-tuple-element.97.gain0_ref), channel_id=1, source_target_pairs={{0,4},{2,6},{4,0},{6,2},{1,5},{3,7},{5,1},{7,3},{8,12},{10,14},{12... | collective-permute-start | bytes 49160 | tf_op jit(solution)/shard_map/ppermute | solution.py:492
  104.7 1.4 collective-permute-start.21
  106.1 7.9 %weights.1 = (bf16[2,128,2048]{2,1,0:T(8,128)(2,1)}, bf16[2,128,2048]{2,1,0:T(8,128)(2,1)}, bf16[2,128,2048]{2,1,0:T(8,128)(2,1)}, bf16[2,64,2048]{2,1,0:T(8,128)(2,1)}, bf16[2,64,2048]{2,1,0:T(8,128)(2,1)}) custom-call(bf16[512,768]{1,0:T(8,128)(2,1)} %get-tuple-element.89.flip_ref, bf16[2,8,48,2048]{3,2,1,0:T(8,128)(2,1)} %get-tuple-element.90.first_ref, ...), custom_call_target="tpu_custom_call" | custom-call | tf_op jit(solution)/shard_map/weights/pallas_call | solution.py:298
  114.2 3.2 %collective-permute-start.25 = (bf16[2,64,2048]{2,1,0:T(8,128)(2,1)}, bf16[2,64,2048]{2,1,0:T(8,128)(2,1)S(1)}, u32[]{:S(2)}, u32[]{:S(2)}) collective-permute-start(bf16[2,64,2048]{2,1,0:T(8,128)(2,1)} %get-tuple-element.99), channel_id=1, source_target_pairs={{0,6},{2,0},{4,2},{6,4},{1,7},{3,1},{5,3},{7,5},{8,14},{10,8},{12,... | collective-permute-start | bytes 1572872 | tf_op jit(solution)/shard_map/ppermute | solution.py:492
  118.3 4.9 %all-to-all-start.2 = ((bf16[8,16,512]{2,1,0:T(8,128)(2,1)}), bf16[8,16,512]{2,1,0:T(8,128)(2,1)S(1)}, u32[]{:S(2)}, u32[]{:S(2)}) async-start(bf16[8,16,512]{2,1,0:T(8,128)(2,1)} %layers.1), calls=%async_computation.2 | async-start | bytes 262144 | tf_op jit(solution)/shard_map/all_to_all | solution.py:504
  123.2 4.9 %collective-permute-done.24.far_p = bf16[2,64,2048]{2,1,0:T(8,128)(2,1)S(1)} collective-permute-done((bf16[2,64,2048]{2,1,0:T(8,128)(2,1)}, bf16[2,64,2048]{2,1,0:T(8,128)(2,1)S(1)}, u32[]{:S(2)}, u32[]{:S(2)}) %collective-permute-start.24) | collective-permute-done | bytes 524320 | tf_op jit(solution)/shard_map/ppermute | solution.py:492
  128.1 1.8 %relay.1 = (bf16[2,128,2048]{2,1,0:T(8,128)(2,1)S(1)}, bf16[2,128,2048]{2,1,0:T(8,128)(2,1)S(1)}) custom-call(bf16[2,128,2048]{2,1,0:T(8,128)(2,1)} %get-tuple-element.93.near_p, bf16[2,128,2048]{2,1,0:T(8,128)(2,1)} %get-tuple-element.94.near_m, bf16[2,64,2048]{2,1,0:T(8,128)(2,1)S(1)} %collective-permute-done.24.far_p, ...), custom_call_target="tpu_custom_call" | custom-call | tf_op jit(solution)/shard_map/relay/pallas_call | solution.py:330
  133.2 1.4 encoder.1
  134.6 5.1 %all-to-all-start.3 = ((bf16[8,16,4096]{2,1,0:T(8,128)(2,1)}), bf16[8,16,4096]{2,1,0:T(8,128)(2,1)S(1)}, u32[]{:S(2)}, u32[]{:S(2)}) async-start(bf16[8,16,4096]{2,1,0:T(8,128)(2,1)} %encoder.1), calls=%async_computation.3 | async-start | bytes 2097152 | tf_op jit(solution)/shard_map/all_to_all | solution.py:504
  139.7 3.2 %collective-permute-start.27 = (bf16[2,128,2048]{2,1,0:T(8,128)(2,1)}, bf16[2,128,2048]{2,1,0:T(8,128)(2,1)S(1)}, u32[]{:S(2)}, u32[]{:S(2)}) collective-permute-start(bf16[2,128,2048]{2,1,0:T(8,128)(2,1)} %copy-done.7), channel_id=1, source_target_pairs={{0,6},{2,0},{4,2},{6,4},{1,7},{3,1},{5,3},{7,5},{8,14},{10,8},{12,... | collective-permute-start | bytes 3145736 | tf_op jit(solution)/shard_map/ppermute | solution.py:492
  142.9 3.4 %collective-permute-start.20 = (bf16[1,2,1,128,2048]{4,3,2,1,0:T(8,128)(2,1)}, bf16[1,2,1,128,2048]{4,3,2,1,0:T(8,128)(2,1)S(1)}, u32[]{:S(2)}, u32[]{:S(2)}) collective-permute-start(bf16[1,2,1,128,2048]{4,3,2,1,0:T(8,128)(2,1)} %get-tuple-element.87), channel_id=1, source_target_pairs={{32,0},{64,32},{96,64},{128,96},{160,128},{192,160},{224,192},{33,... | collective-permute-start | bytes 3145736 | tf_op jit(solution)/shard_map/ppermute | solution.py:558
  146.3 18.3 %collective-permute-done.27.refs_2_ = bf16[2,128,2048]{2,1,0:T(8,128)(2,1)S(1)} collective-permute-done((bf16[2,128,2048]{2,1,0:T(8,128)(2,1)}, bf16[2,128,2048]{2,1,0:T(8,128)(2,1)S(1)}, u32[]{:S(2)}, u32[]{:S(2)}) %collective-permute-start.27) | collective-permute-done | bytes 1048608 | tf_op jit(solution)/shard_map/ppermute | solution.py:492
  165.0 2.4 %add.1 = (bf16[128,2048]{1,0:T(8,128)(2,1)}, bf16[128,2048]{1,0:T(8,128)(2,1)}) custom-call(bf16[2,128,2048]{2,1,0:T(8,128)(2,1)} %get-tuple-element.92.refs_0_, bf16[2,128,2048]{2,1,0:T(8,128)(2,1)S(1)} %collective-permute-done.26.refs_1_, bf16[2,128,2048]{2,1,0:T(8,128)(2,1)S(1)} %collective-permute-done.27.refs_2_), custom_call_target="tpu_custom_call" | custom-call | bytes 62914560 | tf_op jit(solution)/shard_map/add/pallas_call | solution.py:461
  167.5 7.5 %collective-permute-done.20.in_ref = bf16[1,2,1,128,2048]{4,3,2,1,0:T(8,128)(2,1)S(1)} collective-permute-done((bf16[1,2,1,128,2048]{4,3,2,1,0:T(8,128)(2,1)}, bf16[1,2,1,128,2048]{4,3,2,1,0:T(8,128)(2,1)S(1)}, u32[]{:S(2)}, u32[]{:S(2)}) %collective-permute-start.20) | collective-permute-done | bytes 1048608 | tf_op jit(solution)/shard_map/ppermute | solution.py:558
  (62 shorter events, 16.8 us)
Async XLA Ops:
  7.9 68.0 %copy-start.3 = (bf16[48,4096]{1,0:T(8,128)(2,1)S(1)}, bf16[48,4096]{1,0:T(8,128)(2,1)}, u32[]{:S(2)}) copy-start(bf16[48,4096]{1,0:T(8,128)(2,1)} %get-tuple-element.58.refs_4_) | copy-start | bytes 1179652
  8.0 2.0 %collective-permute-start = (bf16[48,4096]{1,0:T(8,128)(2,1)}, bf16[48,4096]{1,0:T(8,128)(2,1)S(1)}, u32[]{:S(2)}, u32[]{:S(2)}) collective-permute-start(bf16[48,4096]{1,0:T(8,128)(2,1)} %get-tuple-element.58.refs_4_), channel_id=1, source_target_pairs={{0,1},{1,0},{2,3},{3,2},{4,5},{5,4},{6,7},{7,6},{8,9},{9,8},{10,11... | collective-permute-start | bytes 1179656 | tf_op jit(solution)/shard_map/ppermute | solution.py:496
  10.0 34.6 %collective-permute-start.4 = (bf16[2,128,2048]{2,1,0:T(8,128)(2,1)}, bf16[2,128,2048]{2,1,0:T(8,128)(2,1)S(1)}, u32[]{:S(2)}, u32[]{:S(2)}) collective-permute-start(bf16[2,128,2048]{2,1,0:T(8,128)(2,1)} %get-tuple-element.68.refs_0_), channel_id=1, source_target_pairs={{0,6},{2,0},{4,2},{6,4},{1,7},{3,1},{5,3},{7,5},{8,14},{10,8},{12,... | collective-permute-start | bytes 3145736 | tf_op jit(solution)/shard_map/ppermute | solution.py:492
  12.7 31.9 %collective-permute-start.3 = (bf16[2,128,2048]{2,1,0:T(8,128)(2,1)}, bf16[2,128,2048]{2,1,0:T(8,128)(2,1)S(1)}, u32[]{:S(2)}, u32[]{:S(2)}) collective-permute-start(bf16[2,128,2048]{2,1,0:T(8,128)(2,1)} %get-tuple-element.68.refs_0_), channel_id=1, source_target_pairs={{0,2},{2,4},{4,6},{6,0},{1,3},{3,5},{5,7},{7,1},{8,10},{10,12},{12... | collective-permute-start | bytes 3145736 | tf_op jit(solution)/shard_map/ppermute | solution.py:492
  12.7 31.8 %collective-permute-start.2 = (bf16[48,4096]{1,0:T(8,128)(2,1)}, bf16[48,4096]{1,0:T(8,128)(2,1)}, u32[]{:S(2)}, u32[]{:S(2)}) collective-permute-start(bf16[48,4096]{1,0:T(8,128)(2,1)} %get-tuple-element.58.refs_4_), channel_id=1, source_target_pairs={{0,24},{8,0},{16,8},{24,16},{1,25},{9,1},{17,9},{25,17},{2,26},{10... | collective-permute-start | bytes 1179656 | tf_op jit(solution)/shard_map/ppermute | solution.py:492
  19.0 25.5 %collective-permute-start.1 = (bf16[48,4096]{1,0:T(8,128)(2,1)}, bf16[48,4096]{1,0:T(8,128)(2,1)}, u32[]{:S(2)}, u32[]{:S(2)}) collective-permute-start(bf16[48,4096]{1,0:T(8,128)(2,1)} %get-tuple-element.58.refs_4_), channel_id=1, source_target_pairs={{0,8},{8,16},{16,24},{24,0},{1,9},{9,17},{17,25},{25,1},{2,10},{10... | collective-permute-start | bytes 1179656 | tf_op jit(solution)/shard_map/ppermute | solution.py:492
  23.6 21.0 %collective-permute-start.5 = (bf16[48,4096]{1,0:T(8,128)(2,1)}, bf16[48,4096]{1,0:T(8,128)(2,1)S(1)}, u32[]{:S(2)}, u32[]{:S(2)}) collective-permute-start(bf16[48,4096]{1,0:T(8,128)(2,1)} %get-tuple-element.73.refs_4_), channel_id=1, source_target_pairs={{0,1},{1,0},{2,3},{3,2},{4,5},{5,4},{6,7},{7,6},{8,9},{9,8},{10,11... | collective-permute-start | bytes 1179656 | tf_op jit(solution)/shard_map/ppermute | solution.py:496
  44.6 28.9 %collective-permute-start.6 = (bf16[2,128,2048]{2,1,0:T(8,128)(2,1)S(1)}, bf16[2,128,2048]{2,1,0:T(8,128)(2,1)S(1)}, u32[]{:S(2)}, u32[]{:S(2)}) collective-permute-start(bf16[2,128,2048]{2,1,0:T(8,128)(2,1)S(1)} %copy-done), channel_id=1, source_target_pairs={{0,4},{2,6},{4,0},{6,2},{1,5},{3,7},{5,1},{7,3},{8,12},{10,14},{12... | collective-permute-start | bytes 3145736 | tf_op jit(solution)/shard_map/ppermute | solution.py:492
  46.6 19.3 %collective-permute-start.8 = (bf16[48,4096]{1,0:T(8,128)(2,1)}, bf16[48,4096]{1,0:T(8,128)(2,1)S(1)}, u32[]{:S(2)}, u32[]{:S(2)}) collective-permute-start(bf16[48,4096]{1,0:T(8,128)(2,1)} %get-tuple-element.73.refs_4_), channel_id=1, source_target_pairs={{0,24},{8,0},{16,8},{24,16},{1,25},{9,1},{17,9},{25,17},{2,26},{10... | collective-permute-start | bytes 1179656 | tf_op jit(solution)/shard_map/ppermute | solution.py:492
  48.5 18.4 %collective-permute-start.7 = (bf16[48,4096]{1,0:T(8,128)(2,1)}, bf16[48,4096]{1,0:T(8,128)(2,1)S(1)}, u32[]{:S(2)}, u32[]{:S(2)}) collective-permute-start(bf16[48,4096]{1,0:T(8,128)(2,1)} %collective-permute-done.1.refs_5_), channel_id=1, source_target_pairs={{0,8},{8,16},{16,24},{24,0},{1,9},{9,17},{17,25},{25,1},{2,10},{10... | collective-permute-start | bytes 1179656 | tf_op jit(solution)/shard_map/ppermute | solution.py:492
  49.5 19.1 %collective-permute-start.12 = (bf16[48,4096]{1,0:T(8,128)(2,1)}, bf16[48,4096]{1,0:T(8,128)(2,1)S(1)}, u32[]{:S(2)}, u32[]{:S(2)}) collective-permute-start(bf16[48,4096]{1,0:T(8,128)(2,1)} %collective-permute-done.2.refs_6_), channel_id=1, source_target_pairs={{0,1},{1,0},{2,3},{3,2},{4,5},{5,4},{6,7},{7,6},{8,9},{9,8},{10,11... | collective-permute-start | bytes 1179656 | tf_op jit(solution)/shard_map/ppermute | solution.py:496
  49.5 21.4 %collective-permute-start.11 = (bf16[48,4096]{1,0:T(8,128)(2,1)}, bf16[48,4096]{1,0:T(8,128)(2,1)S(1)}, u32[]{:S(2)}, u32[]{:S(2)}) collective-permute-start(bf16[48,4096]{1,0:T(8,128)(2,1)} %collective-permute-done.1.refs_5_), channel_id=1, source_target_pairs={{0,1},{1,0},{2,3},{3,2},{4,5},{5,4},{6,7},{7,6},{8,9},{9,8},{10,11... | collective-permute-start | bytes 1179656 | tf_op jit(solution)/shard_map/ppermute | solution.py:496
  66.8 5.8 %collective-permute-start.13 = (bf16[48,4096]{1,0:T(8,128)(2,1)S(1)}, bf16[48,4096]{1,0:T(8,128)(2,1)S(1)}, u32[]{:S(2)}, u32[]{:S(2)}) collective-permute-start(bf16[48,4096]{1,0:T(8,128)(2,1)S(1)} %collective-permute-done.7.refs_7_), channel_id=1, source_target_pairs={{0,1},{1,0},{2,3},{3,2},{4,5},{5,4},{6,7},{7,6},{8,9},{9,8},{10,11... | collective-permute-start | bytes 1179656 | tf_op jit(solution)/shard_map/ppermute | solution.py:496
  66.8 18.8 %collective-permute-start.9 = (bf16[48,4096]{1,0:T(8,128)(2,1)}, bf16[48,4096]{1,0:T(8,128)(2,1)S(1)}, u32[]{:S(2)}, u32[]{:S(2)}) collective-permute-start(bf16[48,4096]{1,0:T(8,128)(2,1)} %get-tuple-element.73.refs_4_), channel_id=1, source_target_pairs={{0,8},{8,16},{16,24},{24,0},{1,9},{9,17},{17,25},{25,1},{2,10},{10... | collective-permute-start | bytes 1179656 | tf_op jit(solution)/shard_map/ppermute | solution.py:492
  68.7 16.9 %collective-permute-start.10 = (bf16[48,4096]{1,0:T(8,128)(2,1)S(1)}, bf16[48,4096]{1,0:T(8,128)(2,1)S(1)}, u32[]{:S(2)}, u32[]{:S(2)}) collective-permute-start(bf16[48,4096]{1,0:T(8,128)(2,1)S(1)} %collective-permute-done.8.refs_6_), channel_id=1, source_target_pairs={{0,24},{8,0},{16,8},{24,16},{1,25},{9,1},{17,9},{25,17},{2,26},{10... | collective-permute-start | bytes 1179656 | tf_op jit(solution)/shard_map/ppermute | solution.py:492
  71.0 9.7 %collective-permute-start.16 = (bf16[8,2,48,128]{3,2,1,0:T(8,128)(2,1)S(1)}, bf16[8,2,48,128]{3,2,1,0:T(8,128)(2,1)S(1)}, u32[]{:S(2)}, u32[]{:S(2)}) collective-permute-start(bf16[8,2,48,128]{3,2,1,0:T(8,128)(2,1)S(1)} %bitcast.11), channel_id=1, source_target_pairs={{0,64},{64,128},{128,192},{192,0},{1,65},{65,129},{129,193},{193,1... | collective-permute-start | bytes 589832 | tf_op jit(solution)/shard_map/ppermute | solution.py:492
  72.6 9.3 %collective-permute-start.15 = (bf16[8,2,48,128]{3,2,1,0:T(8,128)(2,1)S(1)}, bf16[8,2,48,128]{3,2,1,0:T(8,128)(2,1)S(1)}, u32[]{:S(2)}, u32[]{:S(2)}) collective-permute-start(bf16[8,2,48,128]{3,2,1,0:T(8,128)(2,1)S(1)} %bitcast.12), channel_id=1, source_target_pairs={{0,128},{64,192},{128,0},{192,64},{1,129},{65,193},{129,1},{193,65... | collective-permute-start | bytes 589832 | tf_op jit(solution)/shard_map/ppermute | solution.py:492
  73.5 10.5 %collective-permute-start.14 = (bf16[8,2,48,128]{3,2,1,0:T(8,128)(2,1)S(1)}, bf16[8,2,48,128]{3,2,1,0:T(8,128)(2,1)S(1)}, u32[]{:S(2)}, u32[]{:S(2)}) collective-permute-start(bf16[8,2,48,128]{3,2,1,0:T(8,128)(2,1)S(1)} %bitcast.13), channel_id=1, source_target_pairs={{0,192},{64,0},{128,64},{192,128},{1,193},{65,1},{129,65},{193,129... | collective-permute-start | bytes 589832 | tf_op jit(solution)/shard_map/ppermute | solution.py:492
  80.7 5.4 %collective-permute-start.18 = (bf16[48,4096]{1,0:T(8,128)(2,1)S(1)}, bf16[48,4096]{1,0:T(8,128)(2,1)S(1)}, u32[]{:S(2)}, u32[]{:S(2)}) collective-permute-start(bf16[48,4096]{1,0:T(8,128)(2,1)S(1)} %collective-permute-done.8.refs_6_), channel_id=1, source_target_pairs={{0,1},{1,0},{2,3},{3,2},{4,5},{5,4},{6,7},{7,6},{8,9},{9,8},{10,11... | collective-permute-start | bytes 1179656 | tf_op jit(solution)/shard_map/ppermute | solution.py:496
  85.6 1.7 collective-permute-start.17
  85.7 2.2 %collective-permute-start.19 = (bf16[48,4096]{1,0:T(8,128)(2,1)S(1)}, bf16[48,4096]{1,0:T(8,128)(2,1)S(1)}, u32[]{:S(2)}, u32[]{:S(2)}) collective-permute-start(bf16[48,4096]{1,0:T(8,128)(2,1)S(1)} %collective-permute-done.10.refs_7_), channel_id=1, source_target_pairs={{0,1},{1,0},{2,3},{3,2},{4,5},{5,4},{6,7},{7,6},{8,9},{9,8},{10,11... | collective-permute-start | bytes 1179656 | tf_op jit(solution)/shard_map/ppermute | solution.py:496
  93.5 23.9 %all-to-all-start.1 = ((bf16[8,2,48,512]{3,2,1,0:T(8,128)(2,1)}), bf16[8,2,48,512]{3,2,1,0:T(8,128)(2,1)S(1)}, u32[]{:S(2)}, u32[]{:S(2)}) async-start(bf16[8,2,48,512]{3,2,1,0:T(8,128)(2,1)} %get-tuple-element.86), calls=%async_computation.1 | async-start | bytes 1572864 | tf_op jit(solution)/shard_map/all_to_all | solution.py:504
  98.4 15.6 %collective-permute-start.23 = (f32[8,512]{1,0:T(8,128)S(1)}, f32[8,512]{1,0:T(8,128)S(1)}, u32[]{:S(2)}, u32[]{:S(2)}) collective-permute-start(f32[8,512]{1,0:T(8,128)S(1)} %get-tuple-element.97.gain0_ref), channel_id=1, source_target_pairs={{0,6},{2,0},{4,2},{6,4},{1,7},{3,1},{5,3},{7,5},{8,14},{10,8},{12,... | collective-permute-start | bytes 49160 | tf_op jit(solution)/shard_map/ppermute | solution.py:492
  99.7 14.4 %collective-permute-start.22 = (f32[8,512]{1,0:T(8,128)S(1)}, f32[8,512]{1,0:T(8,128)S(1)}, u32[]{:S(2)}, u32[]{:S(2)}) collective-permute-start(f32[8,512]{1,0:T(8,128)S(1)} %get-tuple-element.97.gain0_ref), channel_id=1, source_target_pairs={{0,4},{2,6},{4,0},{6,2},{1,5},{3,7},{5,1},{7,3},{8,12},{10,14},{12... | collective-permute-start | bytes 49160 | tf_op jit(solution)/shard_map/ppermute | solution.py:492
  104.7 9.4 %collective-permute-start.21 = (f32[8,512]{1,0:T(8,128)S(1)}, f32[8,512]{1,0:T(8,128)S(1)}, u32[]{:S(2)}, u32[]{:S(2)}) collective-permute-start(f32[8,512]{1,0:T(8,128)S(1)} %get-tuple-element.97.gain0_ref), channel_id=1, source_target_pairs={{0,2},{2,4},{4,6},{6,0},{1,3},{3,5},{5,7},{7,1},{8,10},{10,12},{12... | collective-permute-start | bytes 49160 | tf_op jit(solution)/shard_map/ppermute | solution.py:492
  114.1 14.1 %collective-permute-start.24 = (bf16[2,64,2048]{2,1,0:T(8,128)(2,1)}, bf16[2,64,2048]{2,1,0:T(8,128)(2,1)S(1)}, u32[]{:S(2)}, u32[]{:S(2)}) collective-permute-start(bf16[2,64,2048]{2,1,0:T(8,128)(2,1)} %get-tuple-element.98), channel_id=1, source_target_pairs={{0,2},{2,4},{4,6},{6,0},{1,3},{3,5},{5,7},{7,1},{8,10},{10,12},{12... | collective-permute-start | bytes 1572872 | tf_op jit(solution)/shard_map/ppermute | solution.py:492
  114.2 14.0 %collective-permute-start.25 = (bf16[2,64,2048]{2,1,0:T(8,128)(2,1)}, bf16[2,64,2048]{2,1,0:T(8,128)(2,1)S(1)}, u32[]{:S(2)}, u32[]{:S(2)}) collective-permute-start(bf16[2,64,2048]{2,1,0:T(8,128)(2,1)} %get-tuple-element.99), channel_id=1, source_target_pairs={{0,6},{2,0},{4,2},{6,4},{1,7},{3,1},{5,3},{7,5},{8,14},{10,8},{12,... | collective-permute-start | bytes 1572872 | tf_op jit(solution)/shard_map/ppermute | solution.py:492
  118.3 14.8 %all-to-all-start.2 = ((bf16[8,16,512]{2,1,0:T(8,128)(2,1)}), bf16[8,16,512]{2,1,0:T(8,128)(2,1)S(1)}, u32[]{:S(2)}, u32[]{:S(2)}) async-start(bf16[8,16,512]{2,1,0:T(8,128)(2,1)} %layers.1), calls=%async_computation.2 | async-start | bytes 262144 | tf_op jit(solution)/shard_map/all_to_all | solution.py:504
  134.6 41.4 %all-to-all-start.3 = ((bf16[8,16,4096]{2,1,0:T(8,128)(2,1)}), bf16[8,16,4096]{2,1,0:T(8,128)(2,1)S(1)}, u32[]{:S(2)}, u32[]{:S(2)}) async-start(bf16[8,16,4096]{2,1,0:T(8,128)(2,1)} %encoder.1), calls=%async_computation.3 | async-start | bytes 2097152 | tf_op jit(solution)/shard_map/all_to_all | solution.py:504
  139.7 25.3 %collective-permute-start.26 = (bf16[2,128,2048]{2,1,0:T(8,128)(2,1)S(1)}, bf16[2,128,2048]{2,1,0:T(8,128)(2,1)S(1)}, u32[]{:S(2)}, u32[]{:S(2)}) collective-permute-start(bf16[2,128,2048]{2,1,0:T(8,128)(2,1)S(1)} %copy-done.6), channel_id=1, source_target_pairs={{0,2},{2,4},{4,6},{6,0},{1,3},{3,5},{5,7},{7,1},{8,10},{10,12},{12... | collective-permute-start | bytes 3145736 | tf_op jit(solution)/shard_map/ppermute | solution.py:492
  139.7 24.9 %collective-permute-start.27 = (bf16[2,128,2048]{2,1,0:T(8,128)(2,1)}, bf16[2,128,2048]{2,1,0:T(8,128)(2,1)S(1)}, u32[]{:S(2)}, u32[]{:S(2)}) collective-permute-start(bf16[2,128,2048]{2,1,0:T(8,128)(2,1)} %copy-done.7), channel_id=1, source_target_pairs={{0,6},{2,0},{4,2},{6,4},{1,7},{3,1},{5,3},{7,5},{8,14},{10,8},{12,... | collective-permute-start | bytes 3145736 | tf_op jit(solution)/shard_map/ppermute | solution.py:492
  142.9 32.1 %collective-permute-start.20 = (bf16[1,2,1,128,2048]{4,3,2,1,0:T(8,128)(2,1)}, bf16[1,2,1,128,2048]{4,3,2,1,0:T(8,128)(2,1)S(1)}, u32[]{:S(2)}, u32[]{:S(2)}) collective-permute-start(bf16[1,2,1,128,2048]{4,3,2,1,0:T(8,128)(2,1)} %get-tuple-element.87), channel_id=1, source_target_pairs={{32,0},{64,32},{96,64},{128,96},{160,128},{192,160},{224,192},{33,... | collective-permute-start | bytes 3145736 | tf_op jit(solution)/shard_map/ppermute | solution.py:558
  (8 other events, 147.6 us)

commit v2 on v1

--- a/solution.py
+++ b/solution.py
@@ -331,7 +331,7 @@
         relay_kernel,
         in_specs=[PIN, PIN, HBM, HBM],
         out_specs=[VMEM] * 2,
-        out_shape=[shape(near_p.shape)] * 2,
+        out_shape=[shape((2, 128, HD))] * 2,
         scratch_shapes=[
             pltpu.VMEM((2, 2, 128, HD), BF),
             pltpu.VMEM((2, 2, 64, HD), BF),
@@ -404,8 +404,7 @@
     mine = inverse * scaled - hidden * (inverse * inverse * inverse * row_mean)
     row = lax.broadcasted_iota(jnp.int32, (16, D), 0)
     packed = jnp.where(row < 2 * PIECE, mine, own).astype(BF)
-    for s in range(8):
-        out_ref[s] = packed
+    out_ref[...] = packed
 
 
 def encoder_rows(own, pre, gain):
@@ -413,7 +412,7 @@
         encoder_kernel,
         in_specs=[VMEM, VMEM, VMEM],
         out_specs=VMEM,
-        out_shape=shape((8, 16, D)),
+        out_shape=shape((16, D)),
         scratch_shapes=[pltpu.VMEM((16, D), BF)],
         compiler_params=params(),
         cost_estimate=cost(),
@@ -421,8 +420,15 @@
     )(own, pre, gain)
 
 
-def finish_kernel(packed_ref, gain_ref, out_ref, gain_out_ref):
-    packed = packed_ref[...].reshape(128, D)
+def finish_kernel(a_ref, b_ref, c_ref, d_ref, gain_ref, out_ref, gain_out_ref, packed_s, sems):
+    y, zlo = lax.axis_index("y"), lax.axis_index("zlo")
+    pairs = []
+    for r, ref in enumerate((a_ref, b_ref, c_ref, d_ref)):
+        for j in range(2):
+            rank = lax.rem(y + r, 4) * 2 + (zlo if j == 0 else 1 - zlo)
+            pairs.append((ref.at[j], packed_s.at[rank]))
+    wait_all(start_all(pairs, sems))
+    packed = packed_s[...].reshape(128, D)
     move = pick_rows(
         2 * SRC,
         128,
@@ -439,18 +445,20 @@
 def finish(packed, gain):
     return pl.pallas_call(
         finish_kernel,
-        in_specs=[VMEM, VMEM],
+        in_specs=[HBM] * 4 + [VMEM],
         out_specs=[VMEM, VMEM],
         out_shape=[shape((2 * SRC, D)), shape((1, D), F32)],
+        scratch_shapes=[pltpu.VMEM((8, 16, D), BF), pltpu.SemaphoreType.DMA((8,))],
         compiler_params=params(),
         cost_estimate=cost(),
         name="finish",
-    )(packed, gain)
+    )(*packed, gain)
 
 
 def add_kernel(*refs):
     terms, (key_out, value_out), (terms_s, sems) = refs[:3], refs[3:5], refs[5:]
-    wait_all(start_all([(ref, terms_s.at[i]) for i, ref in enumerate(terms)], sems))
+    pairs = [(ref.at[:, pl.ds(0, 128)], terms_s.at[i]) for i, ref in enumerate(terms)]
+    wait_all(start_all(pairs, sems))
     for half, out in enumerate((key_out, value_out)):
         total = terms_s[0, half].astype(F32) + terms_s[1, half].astype(F32)
         out[...] = (total + terms_s[2, half].astype(F32)).astype(BF)
@@ -465,7 +473,7 @@
         out_shape=[shape(dims[1:])] * 2,
         scratch_shapes=[pltpu.VMEM((3,) + dims, BF), pltpu.SemaphoreType.DMA((3,))],
         compiler_params=params(),
-        cost_estimate=cost(60),
+        cost_estimate=cost(400),
         name="add",
     )(*hold(terms[0]), *terms[1:])
 
@@ -483,7 +491,7 @@
         out_shape=pinned(value.shape),
         scratch_shapes=[pltpu.VMEM(value.shape, BF), pltpu.SemaphoreType.DMA((1,))],
         compiler_params=params(),
-        cost_estimate=cost(80),
+        cost_estimate=cost(400),
         name="hand",
     )(value)
 
@@ -502,16 +510,6 @@
 
 def exchange(value, axes):
     return lax.all_to_all(value, axes, split_axis=0, concat_axis=0, tiled=True)
-
-
-class Chain:
-    def __init__(self):
-        self.last = ()
-
-    def __call__(self, value, move, *others):
-        result = move(after(value, *self.last, *others))
-        self.last = (result,)
-        return result
 
 
 def body(pre_norm, norm_gain, queries, keys, values, head_grad, key_weight, value_weight):
@@ -519,26 +517,22 @@
     rows = batches * source_n
     gain = norm_gain.reshape(1, features)
     hidden = pre_norm.reshape(rows, features)
-    side = Chain()
-
-    blocks = memory_blocks(hidden, gain)
-    quarter = exchange(blocks, ZC).reshape(8, batches, source_n, 128)
-    queries = after(queries, blocks)
+
     local, own0, stacked = heads(queries, keys, values, head_grad, 0, key_weight, value_weight)
     minus0, plus0 = shift(own0, "zhi", 1), shift(own0, "zhi", -1)
-    own0_s = side(own0, swap)
-    stacked = after(stacked, own0_s)
+    own0_s = swap(own0)
     weight_m, weight_p = shift(stacked, "x", 1), shift(stacked, "x", -1)
-    local, own1 = heads(after(queries, own0), keys, values, head_grad, 1, local)
-    own1_s = side(own1, swap)
-    minus0, plus0, weight_m, weight_p, own1, own1_s, quarter = lax.optimization_barrier(
-        (minus0, plus0, weight_m, weight_p, own1, own1_s, quarter)
+    blocks = memory_blocks(after(hidden, own0), gain)
+    quarter = exchange(blocks, ZC).reshape(8, batches, source_n, 128)
+    local, own1 = heads(after(queries, blocks), keys, values, head_grad, 1, local)
+    minus0, plus0, weight_m, weight_p, own1, own0_s, quarter = lax.optimization_barrier(
+        (minus0, plus0, weight_m, weight_p, own1, own0_s, quarter)
     )
 
     far0 = shift(minus0, "zhi", 1)
     plus1 = shift(own1, "zhi", -1)
     weight_2 = shift(after(stacked, weight_m), "x", 2)
-    minus0_s, plus0_s = swap(minus0), swap(plus0)
+    minus0_s, plus0_s, own1_s = swap(minus0), swap(plus0), swap(own1)
     far0, plus1, quarter = lax.optimization_barrier((far0, plus1, quarter))
 
     minus1 = shift(after(own1, far0), "zhi", 1)
@@ -556,7 +550,7 @@
     returned, gain_part, all1 = return_blocks(1, weights, blocks1, columns, plain, returned)
     layers = exchange(returned, SEC)
     query_in = lax.ppermute(
-        after(local, layers), SEC, [(s, s - 1) for s in range(1, 8)]
+        after(local, minus1_s, far1_s), SEC, [(s, s - 1) for s in range(1, 8)]
     )
     gains = [gain_part] + [shift(gain_part, "x", r) for r in (1, 2, 3)]
     part = weight_blocks(after(flipped, returned), all0, all1)
@@ -565,12 +559,14 @@
     far_p, far_m = lax.optimization_barrier((part[3], part[4], *gains))[:2]
     far_p, far_m = shift(far_p, "x", 1), shift(far_m, "x", -1)
     near_p, near_m = relay_blocks(part[1], part[2], far_p, far_m)
-    packed = encoder_rows(after(own, near_p), hidden, gain)
+    packed = encoder_rows(after(own, near_p, query_in), hidden, gain)
     near_p, near_m = shift(near_p, "x", 1), shift(near_m, "x", -1)
-    packed = exchange(packed, SEC)
+    other = lax.ppermute(packed, "zlo", [(0, 1), (1, 0)])
+    packed = jnp.stack([packed, other])
+    packed = [packed] + [shift(packed, "y", -r) for r in (1, 2, 3)]
     grad_key, grad_value = add_blocks(part[0], near_p, near_m)
     query_grad = hand_on(query_in)
-    encoder_grad, gain_grad = finish(after(packed, grad_key, query_grad), gain)
+    encoder_grad, gain_grad = finish(packed, gain)
     return (
         query_grad,
         grad_key[None],

time: 178 us -> 161 us (0.904)
  blocking collectives: 21 us -> 0 us
  starting transfers between devices: 56.7 us -> 70.1 us
  waiting for transfers between devices: 56.3 us -> 44.4 us
  Pallas kernels: 40.5 us -> 43.3 us
    all_to_all x1 -> x0, blocking collectives: 21 us -> none  [exchange(): return lax.all_to_all(value, axes, split_axis=0, concat_axis=0, tiled=True)]
    ppermute x19 -> x22, waiting for transfers between devices: 43.8 us -> 27.4 us  [shift(): return lax.ppermute(value, axis, [(i, (i + step) % 4) for i in range(4)])]
    all_to_all x3, waiting for transfers between devices: 1.23 us -> 11.6 us  [exchange(): return lax.all_to_all(value, axes, split_axis=0, concat_axis=0, tiled=True)]
    all_to_all x3, starting transfers between devices: 15 us -> 22.9 us  [exchange(): return lax.all_to_all(value, axes, split_axis=0, concat_axis=0, tiled=True)]
    ppermute x1 -> x2, waiting for transfers between devices: 7.52 us -> 3.58 us  [the longest x1 3.57 us: body(): other = lax.ppermute(packed, 'zlo', [(0, 1), (1, 0)])]
    ppermute x19 -> x22, starting transfers between devices: 37.2 us -> 40.6 us  [shift(): return lax.ppermute(value, axis, [(i, (i + step) % 4) for i in range(4)])]
    ppermute x8, waiting for transfers between devices: 3.7 us -> 1.78 us  [swap(): return lax.ppermute(value, 'core', [(0, 1), (1, 0)])]
    ppermute x1 -> x2, starting transfers between devices: 3.36 us -> 4.92 us  [the longest x1 3.36 us: body(): lax.ppermute(after(local, minus1_s, far1_s), SEC, [(s, s - 1) for s in ra...]
  transfers between devices with their start and end apart: 31 -> 35, of which waited for: 13 -> 13; matrix products, arithmetic and copies ran while one was open for 0% -> 0% of each run, Pallas kernels for 14% -> 19%
where the time goes in v2:
time: 161 us; the launch traced here: 160 us
  starting transfers between devices  70.1 us (44%)
  waiting for transfers between devices  44.4 us (28%)
  Pallas kernels  43.3 us (27%)
    ppermute x22, starting transfers between devices, shift(): return lax.ppermute(value, axis, [(i, (i + step) % 4) for i in range(4)])  40.6 us
    ppermute x22, waiting for transfers between devices, shift(): return lax.ppermute(value, axis, [(i, (i + step) % 4) for i in range(4)])  27.4 us
    all_to_all x3, starting transfers between devices, exchange(): return lax.all_to_all(value, axes, split_axis=0, concat_axis=0, tiled=True)  22.9 us
    all_to_all x3, waiting for transfers between devices, exchange(): return lax.all_to_all(value, axes, split_axis=0, concat_axis=0, tiled=True)  11.6 us
    pallas_call x2, Pallas kernels, return_blocks(): pl.pallas_call(functools.partial(return_kernel, m), in_specs=[HBM] * 12 +...  10.3 us
    pallas_call x2, Pallas kernels, heads(): pl.pallas_call(functools.partial(heads_kernel, m == 0), grid=(1,), in_spe...  9.77 us
    pallas_call x1, Pallas kernels, weight_blocks(): pl.pallas_call(weight_kernel, in_specs=[PIN] * 3, out_specs=[PIN] * 3 + [...  7.95 us
    ppermute x1, waiting for transfers between devices, body(): other = lax.ppermute(packed, 'zlo', [(0, 1), (1, 0)])  3.57 us
  transfers between devices with their start and end apart: 35, of which 13 were waited for; matrix products, arithmetic and copies ran while one was open for 0% of the time, Pallas kernels for 19%

profile of v2, /device:TPU:8, one launch (start us, length us, event | category | flops | bytes accessed | tf_op | source)
XLA Modules:
  0.0 159.9 jit_solution(2566153007347196990)
XLA Ops:
  0.6 5.2 %heads.2 = (bf16[1,2,1,128,2048]{4,3,2,1,0:T(8,128)(2,1)}, bf16[48,4096]{1,0:T(8,128)(2,1)}, bf16[2,128,2048]{2,1,0:T(8,128)(2,1)}) custom-call(bf16[1,2,1,128,2048]{4,3,2,1,0:T(8,128)(2,1)} %q_ref.2, bf16[1,2,1,48,2048]{4,3,2,1,0:T(8,128)(2,1)} %k_ref.3, bf16[1,2,1,48,2048]{4,3,2,1,0:T(8,128)(2,1)} %v_ref.3, bf16[1,2,1,128,2048]{4,3,2,1,0:T(8,128)(2,1)} %g_ref.3, ...), custom_call_target="tpu_custom_call" | custom-call | bytes 41943040 | tf_op jit(solution)/shard_map/heads/pallas_call | solution.py:106
  5.9 2.8 %collective-permute-start.3 = (bf16[2,128,2048]{2,1,0:T(8,128)(2,1)}, bf16[2,128,2048]{2,1,0:T(8,128)(2,1)S(1)}, u32[]{:S(2)}, u32[]{:S(2)}) collective-permute-start(bf16[2,128,2048]{2,1,0:T(8,128)(2,1)} %get-tuple-element.70.refs_0_), channel_id=1, source_target_pairs={{0,6},{2,0},{4,2},{6,4},{1,7},{3,1},{5,3},{7,5},{8,14},{10,8},{12,... | collective-permute-start | bytes 3145736 | tf_op jit(solution)/shard_map/ppermute | solution.py:500
  8.6 6.3 %collective-permute-start.1 = (bf16[48,4096]{1,0:T(8,128)(2,1)}, bf16[48,4096]{1,0:T(8,128)(2,1)}, u32[]{:S(2)}, u32[]{:S(2)}) collective-permute-start(bf16[48,4096]{1,0:T(8,128)(2,1)} %get-tuple-element.54.refs_4_), channel_id=1, source_target_pairs={{0,24},{8,0},{16,8},{24,16},{1,25},{9,1},{17,9},{25,17},{2,26},{10... | collective-permute-start | bytes 1179656 | tf_op jit(solution)/shard_map/ppermute | solution.py:500
  14.9 2.1 %memory.1 = bf16[8,96,128]{2,1,0:T(8,128)(2,1)} custom-call(bf16[96,4096]{1,0:T(8,128)(2,1)} %bitcast.11, f32[1,4096]{1,0:T(1,128)} %bitcast.18), custom_call_target="tpu_custom_call" | custom-call | tf_op jit(solution)/shard_map/memory/pallas_call | solution.py:135
  17.0 5.4 %all-to-all-start = ((bf16[8,96,128]{2,1,0:T(8,128)(2,1)}), bf16[8,96,128]{2,1,0:T(8,128)(2,1)S(1)}, u32[]{:S(2)}, u32[]{:S(2)}) async-start(bf16[8,96,128]{2,1,0:T(8,128)(2,1)} %memory.1), calls=%async_computation | async-start | bytes 393216 | tf_op jit(solution)/shard_map/all_to_all | solution.py:512
  22.4 4.6 %heads.3 = (bf16[1,2,1,128,2048]{4,3,2,1,0:T(8,128)(2,1)}, bf16[48,4096]{1,0:T(8,128)(2,1)}) custom-call(bf16[1,2,1,128,2048]{4,3,2,1,0:T(8,128)(2,1)} %q_ref.2, bf16[1,2,1,48,2048]{4,3,2,1,0:T(8,128)(2,1)} %k_ref.3, bf16[1,2,1,48,2048]{4,3,2,1,0:T(8,128)(2,1)} %v_ref.3, bf16[1,2,1,128,2048]{4,3,2,1,0:T(8,128)(2,1)} %g_ref.3, ...), custom_call_target="tpu_custom_call", output_to_operand_aliasing={{0}: (4, {})} | custom-call | bytes 41943040 | tf_op jit(solution)/shard_map/heads/pallas_call | solution.py:106
  26.9 9.9 %all-to-all-done = bf16[8,96,128]{2,1,0:T(8,128)(2,1)S(1)} async-done(((bf16[8,96,128]{2,1,0:T(8,128)(2,1)}), bf16[8,96,128]{2,1,0:T(8,128)(2,1)S(1)}, u32[]{:S(2)}, u32[]{:S(2)}) %all-to-all-start) | async-done | bytes 196640 | tf_op jit(solution)/shard_map/all_to_all | solution.py:512
  37.0 2.4 %collective-permute-start.9 = (bf16[2,128,2048]{2,1,0:T(8,128)(2,1)S(1)}, bf16[2,128,2048]{2,1,0:T(8,128)(2,1)S(1)}, u32[]{:S(2)}, u32[]{:S(2)}) collective-permute-start(bf16[2,128,2048]{2,1,0:T(8,128)(2,1)S(1)} %copy-done), channel_id=1, source_target_pairs={{0,4},{2,6},{4,0},{6,2},{1,5},{3,7},{5,1},{7,3},{8,12},{10,14},{12... | collective-permute-start | bytes 3145736 | tf_op jit(solution)/shard_map/ppermute | solution.py:500
  39.3 6.2 %collective-permute-start.5 = (bf16[48,4096]{1,0:T(8,128)(2,1)}, bf16[48,4096]{1,0:T(8,128)(2,1)S(1)}, u32[]{:S(2)}, u32[]{:S(2)}) collective-permute-start(bf16[48,4096]{1,0:T(8,128)(2,1)} %collective-permute-done.refs_5_), channel_id=1, source_target_pairs={{0,8},{8,16},{16,24},{24,0},{1,9},{9,17},{17,25},{25,1},{2,10},{10... | collective-permute-start | bytes 1179656 | tf_op jit(solution)/shard_map/ppermute | solution.py:500
  46.0 7.8 %collective-permute-done.5.refs_7_ = bf16[48,4096]{1,0:T(8,128)(2,1)S(1)} collective-permute-done((bf16[48,4096]{1,0:T(8,128)(2,1)}, bf16[48,4096]{1,0:T(8,128)(2,1)S(1)}, u32[]{:S(2)}, u32[]{:S(2)}) %collective-permute-start.5) | collective-permute-done | bytes 393248 | tf_op jit(solution)/shard_map/ppermute | solution.py:500
  56.3 2.9 %collective-permute-start.8 = (bf16[48,4096]{1,0:T(8,128)(2,1)S(1)}, bf16[48,4096]{1,0:T(8,128)(2,1)S(1)}, u32[]{:S(2)}, u32[]{:S(2)}) collective-permute-start(bf16[48,4096]{1,0:T(8,128)(2,1)S(1)} %collective-permute-done.6.refs_6_), channel_id=1, source_target_pairs={{0,24},{8,0},{16,8},{24,16},{1,25},{9,1},{17,9},{25,17},{2,26},{10... | collective-permute-start | bytes 1179656 | tf_op jit(solution)/shard_map/ppermute | solution.py:500
  65.2 4.8 %returned.2 = (bf16[8,2,48,512]{3,2,1,0:T(8,128)(2,1)}, bf16[384,512]{1,0:T(8,128)(2,1)}, bf16[2,8,48,2048]{3,2,1,0:T(8,128)(2,1)}) custom-call(bf16[2,128,2048]{2,1,0:T(8,128)(2,1)S(1)} %copy-done, bf16[2,128,2048]{2,1,0:T(8,128)(2,1)S(1)} %collective-permute-done.3.refs_1_, bf16[2,128,2048]{2,1,0:T(8,128)(2,1)S(1)} %collective-permute-done.9.refs_2_, ...), custom_call_target="tpu_custom_call" | custom-call | tf_op jit(solution)/shard_map/returned/pallas_call | solution.py:260
  70.6 2.3 %collective-permute-done.13.refs_1_ = bf16[8,2,48,128]{3,2,1,0:T(8,128)(2,1)S(1)} collective-permute-done((bf16[8,2,48,128]{3,2,1,0:T(8,128)(2,1)S(1)}, bf16[8,2,48,128]{3,2,1,0:T(8,128)(2,1)S(1)}, u32[]{:S(2)}, u32[]{:S(2)}) %collective-permute-start.13) | collective-permute-done | bytes 196640 | tf_op jit(solution)/shard_map/ppermute | solution.py:500
  76.7 5.5 %returned.3 = (bf16[8,2,48,512]{3,2,1,0:T(8,128)(2,1)}, f32[8,512]{1,0:T(8,128)S(1)}, bf16[2,8,48,2048]{3,2,1,0:T(8,128)(2,1)}) custom-call(bf16[2,128,2048]{2,1,0:T(8,128)(2,1)S(1)} %copy-done, bf16[2,128,2048]{2,1,0:T(8,128)(2,1)S(1)} %collective-permute-done.3.refs_1_, ...), custom_call_target="tpu_custom_call", output_to_operand_aliasing={{0}: (14, {})} | custom-call | tf_op jit(solution)/shard_map/returned/pallas_call | solution.py:260
  82.2 12.9 %all-to-all-start.1 = ((bf16[8,2,48,512]{3,2,1,0:T(8,128)(2,1)}), bf16[8,2,48,512]{3,2,1,0:T(8,128)(2,1)S(1)}, u32[]{:S(2)}, u32[]{:S(2)}) async-start(bf16[8,2,48,512]{3,2,1,0:T(8,128)(2,1)} %get-tuple-element.83), calls=%async_computation.1 | async-start | bytes 1572864 | tf_op jit(solution)/shard_map/all_to_all | solution.py:512
  95.1 3.4 %collective-permute-start.18 = (bf16[1,2,1,128,2048]{4,3,2,1,0:T(8,128)(2,1)}, bf16[1,2,1,128,2048]{4,3,2,1,0:T(8,128)(2,1)}, u32[]{:S(2)}, u32[]{:S(2)}) collective-permute-start(bf16[1,2,1,128,2048]{4,3,2,1,0:T(8,128)(2,1)} %get-tuple-element.79), channel_id=1, source_target_pairs={{32,0},{64,32},{96,64},{128,96},{160,128},{192,160},{224,192},{33,... | collective-permute-start | bytes 3145736 | tf_op jit(solution)/shard_map/ppermute | solution.py:552
  99.9 2.5 %collective-permute-start.22 = (f32[8,512]{1,0:T(8,128)S(1)}, f32[8,512]{1,0:T(8,128)S(1)}, u32[]{:S(2)}, u32[]{:S(2)}) collective-permute-start(f32[8,512]{1,0:T(8,128)S(1)} %get-tuple-element.92.gain0_ref), channel_id=1, source_target_pairs={{0,4},{2,6},{4,0},{6,2},{1,5},{3,7},{5,1},{7,3},{8,12},{10,14},{12... | collective-permute-start | bytes 49160 | tf_op jit(solution)/shard_map/ppermute | solution.py:500
  102.4 8.0 %weights.1 = (bf16[2,128,2048]{2,1,0:T(8,128)(2,1)}, bf16[2,128,2048]{2,1,0:T(8,128)(2,1)}, bf16[2,128,2048]{2,1,0:T(8,128)(2,1)}, bf16[2,64,2048]{2,1,0:T(8,128)(2,1)}, bf16[2,64,2048]{2,1,0:T(8,128)(2,1)}) custom-call(bf16[512,768]{1,0:T(8,128)(2,1)} %get-tuple-element.84.flip_ref, bf16[2,8,48,2048]{3,2,1,0:T(8,128)(2,1)} %get-tuple-element.85.first_ref, ...), custom_call_target="tpu_custom_call" | custom-call | tf_op jit(solution)/shard_map/weights/pallas_call | solution.py:298
  111.5 2.3 %collective-permute-start.25 = (bf16[2,64,2048]{2,1,0:T(8,128)(2,1)}, bf16[2,64,2048]{2,1,0:T(8,128)(2,1)S(1)}, u32[]{:S(2)}, u32[]{:S(2)}) collective-permute-start(bf16[2,64,2048]{2,1,0:T(8,128)(2,1)} %get-tuple-element.94), channel_id=1, source_target_pairs={{0,6},{2,0},{4,2},{6,4},{1,7},{3,1},{5,3},{7,5},{8,14},{10,8},{12,... | collective-permute-start | bytes 1572872 | tf_op jit(solution)/shard_map/ppermute | solution.py:500
  114.8 4.6 %all-to-all-start.2 = ((bf16[8,16,512]{2,1,0:T(8,128)(2,1)}), bf16[8,16,512]{2,1,0:T(8,128)(2,1)S(1)}, u32[]{:S(2)}, u32[]{:S(2)}) async-start(bf16[8,16,512]{2,1,0:T(8,128)(2,1)} %layers.1), calls=%async_computation.2 | async-start | bytes 262144 | tf_op jit(solution)/shard_map/all_to_all | solution.py:512
  119.4 5.1 %collective-permute-done.24.far_p = bf16[2,64,2048]{2,1,0:T(8,128)(2,1)S(1)} collective-permute-done((bf16[2,64,2048]{2,1,0:T(8,128)(2,1)}, bf16[2,64,2048]{2,1,0:T(8,128)(2,1)S(1)}, u32[]{:S(2)}, u32[]{:S(2)}) %collective-permute-start.24) | collective-permute-done | bytes 524320 | tf_op jit(solution)/shard_map/ppermute | solution.py:500
  124.5 3.1 %relay.1 = (bf16[2,128,2048]{2,1,0:T(8,128)(2,1)}, bf16[2,128,2048]{2,1,0:T(8,128)(2,1)}) custom-call(bf16[2,128,2048]{2,1,0:T(8,128)(2,1)} %get-tuple-element.88.near_p, bf16[2,128,2048]{2,1,0:T(8,128)(2,1)} %get-tuple-element.89.near_m, bf16[2,64,2048]{2,1,0:T(8,128)(2,1)S(1)} %collective-permute-done.24.far_p, ...), custom_call_target="tpu_custom_call" | custom-call | tf_op jit(solution)/shard_map/relay/pallas_call | solution.py:330
  127.6 3.1 %collective-permute-start.27 = (bf16[2,128,2048]{2,1,0:T(8,128)(2,1)}, bf16[2,128,2048]{2,1,0:T(8,128)(2,1)S(1)}, u32[]{:S(2)}, u32[]{:S(2)}) collective-permute-start(bf16[2,128,2048]{2,1,0:T(8,128)(2,1)} %get-tuple-element.96), channel_id=1, source_target_pairs={{0,6},{2,0},{4,2},{6,4},{1,7},{3,1},{5,3},{7,5},{8,14},{10,8},{12,... | collective-permute-start | bytes 3145736 | tf_op jit(solution)/shard_map/ppermute | solution.py:500
  130.8 1.7 %all-to-all-done.2.own_ref = bf16[8,16,512]{2,1,0:T(8,128)(2,1)S(1)} async-done(((bf16[8,16,512]{2,1,0:T(8,128)(2,1)}), bf16[8,16,512]{2,1,0:T(8,128)(2,1)S(1)}, u32[]{:S(2)}, u32[]{:S(2)}) %all-to-all-start.2) | async-done | bytes 131104 | tf_op jit(solution)/shard_map/all_to_all | solution.py:512
  134.4 3.6 %collective-permute-done.28 = bf16[16,4096]{1,0:T(8,128)(2,1)S(1)} collective-permute-done((bf16[16,4096]{1,0:T(8,128)(2,1)S(1)}, bf16[16,4096]{1,0:T(8,128)(2,1)S(1)}, u32[]{:S(2)}, u32[]{:S(2)}) %collective-permute-start.28) | collective-permute-done | bytes 131104 | tf_op jit(solution)/shard_map/ppermute | solution.py:564
  138.0 2.1 %collective-permute-start.31 = (bf16[2,16,4096]{2,1,0:T(8,128)(2,1)S(1)}, bf16[2,16,4096]{2,1,0:T(8,128)(2,1)S(1)}, u32[]{:S(2)}, u32[]{:S(2)}) collective-permute-start(bf16[2,16,4096]{2,1,0:T(8,128)(2,1)S(1)} %pad_maximum_fusion.a_ref), channel_id=1, source_target_pairs={{0,64},{64,128},{128,192},{192,0},{1,65},{65,129},{129,193},{193,1... | collective-permute-start | bytes 786440 | tf_op jit(solution)/shard_map/ppermute | solution.py:500
  140.4 2.3 %collective-permute-start.29 = (bf16[2,16,4096]{2,1,0:T(8,128)(2,1)S(1)}, bf16[2,16,4096]{2,1,0:T(8,128)(2,1)S(1)}, u32[]{:S(2)}, u32[]{:S(2)}) collective-permute-start(bf16[2,16,4096]{2,1,0:T(8,128)(2,1)S(1)} %pad_maximum_fusion.a_ref), channel_id=1, source_target_pairs={{0,192},{64,0},{128,64},{192,128},{1,193},{65,1},{129,65},{193,129... | collective-permute-start | bytes 786440 | tf_op jit(solution)/shard_map/ppermute | solution.py:500
  142.7 2.2 %hand.1 = bf16[1,2,1,128,2048]{4,3,2,1,0:T(8,128)(2,1)} custom-call(bf16[1,2,1,128,2048]{4,3,2,1,0:T(8,128)(2,1)} %collective-permute-done.18.in_ref), custom_call_target="tpu_custom_call" | custom-call | bytes 419430400 | tf_op jit(solution)/shard_map/hand/pallas_call | solution.py:487
  145.0 6.2 %collective-permute-done.27.refs_2_ = bf16[2,128,2048]{2,1,0:T(8,128)(2,1)S(1)} collective-permute-done((bf16[2,128,2048]{2,1,0:T(8,128)(2,1)}, bf16[2,128,2048]{2,1,0:T(8,128)(2,1)S(1)}, u32[]{:S(2)}, u32[]{:S(2)}) %collective-permute-start.27) | collective-permute-done | bytes 1048608 | tf_op jit(solution)/shard_map/ppermute | solution.py:500
  151.2 3.3 %collective-permute-done.26.refs_1_ = bf16[2,128,2048]{2,1,0:T(8,128)(2,1)S(1)} collective-permute-done((bf16[2,128,2048]{2,1,0:T(8,128)(2,1)}, bf16[2,128,2048]{2,1,0:T(8,128)(2,1)S(1)}, u32[]{:S(2)}, u32[]{:S(2)}) %collective-permute-start.26) | collective-permute-done | bytes 1048608 | tf_op jit(solution)/shard_map/ppermute | solution.py:500
  154.5 2.4 %add.1 = (bf16[128,2048]{1,0:T(8,128)(2,1)}, bf16[128,2048]{1,0:T(8,128)(2,1)}) custom-call(bf16[2,128,2048]{2,1,0:T(8,128)(2,1)} %get-tuple-element.87.refs_0_, bf16[2,128,2048]{2,1,0:T(8,128)(2,1)S(1)} %collective-permute-done.26.refs_1_, bf16[2,128,2048]{2,1,0:T(8,128)(2,1)S(1)} %collective-permute-done.27.refs_2_), custom_call_target="tpu_custom_call" | custom-call | bytes 419430400 | tf_op jit(solution)/shard_map/add/pallas_call | solution.py:469
  156.9 2.8 %finish.1 = (bf16[96,4096]{1,0:T(8,128)(2,1)}, f32[1,4096]{1,0:T(1,128)}) custom-call(bf16[2,16,4096]{2,1,0:T(8,128)(2,1)S(1)} %pad_maximum_fusion.a_ref, bf16[2,16,4096]{2,1,0:T(8,128)(2,1)S(1)} %collective-permute-done.29.b_ref, bf16[2,16,4096]{2,1,0:T(8,128)(2,1)S(1)} %collective-permute-done.30.c_ref, ...), custom_call_target="tpu_custom_call" | custom-call | tf_op jit(solution)/shard_map/finish/pallas_call | solution.py:446
  (62 shorter events, 19.1 us)
Async XLA Ops:
  5.9 31.1 %collective-permute-start.3 = (bf16[2,128,2048]{2,1,0:T(8,128)(2,1)}, bf16[2,128,2048]{2,1,0:T(8,128)(2,1)S(1)}, u32[]{:S(2)}, u32[]{:S(2)}) collective-permute-start(bf16[2,128,2048]{2,1,0:T(8,128)(2,1)} %get-tuple-element.70.refs_0_), channel_id=1, source_target_pairs={{0,6},{2,0},{4,2},{6,4},{1,7},{3,1},{5,3},{7,5},{8,14},{10,8},{12,... | collective-permute-start | bytes 3145736 | tf_op jit(solution)/shard_map/ppermute | solution.py:500
  8.6 28.3 %collective-permute-start.2 = (bf16[2,128,2048]{2,1,0:T(8,128)(2,1)}, bf16[2,128,2048]{2,1,0:T(8,128)(2,1)S(1)}, u32[]{:S(2)}, u32[]{:S(2)}) collective-permute-start(bf16[2,128,2048]{2,1,0:T(8,128)(2,1)} %get-tuple-element.70.refs_0_), channel_id=1, source_target_pairs={{0,2},{2,4},{4,6},{6,0},{1,3},{3,5},{5,7},{7,1},{8,10},{10,12},{12... | collective-permute-start | bytes 3145736 | tf_op jit(solution)/shard_map/ppermute | solution.py:500
  8.6 28.3 %collective-permute-start.4 = (bf16[48,4096]{1,0:T(8,128)(2,1)}, bf16[48,4096]{1,0:T(8,128)(2,1)}, u32[]{:S(2)}, u32[]{:S(2)}) collective-permute-start(bf16[48,4096]{1,0:T(8,128)(2,1)} %get-tuple-element.54.refs_4_), channel_id=1, source_target_pairs={{0,1},{1,0},{2,3},{3,2},{4,5},{5,4},{6,7},{7,6},{8,9},{9,8},{10,11... | collective-permute-start | bytes 1179656 | tf_op jit(solution)/shard_map/ppermute | solution.py:504
  8.6 28.3 %collective-permute-start.1 = (bf16[48,4096]{1,0:T(8,128)(2,1)}, bf16[48,4096]{1,0:T(8,128)(2,1)}, u32[]{:S(2)}, u32[]{:S(2)}) collective-permute-start(bf16[48,4096]{1,0:T(8,128)(2,1)} %get-tuple-element.54.refs_4_), channel_id=1, source_target_pairs={{0,24},{8,0},{16,8},{24,16},{1,25},{9,1},{17,9},{25,17},{2,26},{10... | collective-permute-start | bytes 1179656 | tf_op jit(solution)/shard_map/ppermute | solution.py:500
  14.9 22.0 %collective-permute-start = (bf16[48,4096]{1,0:T(8,128)(2,1)}, bf16[48,4096]{1,0:T(8,128)(2,1)}, u32[]{:S(2)}, u32[]{:S(2)}) collective-permute-start(bf16[48,4096]{1,0:T(8,128)(2,1)} %get-tuple-element.54.refs_4_), channel_id=1, source_target_pairs={{0,8},{8,16},{16,24},{24,0},{1,9},{9,17},{17,25},{25,1},{2,10},{10... | collective-permute-start | bytes 1179656 | tf_op jit(solution)/shard_map/ppermute | solution.py:500
  17.0 19.9 %all-to-all-start = ((bf16[8,96,128]{2,1,0:T(8,128)(2,1)}), bf16[8,96,128]{2,1,0:T(8,128)(2,1)S(1)}, u32[]{:S(2)}, u32[]{:S(2)}) async-start(bf16[8,96,128]{2,1,0:T(8,128)(2,1)} %memory.1), calls=%async_computation | async-start | bytes 393216 | tf_op jit(solution)/shard_map/all_to_all | solution.py:512
  37.0 26.2 %collective-permute-start.9 = (bf16[2,128,2048]{2,1,0:T(8,128)(2,1)S(1)}, bf16[2,128,2048]{2,1,0:T(8,128)(2,1)S(1)}, u32[]{:S(2)}, u32[]{:S(2)}) collective-permute-start(bf16[2,128,2048]{2,1,0:T(8,128)(2,1)S(1)} %copy-done), channel_id=1, source_target_pairs={{0,4},{2,6},{4,0},{6,2},{1,5},{3,7},{5,1},{7,3},{8,12},{10,14},{12... | collective-permute-start | bytes 3145736 | tf_op jit(solution)/shard_map/ppermute | solution.py:500
  39.3 14.5 %collective-permute-start.5 = (bf16[48,4096]{1,0:T(8,128)(2,1)}, bf16[48,4096]{1,0:T(8,128)(2,1)S(1)}, u32[]{:S(2)}, u32[]{:S(2)}) collective-permute-start(bf16[48,4096]{1,0:T(8,128)(2,1)} %collective-permute-done.refs_5_), channel_id=1, source_target_pairs={{0,8},{8,16},{16,24},{24,0},{1,9},{9,17},{17,25},{25,1},{2,10},{10... | collective-permute-start | bytes 1179656 | tf_op jit(solution)/shard_map/ppermute | solution.py:500
  45.5 9.6 %collective-permute-start.6 = (bf16[48,4096]{1,0:T(8,128)(2,1)}, bf16[48,4096]{1,0:T(8,128)(2,1)S(1)}, u32[]{:S(2)}, u32[]{:S(2)}) collective-permute-start(bf16[48,4096]{1,0:T(8,128)(2,1)} %get-tuple-element.65.refs_4_), channel_id=1, source_target_pairs={{0,24},{8,0},{16,8},{24,16},{1,25},{9,1},{17,9},{25,17},{2,26},{10... | collective-permute-start | bytes 1179656 | tf_op jit(solution)/shard_map/ppermute | solution.py:500
  45.5 10.8 %collective-permute-start.11 = (bf16[48,4096]{1,0:T(8,128)(2,1)}, bf16[48,4096]{1,0:T(8,128)(2,1)S(1)}, u32[]{:S(2)}, u32[]{:S(2)}) collective-permute-start(bf16[48,4096]{1,0:T(8,128)(2,1)} %collective-permute-done.1.refs_6_), channel_id=1, source_target_pairs={{0,1},{1,0},{2,3},{3,2},{4,5},{5,4},{6,7},{7,6},{8,9},{9,8},{10,11... | collective-permute-start | bytes 1179656 | tf_op jit(solution)/shard_map/ppermute | solution.py:504
  45.5 13.7 %collective-permute-start.10 = (bf16[48,4096]{1,0:T(8,128)(2,1)}, bf16[48,4096]{1,0:T(8,128)(2,1)S(1)}, u32[]{:S(2)}, u32[]{:S(2)}) collective-permute-start(bf16[48,4096]{1,0:T(8,128)(2,1)} %collective-permute-done.refs_5_), channel_id=1, source_target_pairs={{0,1},{1,0},{2,3},{3,2},{4,5},{5,4},{6,7},{7,6},{8,9},{9,8},{10,11... | collective-permute-start | bytes 1179656 | tf_op jit(solution)/shard_map/ppermute | solution.py:504
  55.1 5.8 %collective-permute-start.12 = (bf16[48,4096]{1,0:T(8,128)(2,1)S(1)}, bf16[48,4096]{1,0:T(8,128)(2,1)S(1)}, u32[]{:S(2)}, u32[]{:S(2)}) collective-permute-start(bf16[48,4096]{1,0:T(8,128)(2,1)S(1)} %collective-permute-done.5.refs_7_), channel_id=1, source_target_pairs={{0,1},{1,0},{2,3},{3,2},{4,5},{5,4},{6,7},{7,6},{8,9},{9,8},{10,11... | collective-permute-start | bytes 1179656 | tf_op jit(solution)/shard_map/ppermute | solution.py:504
  55.1 19.2 %collective-permute-start.7 = (bf16[48,4096]{1,0:T(8,128)(2,1)}, bf16[48,4096]{1,0:T(8,128)(2,1)S(1)}, u32[]{:S(2)}, u32[]{:S(2)}) collective-permute-start(bf16[48,4096]{1,0:T(8,128)(2,1)} %get-tuple-element.65.refs_4_), channel_id=1, source_target_pairs={{0,8},{8,16},{16,24},{24,0},{1,9},{9,17},{17,25},{25,1},{2,10},{10... | collective-permute-start | bytes 1179656 | tf_op jit(solution)/shard_map/ppermute | solution.py:500
  56.3 18.0 %collective-permute-start.8 = (bf16[48,4096]{1,0:T(8,128)(2,1)S(1)}, bf16[48,4096]{1,0:T(8,128)(2,1)S(1)}, u32[]{:S(2)}, u32[]{:S(2)}) collective-permute-start(bf16[48,4096]{1,0:T(8,128)(2,1)S(1)} %collective-permute-done.6.refs_6_), channel_id=1, source_target_pairs={{0,24},{8,0},{16,8},{24,16},{1,25},{9,1},{17,9},{25,17},{2,26},{10... | collective-permute-start | bytes 1179656 | tf_op jit(solution)/shard_map/ppermute | solution.py:500
  59.2 10.7 %collective-permute-start.15 = (bf16[8,2,48,128]{3,2,1,0:T(8,128)(2,1)S(1)}, bf16[8,2,48,128]{3,2,1,0:T(8,128)(2,1)S(1)}, u32[]{:S(2)}, u32[]{:S(2)}) collective-permute-start(bf16[8,2,48,128]{3,2,1,0:T(8,128)(2,1)S(1)} %bitcast.13), channel_id=1, source_target_pairs={{0,64},{64,128},{128,192},{192,0},{1,65},{65,129},{129,193},{193,1... | collective-permute-start | bytes 589832 | tf_op jit(solution)/shard_map/ppermute | solution.py:500
  60.8 9.3 %collective-permute-start.14 = (bf16[8,2,48,128]{3,2,1,0:T(8,128)(2,1)S(1)}, bf16[8,2,48,128]{3,2,1,0:T(8,128)(2,1)S(1)}, u32[]{:S(2)}, u32[]{:S(2)}) collective-permute-start(bf16[8,2,48,128]{3,2,1,0:T(8,128)(2,1)S(1)} %bitcast.14), channel_id=1, source_target_pairs={{0,128},{64,192},{128,0},{192,64},{1,129},{65,193},{129,1},{193,65... | collective-permute-start | bytes 589832 | tf_op jit(solution)/shard_map/ppermute | solution.py:500
  63.2 9.7 %collective-permute-start.13 = (bf16[8,2,48,128]{3,2,1,0:T(8,128)(2,1)S(1)}, bf16[8,2,48,128]{3,2,1,0:T(8,128)(2,1)S(1)}, u32[]{:S(2)}, u32[]{:S(2)}) collective-permute-start(bf16[8,2,48,128]{3,2,1,0:T(8,128)(2,1)S(1)} %bitcast.15), channel_id=1, source_target_pairs={{0,192},{64,0},{128,64},{192,128},{1,193},{65,1},{129,65},{193,129... | collective-permute-start | bytes 589832 | tf_op jit(solution)/shard_map/ppermute | solution.py:500
  70.0 4.9 %collective-permute-start.19 = (bf16[48,4096]{1,0:T(8,128)(2,1)S(1)}, bf16[48,4096]{1,0:T(8,128)(2,1)S(1)}, u32[]{:S(2)}, u32[]{:S(2)}) collective-permute-start(bf16[48,4096]{1,0:T(8,128)(2,1)S(1)} %copy-done.2), channel_id=1, source_target_pairs={{0,1},{1,0},{2,3},{3,2},{4,5},{5,4},{6,7},{7,6},{8,9},{9,8},{10,11... | collective-permute-start | bytes 1179656 | tf_op jit(solution)/shard_map/ppermute | solution.py:504
  82.2 31.6 %all-to-all-start.1 = ((bf16[8,2,48,512]{3,2,1,0:T(8,128)(2,1)}), bf16[8,2,48,512]{3,2,1,0:T(8,128)(2,1)S(1)}, u32[]{:S(2)}, u32[]{:S(2)}) async-start(bf16[8,2,48,512]{3,2,1,0:T(8,128)(2,1)} %get-tuple-element.83), calls=%async_computation.1 | async-start | bytes 1572864 | tf_op jit(solution)/shard_map/all_to_all | solution.py:512
  95.1 35.7 %collective-permute-start.18 = (bf16[1,2,1,128,2048]{4,3,2,1,0:T(8,128)(2,1)}, bf16[1,2,1,128,2048]{4,3,2,1,0:T(8,128)(2,1)}, u32[]{:S(2)}, u32[]{:S(2)}) collective-permute-start(bf16[1,2,1,128,2048]{4,3,2,1,0:T(8,128)(2,1)} %get-tuple-element.79), channel_id=1, source_target_pairs={{32,0},{64,32},{96,64},{128,96},{160,128},{192,160},{224,192},{33,... | collective-permute-start | bytes 3145736 | tf_op jit(solution)/shard_map/ppermute | solution.py:552
  98.5 11.9 %collective-permute-start.23 = (f32[8,512]{1,0:T(8,128)S(1)}, f32[8,512]{1,0:T(8,128)S(1)}, u32[]{:S(2)}, u32[]{:S(2)}) collective-permute-start(f32[8,512]{1,0:T(8,128)S(1)} %get-tuple-element.92.gain0_ref), channel_id=1, source_target_pairs={{0,6},{2,0},{4,2},{6,4},{1,7},{3,1},{5,3},{7,5},{8,14},{10,8},{12,... | collective-permute-start | bytes 49160 | tf_op jit(solution)/shard_map/ppermute | solution.py:500
  99.9 10.5 %collective-permute-start.22 = (f32[8,512]{1,0:T(8,128)S(1)}, f32[8,512]{1,0:T(8,128)S(1)}, u32[]{:S(2)}, u32[]{:S(2)}) collective-permute-start(f32[8,512]{1,0:T(8,128)S(1)} %get-tuple-element.92.gain0_ref), channel_id=1, source_target_pairs={{0,4},{2,6},{4,0},{6,2},{1,5},{3,7},{5,1},{7,3},{8,12},{10,14},{12... | collective-permute-start | bytes 49160 | tf_op jit(solution)/shard_map/ppermute | solution.py:500
  102.4 8.0 %collective-permute-start.21 = (f32[8,512]{1,0:T(8,128)S(1)}, f32[8,512]{1,0:T(8,128)S(1)}, u32[]{:S(2)}, u32[]{:S(2)}) collective-permute-start(f32[8,512]{1,0:T(8,128)S(1)} %get-tuple-element.92.gain0_ref), channel_id=1, source_target_pairs={{0,2},{2,4},{4,6},{6,0},{1,3},{3,5},{5,7},{7,1},{8,10},{10,12},{12... | collective-permute-start | bytes 49160 | tf_op jit(solution)/shard_map/ppermute | solution.py:500
  110.4 14.1 %collective-permute-start.24 = (bf16[2,64,2048]{2,1,0:T(8,128)(2,1)}, bf16[2,64,2048]{2,1,0:T(8,128)(2,1)S(1)}, u32[]{:S(2)}, u32[]{:S(2)}) collective-permute-start(bf16[2,64,2048]{2,1,0:T(8,128)(2,1)} %get-tuple-element.93), channel_id=1, source_target_pairs={{0,2},{2,4},{4,6},{6,0},{1,3},{3,5},{5,7},{7,1},{8,10},{10,12},{12... | collective-permute-start | bytes 1572872 | tf_op jit(solution)/shard_map/ppermute | solution.py:500
  111.5 13.0 %collective-permute-start.25 = (bf16[2,64,2048]{2,1,0:T(8,128)(2,1)}, bf16[2,64,2048]{2,1,0:T(8,128)(2,1)S(1)}, u32[]{:S(2)}, u32[]{:S(2)}) collective-permute-start(bf16[2,64,2048]{2,1,0:T(8,128)(2,1)} %get-tuple-element.94), channel_id=1, source_target_pairs={{0,6},{2,0},{4,2},{6,4},{1,7},{3,1},{5,3},{7,5},{8,14},{10,8},{12,... | collective-permute-start | bytes 1572872 | tf_op jit(solution)/shard_map/ppermute | solution.py:500
  114.8 17.7 %all-to-all-start.2 = ((bf16[8,16,512]{2,1,0:T(8,128)(2,1)}), bf16[8,16,512]{2,1,0:T(8,128)(2,1)S(1)}, u32[]{:S(2)}, u32[]{:S(2)}) async-start(bf16[8,16,512]{2,1,0:T(8,128)(2,1)} %layers.1), calls=%async_computation.2 | async-start | bytes 262144 | tf_op jit(solution)/shard_map/all_to_all | solution.py:512
  127.6 23.5 %collective-permute-start.27 = (bf16[2,128,2048]{2,1,0:T(8,128)(2,1)}, bf16[2,128,2048]{2,1,0:T(8,128)(2,1)S(1)}, u32[]{:S(2)}, u32[]{:S(2)}) collective-permute-start(bf16[2,128,2048]{2,1,0:T(8,128)(2,1)} %get-tuple-element.96), channel_id=1, source_target_pairs={{0,6},{2,0},{4,2},{6,4},{1,7},{3,1},{5,3},{7,5},{8,14},{10,8},{12,... | collective-permute-start | bytes 3145736 | tf_op jit(solution)/shard_map/ppermute | solution.py:500
  130.7 23.7 %collective-permute-start.26 = (bf16[2,128,2048]{2,1,0:T(8,128)(2,1)}, bf16[2,128,2048]{2,1,0:T(8,128)(2,1)S(1)}, u32[]{:S(2)}, u32[]{:S(2)}) collective-permute-start(bf16[2,128,2048]{2,1,0:T(8,128)(2,1)} %get-tuple-element.95), channel_id=1, source_target_pairs={{0,2},{2,4},{4,6},{6,0},{1,3},{3,5},{5,7},{7,1},{8,10},{10,12},{12... | collective-permute-start | bytes 3145736 | tf_op jit(solution)/shard_map/ppermute | solution.py:500
  132.8 5.1 %collective-permute-start.28 = (bf16[16,4096]{1,0:T(8,128)(2,1)S(1)}, bf16[16,4096]{1,0:T(8,128)(2,1)S(1)}, u32[]{:S(2)}, u32[]{:S(2)}) collective-permute-start(bf16[16,4096]{1,0:T(8,128)(2,1)S(1)} %encoder.1), channel_id=1, source_target_pairs={{0,32},{32,0},{1,33},{33,1},{2,34},{34,2},{3,35},{35,3},{4,36},{36... | collective-permute-start | bytes 393224 | tf_op jit(solution)/shard_map/ppermute | solution.py:564
  138.0 18.9 %collective-permute-start.31 = (bf16[2,16,4096]{2,1,0:T(8,128)(2,1)S(1)}, bf16[2,16,4096]{2,1,0:T(8,128)(2,1)S(1)}, u32[]{:S(2)}, u32[]{:S(2)}) collective-permute-start(bf16[2,16,4096]{2,1,0:T(8,128)(2,1)S(1)} %pad_maximum_fusion.a_ref), channel_id=1, source_target_pairs={{0,64},{64,128},{128,192},{192,0},{1,65},{65,129},{129,193},{193,1... | collective-permute-start | bytes 786440 | tf_op jit(solution)/shard_map/ppermute | solution.py:500
  140.1 16.9 %collective-permute-start.30 = (bf16[2,16,4096]{2,1,0:T(8,128)(2,1)S(1)}, bf16[2,16,4096]{2,1,0:T(8,128)(2,1)S(1)}, u32[]{:S(2)}, u32[]{:S(2)}) collective-permute-start(bf16[2,16,4096]{2,1,0:T(8,128)(2,1)S(1)} %pad_maximum_fusion.a_ref), channel_id=1, source_target_pairs={{0,128},{64,192},{128,0},{192,64},{1,129},{65,193},{129,1},{193,65... | collective-permute-start | bytes 786440 | tf_op jit(solution)/shard_map/ppermute | solution.py:500
  140.4 16.5 %collective-permute-start.29 = (bf16[2,16,4096]{2,1,0:T(8,128)(2,1)S(1)}, bf16[2,16,4096]{2,1,0:T(8,128)(2,1)S(1)}, u32[]{:S(2)}, u32[]{:S(2)}) collective-permute-start(bf16[2,16,4096]{2,1,0:T(8,128)(2,1)S(1)} %pad_maximum_fusion.a_ref), channel_id=1, source_target_pairs={{0,192},{64,0},{128,64},{192,128},{1,193},{65,1},{129,65},{193,129... | collective-permute-start | bytes 786440 | tf_op jit(solution)/shard_map/ppermute | solution.py:500
  (8 other events, 118.1 us)

commit v3 on v2

--- a/solution.py
+++ b/solution.py
@@ -271,7 +271,7 @@
 
 
 def weight_kernel(flip_ref, first_ref, second_ref, *refs):
-    outs, far_p, far_m, grad_s, flip_s, outs_s, sems = refs[:3], *refs[3:]
+    own, sum_p, sum_m, raw_p, raw_m, far_p, far_m, grad_s, flip_s, own_s, sum_s, sems = refs
     kept = []
     pairs = [(flip_ref, flip_s)]
     for half in (1, 0):
@@ -284,12 +284,15 @@
             at = pl.ds(n * 512, 512)
             grad = grad_s[half, :, :, :, at].reshape(16 * SRC, 512)
             partial = jnp.dot(flip_s[...], grad, preferred_element_type=F32).astype(BF)
-            outs_s[0, half, :, at] = partial[:128]
-            outs_s[1, half, :, at] = partial[128:256]
+            own_s[half, :, at] = partial[:128]
+            sum_s[0, half, :, at] = partial[128:192]
+            raw_p[half, :, at] = partial[192:256]
             far_p[half, :, at] = partial[256:320]
             far_m[half, :, at] = partial[320:384]
-            outs_s[2, half, :, at] = partial[384:]
-        pairs = [(outs_s.at[i, half], out.at[half]) for i, out in enumerate(outs)]
+            raw_m[half, :, at] = partial[384:448]
+            sum_s[1, half, :, at] = partial[448:]
+        pairs = [(own_s.at[half], own.at[half])]
+        pairs += [(sum_s.at[i, half], out.at[half]) for i, out in enumerate((sum_p, sum_m))]
         kept += start_all(pairs, sems, 5 + 3 * half)
     wait_all(kept)
 
@@ -298,12 +301,13 @@
     return pl.pallas_call(
         weight_kernel,
         in_specs=[PIN] * 3,
-        out_specs=[PIN] * 3 + [VMEM] * 2,
-        out_shape=[pinned((2, 128, HD))] * 3 + [shape((2, 64, HD))] * 2,
+        out_specs=[PIN] * 3 + [VMEM] * 4,
+        out_shape=[pinned((2, n, HD)) for n in (128, 64, 64)] + [shape((2, 64, HD))] * 4,
         scratch_shapes=[
             pltpu.VMEM((2, 2, 8, SRC, HD), BF),
             pltpu.VMEM((COLS, 16 * SRC), BF),
-            pltpu.VMEM((3, 2, 128, HD), BF),
+            pltpu.VMEM((2, 128, HD), BF),
+            pltpu.VMEM((2, 2, 64, HD), BF),
             pltpu.SemaphoreType.DMA((11,)),
         ],
         compiler_params=params(),
@@ -312,35 +316,24 @@
     )(*hold(flipped, first, second))
 
 
-def relay_kernel(near_p, near_m, far_p, far_m, out_p, out_m, near_s, far_s, sems):
-    pairs = [(near_p, near_s.at[0]), (near_m, near_s.at[1])]
-    pairs += [(far_p, far_s.at[0]), (far_m, far_s.at[1])]
-    wait_all(start_all(pairs, sems))
-    first, second = pl.ds(0, 64), pl.ds(64, 64)
-    for half in range(2):
-        added = near_s[0, half, first].astype(F32) + far_s[0, half].astype(F32)
-        out_p[half, first] = added.astype(BF)
-        out_p[half, second] = near_s[0, half, second]
-        out_m[half, first] = near_s[1, half, first]
-        added = near_s[1, half, second].astype(F32) + far_s[1, half].astype(F32)
-        out_m[half, second] = added.astype(BF)
-
-
-def relay_blocks(near_p, near_m, far_p, far_m):
+def relay_kernel(sum_p, sum_m, far_p, far_m, out_p, out_m, terms_s, sems):
+    refs = (sum_p, sum_m, far_p, far_m)
+    wait_all(start_all([(ref, terms_s.at[i]) for i, ref in enumerate(refs)], sems))
+    out_p[...] = (terms_s[0].astype(F32) + terms_s[2].astype(F32)).astype(BF)
+    out_m[...] = (terms_s[1].astype(F32) + terms_s[3].astype(F32)).astype(BF)
+
+
+def relay_blocks(sum_p, sum_m, far_p, far_m):
     return pl.pallas_call(
         relay_kernel,
         in_specs=[PIN, PIN, HBM, HBM],
         out_specs=[VMEM] * 2,
-        out_shape=[shape((2, 128, HD))] * 2,
-        scratch_shapes=[
-            pltpu.VMEM((2, 2, 128, HD), BF),
-            pltpu.VMEM((2, 2, 64, HD), BF),
-            pltpu.SemaphoreType.DMA((4,)),
-        ],
+        out_shape=[shape(sum_p.shape)] * 2,
+        scratch_shapes=[pltpu.VMEM((4, 2, 64, HD), BF), pltpu.SemaphoreType.DMA((4,))],
         compiler_params=params(),
         cost_estimate=cost(),
         name="relay",
-    )(*hold(near_p, near_m), far_p, far_m)
+    )(*hold(sum_p, sum_m), far_p, far_m)
 
 
 def pick_rows(rows, cols, wanted, keep):
@@ -420,14 +413,12 @@
     )(own, pre, gain)
 
 
-def finish_kernel(a_ref, b_ref, c_ref, d_ref, gain_ref, out_ref, gain_out_ref, packed_s, sems):
+def finish_kernel(a_ref, b_ref, c_ref, d_ref, gain_ref, out_ref, gain_out_ref, packed_s):
     y, zlo = lax.axis_index("y"), lax.axis_index("zlo")
-    pairs = []
     for r, ref in enumerate((a_ref, b_ref, c_ref, d_ref)):
         for j in range(2):
             rank = lax.rem(y + r, 4) * 2 + (zlo if j == 0 else 1 - zlo)
-            pairs.append((ref.at[j], packed_s.at[rank]))
-    wait_all(start_all(pairs, sems))
+            packed_s[rank] = ref[j]
     packed = packed_s[...].reshape(128, D)
     move = pick_rows(
         2 * SRC,
@@ -445,37 +436,42 @@
 def finish(packed, gain):
     return pl.pallas_call(
         finish_kernel,
-        in_specs=[HBM] * 4 + [VMEM],
+        in_specs=[VMEM] * 5,
         out_specs=[VMEM, VMEM],
         out_shape=[shape((2 * SRC, D)), shape((1, D), F32)],
-        scratch_shapes=[pltpu.VMEM((8, 16, D), BF), pltpu.SemaphoreType.DMA((8,))],
+        scratch_shapes=[pltpu.VMEM((8, 16, D), BF)],
         compiler_params=params(),
         cost_estimate=cost(),
         name="finish",
     )(*packed, gain)
 
 
-def add_kernel(*refs):
-    terms, (key_out, value_out), (terms_s, sems) = refs[:3], refs[3:5], refs[5:]
-    pairs = [(ref.at[:, pl.ds(0, 128)], terms_s.at[i]) for i, ref in enumerate(terms)]
-    wait_all(start_all(pairs, sems))
+def add_kernel(own_ref, *refs):
+    terms, (key_out, value_out), (own_s, terms_s, sems) = refs[:4], refs[4:6], refs[6:]
+    copies = start_all([(own_ref, own_s)], sems)
+    wait_all(copies + start_all([(ref, terms_s.at[i]) for i, ref in enumerate(terms)], sems, 1))
     for half, out in enumerate((key_out, value_out)):
-        total = terms_s[0, half].astype(F32) + terms_s[1, half].astype(F32)
-        out[...] = (total + terms_s[2, half].astype(F32)).astype(BF)
-
-
-def add_blocks(*terms):
-    dims = terms[0].shape
+        for rows, first, second in ((0, 0, 3), (64, 2, 1)):
+            total = own_s[half, rows : rows + 64].astype(F32) + terms_s[first, half].astype(F32)
+            out[rows : rows + 64] = (total + terms_s[second, half].astype(F32)).astype(BF)
+
+
+def add_blocks(own, *terms):
+    dims = own.shape
     return pl.pallas_call(
         add_kernel,
-        in_specs=[PIN, HBM, HBM],
+        in_specs=[PIN] + [HBM] * 4,
         out_specs=[VMEM] * 2,
         out_shape=[shape(dims[1:])] * 2,
-        scratch_shapes=[pltpu.VMEM((3,) + dims, BF), pltpu.SemaphoreType.DMA((3,))],
-        compiler_params=params(),
-        cost_estimate=cost(400),
+        scratch_shapes=[
+            pltpu.VMEM(dims, BF),
+            pltpu.VMEM((4,) + terms[0].shape, BF),
+            pltpu.SemaphoreType.DMA((5,)),
+        ],
+        compiler_params=params(),
+        cost_estimate=cost(),
         name="add",
-    )(*hold(terms[0]), *terms[1:])
+    )(*hold(own), *terms)
 
 
 def hand_kernel(in_ref, out_ref, held_s, sems):
@@ -556,15 +552,18 @@
     part = weight_blocks(after(flipped, returned), all0, all1)
     sums = sum_layers(after(layers, part[0]), gains)
     own = exchange(sums, ZC)
-    far_p, far_m = lax.optimization_barrier((part[3], part[4], *gains))[:2]
+    own_part, sum_p, sum_m, raw_p, raw_m, far_p, far_m = part
+    far_p, far_m, raw_p, raw_m = lax.optimization_barrier((far_p, far_m, raw_p, raw_m, *gains))[:4]
     far_p, far_m = shift(far_p, "x", 1), shift(far_m, "x", -1)
-    near_p, near_m = relay_blocks(part[1], part[2], far_p, far_m)
-    packed = encoder_rows(after(own, near_p, query_in), hidden, gain)
-    near_p, near_m = shift(near_p, "x", 1), shift(near_m, "x", -1)
+    raw_p, raw_m = shift(raw_p, "x", 1), shift(raw_m, "x", -1)
+    far_p, far_m = lax.optimization_barrier((far_p, far_m, raw_p, raw_m))[:2]
+    sum_p, sum_m = relay_blocks(sum_p, sum_m, far_p, far_m)
+    packed = encoder_rows(after(own, query_in), hidden, gain)
+    sum_p, sum_m = shift(sum_p, "x", 1), shift(sum_m, "x", -1)
     other = lax.ppermute(packed, "zlo", [(0, 1), (1, 0)])
     packed = jnp.stack([packed, other])
     packed = [packed] + [shift(packed, "y", -r) for r in (1, 2, 3)]
-    grad_key, grad_value = add_blocks(part[0], near_p, near_m)
+    grad_key, grad_value = add_blocks(own_part, sum_p, sum_m, raw_p, raw_m)
     query_grad = hand_on(query_in)
     encoder_grad, gain_grad = finish(packed, gain)
     return (

time: 161 us -> 156 us (0.969)
  waiting for transfers between devices: 44.4 us -> 40.4 us
  starting transfers between devices: 70.1 us -> 73.7 us
  Pallas kernels: 43.3 us -> 39.8 us
    ppermute x22 -> x24, waiting for transfers between devices: 27.4 us -> 19 us  [shift(): return lax.ppermute(value, axis, [(i, (i + step) % 4) for i in range(4)])]
    ppermute x1, waiting for transfers between devices: 0.01 us -> 7.17 us  [body(): lax.ppermute(after(local, minus1_s, far1_s), SEC, [(s, s - 1) for s in ra...]
    ppermute x22 -> x24, starting transfers between devices: 40.6 us -> 44.3 us  [shift(): return lax.ppermute(value, axis, [(i, (i + step) % 4) for i in range(4)])]
    ppermute x1, waiting for transfers between devices: 3.57 us -> 0.01 us  [body(): other = lax.ppermute(packed, 'zlo', [(0, 1), (1, 0)])]
  transfers between devices with their start and end apart: 35 -> 37, of which waited for: 13 -> 14; matrix products, arithmetic and copies ran while one was open for 0% -> 0% of each run, Pallas kernels for 19% -> 18%
where the time goes in v3:
time: 156 us
  starting transfers between devices  73.7 us (47%)
  waiting for transfers between devices  40.4 us (26%)
  Pallas kernels  39.8 us (26%)
    ppermute x24, starting transfers between devices, shift(): return lax.ppermute(value, axis, [(i, (i + step) % 4) for i in range(4)])  44.3 us
    all_to_all x3, starting transfers between devices, exchange(): return lax.all_to_all(value, axes, split_axis=0, concat_axis=0, tiled=True)  22.8 us
    ppermute x24, waiting for transfers between devices, shift(): return lax.ppermute(value, axis, [(i, (i + step) % 4) for i in range(4)])  19 us
    all_to_all x3, waiting for transfers between devices, exchange(): return lax.all_to_all(value, axes, split_axis=0, concat_axis=0, tiled=True)  12.5 us
    pallas_call x2, Pallas kernels, return_blocks(): pl.pallas_call(functools.partial(return_kernel, m), in_specs=[HBM] * 12 +...  10.4 us
    pallas_call x2, Pallas kernels, heads(): pl.pallas_call(functools.partial(heads_kernel, m == 0), grid=(1,), in_spe...  9.77 us
    pallas_call x1, Pallas kernels, weight_blocks(): pl.pallas_call(weight_kernel, in_specs=[PIN] * 3, out_specs=[PIN] * 3 + [...  8.06 us
    ppermute x1, waiting for transfers between devices, body(): lax.ppermute(after(local, minus1_s, far1_s), SEC, [(s, s - 1) for s in ra...  7.17 us
  transfers between devices with their start and end apart: 37, of which 14 were waited for; matrix products, arithmetic and copies ran while one was open for 0% of the time, Pallas kernels for 18%

profile of v3, /device:TPU:8, one launch (start us, length us, event | category | flops | bytes accessed | tf_op | source)
XLA Modules:
  0.0 155.8 jit_solution(4419056257123041929)
XLA Ops:
  0.6 5.2 %heads.2 = (bf16[1,2,1,128,2048]{4,3,2,1,0:T(8,128)(2,1)}, bf16[48,4096]{1,0:T(8,128)(2,1)}, bf16[2,128,2048]{2,1,0:T(8,128)(2,1)}) custom-call(bf16[1,2,1,128,2048]{4,3,2,1,0:T(8,128)(2,1)} %q_ref.2, bf16[1,2,1,48,2048]{4,3,2,1,0:T(8,128)(2,1)} %k_ref.3, bf16[1,2,1,48,2048]{4,3,2,1,0:T(8,128)(2,1)} %v_ref.3, bf16[1,2,1,128,2048]{4,3,2,1,0:T(8,128)(2,1)} %g_ref.3, ...), custom_call_target="tpu_custom_call" | custom-call | bytes 41943040 | tf_op jit(solution)/shard_map/heads/pallas_call | solution.py:106
  5.9 2.8 %collective-permute-start.3 = (bf16[2,128,2048]{2,1,0:T(8,128)(2,1)}, bf16[2,128,2048]{2,1,0:T(8,128)(2,1)S(1)}, u32[]{:S(2)}, u32[]{:S(2)}) collective-permute-start(bf16[2,128,2048]{2,1,0:T(8,128)(2,1)} %get-tuple-element.76.refs_0_), channel_id=1, source_target_pairs={{0,6},{2,0},{4,2},{6,4},{1,7},{3,1},{5,3},{7,5},{8,14},{10,8},{12,... | collective-permute-start | bytes 3145736 | tf_op jit(solution)/shard_map/ppermute | solution.py:496
  8.6 6.3 %collective-permute-start.1 = (bf16[48,4096]{1,0:T(8,128)(2,1)}, bf16[48,4096]{1,0:T(8,128)(2,1)}, u32[]{:S(2)}, u32[]{:S(2)}) collective-permute-start(bf16[48,4096]{1,0:T(8,128)(2,1)} %get-tuple-element.60.refs_4_), channel_id=1, source_target_pairs={{0,24},{8,0},{16,8},{24,16},{1,25},{9,1},{17,9},{25,17},{2,26},{10... | collective-permute-start | bytes 1179656 | tf_op jit(solution)/shard_map/ppermute | solution.py:496
  14.9 2.1 %memory.1 = bf16[8,96,128]{2,1,0:T(8,128)(2,1)} custom-call(bf16[96,4096]{1,0:T(8,128)(2,1)} %bitcast.11, f32[1,4096]{1,0:T(1,128)} %bitcast.18), custom_call_target="tpu_custom_call" | custom-call | tf_op jit(solution)/shard_map/memory/pallas_call | solution.py:135
  17.0 5.4 %all-to-all-start = ((bf16[8,96,128]{2,1,0:T(8,128)(2,1)}), bf16[8,96,128]{2,1,0:T(8,128)(2,1)S(1)}, u32[]{:S(2)}, u32[]{:S(2)}) async-start(bf16[8,96,128]{2,1,0:T(8,128)(2,1)} %memory.1), calls=%async_computation | async-start | bytes 393216 | tf_op jit(solution)/shard_map/all_to_all | solution.py:508
  22.4 4.6 %heads.3 = (bf16[1,2,1,128,2048]{4,3,2,1,0:T(8,128)(2,1)}, bf16[48,4096]{1,0:T(8,128)(2,1)}) custom-call(bf16[1,2,1,128,2048]{4,3,2,1,0:T(8,128)(2,1)} %q_ref.2, bf16[1,2,1,48,2048]{4,3,2,1,0:T(8,128)(2,1)} %k_ref.3, bf16[1,2,1,48,2048]{4,3,2,1,0:T(8,128)(2,1)} %v_ref.3, bf16[1,2,1,128,2048]{4,3,2,1,0:T(8,128)(2,1)} %g_ref.3, ...), custom_call_target="tpu_custom_call", output_to_operand_aliasing={{0}: (4, {})} | custom-call | bytes 41943040 | tf_op jit(solution)/shard_map/heads/pallas_call | solution.py:106
  26.9 9.9 %all-to-all-done = bf16[8,96,128]{2,1,0:T(8,128)(2,1)S(1)} async-done(((bf16[8,96,128]{2,1,0:T(8,128)(2,1)}), bf16[8,96,128]{2,1,0:T(8,128)(2,1)S(1)}, u32[]{:S(2)}, u32[]{:S(2)}) %all-to-all-start) | async-done | bytes 196640 | tf_op jit(solution)/shard_map/all_to_all | solution.py:508
  37.0 2.4 %collective-permute-start.9 = (bf16[2,128,2048]{2,1,0:T(8,128)(2,1)S(1)}, bf16[2,128,2048]{2,1,0:T(8,128)(2,1)S(1)}, u32[]{:S(2)}, u32[]{:S(2)}) collective-permute-start(bf16[2,128,2048]{2,1,0:T(8,128)(2,1)S(1)} %copy-done), channel_id=1, source_target_pairs={{0,4},{2,6},{4,0},{6,2},{1,5},{3,7},{5,1},{7,3},{8,12},{10,14},{12... | collective-permute-start | bytes 3145736 | tf_op jit(solution)/shard_map/ppermute | solution.py:496
  39.3 6.2 %collective-permute-start.5 = (bf16[48,4096]{1,0:T(8,128)(2,1)}, bf16[48,4096]{1,0:T(8,128)(2,1)S(1)}, u32[]{:S(2)}, u32[]{:S(2)}) collective-permute-start(bf16[48,4096]{1,0:T(8,128)(2,1)} %collective-permute-done.refs_5_), channel_id=1, source_target_pairs={{0,8},{8,16},{16,24},{24,0},{1,9},{9,17},{17,25},{25,1},{2,10},{10... | collective-permute-start | bytes 1179656 | tf_op jit(solution)/shard_map/ppermute | solution.py:496
  46.0 7.8 %collective-permute-done.5.refs_7_ = bf16[48,4096]{1,0:T(8,128)(2,1)S(1)} collective-permute-done((bf16[48,4096]{1,0:T(8,128)(2,1)}, bf16[48,4096]{1,0:T(8,128)(2,1)S(1)}, u32[]{:S(2)}, u32[]{:S(2)}) %collective-permute-start.5) | collective-permute-done | bytes 393248 | tf_op jit(solution)/shard_map/ppermute | solution.py:496
  56.3 2.9 %collective-permute-start.8 = (bf16[48,4096]{1,0:T(8,128)(2,1)S(1)}, bf16[48,4096]{1,0:T(8,128)(2,1)S(1)}, u32[]{:S(2)}, u32[]{:S(2)}) collective-permute-start(bf16[48,4096]{1,0:T(8,128)(2,1)S(1)} %collective-permute-done.6.refs_6_), channel_id=1, source_target_pairs={{0,24},{8,0},{16,8},{24,16},{1,25},{9,1},{17,9},{25,17},{2,26},{10... | collective-permute-start | bytes 1179656 | tf_op jit(solution)/shard_map/ppermute | solution.py:496
  59.2 1.6 %collective-permute-start.15 = (bf16[8,2,48,128]{3,2,1,0:T(8,128)(2,1)S(1)}, bf16[8,2,48,128]{3,2,1,0:T(8,128)(2,1)S(1)}, u32[]{:S(2)}, u32[]{:S(2)}) collective-permute-start(bf16[8,2,48,128]{3,2,1,0:T(8,128)(2,1)S(1)} %bitcast.13), channel_id=1, source_target_pairs={{0,64},{64,128},{128,192},{192,0},{1,65},{65,129},{129,193},{193,1... | collective-permute-start | bytes 589832 | tf_op jit(solution)/shard_map/ppermute | solution.py:496
  65.2 4.8 %returned.2 = (bf16[8,2,48,512]{3,2,1,0:T(8,128)(2,1)}, bf16[384,512]{1,0:T(8,128)(2,1)}, bf16[2,8,48,2048]{3,2,1,0:T(8,128)(2,1)}) custom-call(bf16[2,128,2048]{2,1,0:T(8,128)(2,1)S(1)} %copy-done, bf16[2,128,2048]{2,1,0:T(8,128)(2,1)S(1)} %collective-permute-done.3.refs_1_, bf16[2,128,2048]{2,1,0:T(8,128)(2,1)S(1)} %collective-permute-done.9.refs_2_, ...), custom_call_target="tpu_custom_call" | custom-call | tf_op jit(solution)/shard_map/returned/pallas_call | solution.py:260
  70.6 2.3 %collective-permute-done.13.refs_1_ = bf16[8,2,48,128]{3,2,1,0:T(8,128)(2,1)S(1)} collective-permute-done((bf16[8,2,48,128]{3,2,1,0:T(8,128)(2,1)S(1)}, bf16[8,2,48,128]{3,2,1,0:T(8,128)(2,1)S(1)}, u32[]{:S(2)}, u32[]{:S(2)}) %collective-permute-start.13) | collective-permute-done | bytes 196640 | tf_op jit(solution)/shard_map/ppermute | solution.py:496
  76.8 5.6 %returned.3 = (bf16[8,2,48,512]{3,2,1,0:T(8,128)(2,1)}, f32[8,512]{1,0:T(8,128)S(1)}, bf16[2,8,48,2048]{3,2,1,0:T(8,128)(2,1)}) custom-call(bf16[2,128,2048]{2,1,0:T(8,128)(2,1)S(1)} %copy-done, bf16[2,128,2048]{2,1,0:T(8,128)(2,1)S(1)} %collective-permute-done.3.refs_1_, ...), custom_call_target="tpu_custom_call", output_to_operand_aliasing={{0}: (14, {})} | custom-call | tf_op jit(solution)/shard_map/returned/pallas_call | solution.py:260
  82.4 12.9 %all-to-all-start.1 = ((bf16[8,2,48,512]{3,2,1,0:T(8,128)(2,1)}), bf16[8,2,48,512]{3,2,1,0:T(8,128)(2,1)S(1)}, u32[]{:S(2)}, u32[]{:S(2)}) async-start(bf16[8,2,48,512]{3,2,1,0:T(8,128)(2,1)} %get-tuple-element.89), calls=%async_computation.1 | async-start | bytes 1572864 | tf_op jit(solution)/shard_map/all_to_all | solution.py:508
  95.2 3.4 %collective-permute-start.18 = (bf16[1,2,1,128,2048]{4,3,2,1,0:T(8,128)(2,1)}, bf16[1,2,1,128,2048]{4,3,2,1,0:T(8,128)(2,1)S(1)}, u32[]{:S(2)}, u32[]{:S(2)}) collective-permute-start(bf16[1,2,1,128,2048]{4,3,2,1,0:T(8,128)(2,1)} %get-tuple-element.85), channel_id=1, source_target_pairs={{32,0},{64,32},{96,64},{128,96},{160,128},{192,160},{224,192},{33,... | collective-permute-start | bytes 3145736 | tf_op jit(solution)/shard_map/ppermute | solution.py:548
  100.1 2.5 %collective-permute-start.22 = (f32[8,512]{1,0:T(8,128)S(1)}, f32[8,512]{1,0:T(8,128)S(1)}, u32[]{:S(2)}, u32[]{:S(2)}) collective-permute-start(f32[8,512]{1,0:T(8,128)S(1)} %get-tuple-element.100.gain0_ref), channel_id=1, source_target_pairs={{0,4},{2,6},{4,0},{6,2},{1,5},{3,7},{5,1},{7,3},{8,12},{10,14},{12... | collective-permute-start | bytes 49160 | tf_op jit(solution)/shard_map/ppermute | solution.py:496
  102.6 8.1 %weights.1 = (bf16[2,128,2048]{2,1,0:T(8,128)(2,1)}, bf16[2,64,2048]{2,1,0:T(8,128)(2,1)}, bf16[2,64,2048]{2,1,0:T(8,128)(2,1)}, bf16[2,64,2048]{2,1,0:T(8,128)(...) custom-call(bf16[512,768]{1,0:T(8,128)(2,1)} %get-tuple-element.90.flip_ref, ...), custom_call_target="tpu_custom_call" | custom-call | tf_op jit(solution)/shard_map/weights/pallas_call | solution.py:301
  111.7 2.3 %collective-permute-start.25 = (bf16[2,64,2048]{2,1,0:T(8,128)(2,1)}, bf16[2,64,2048]{2,1,0:T(8,128)(2,1)}, u32[]{:S(2)}, u32[]{:S(2)}) collective-permute-start(bf16[2,64,2048]{2,1,0:T(8,128)(2,1)} %get-tuple-element.102), channel_id=1, source_target_pairs={{0,6},{2,0},{4,2},{6,4},{1,7},{3,1},{5,3},{7,5},{8,14},{10,8},{12,... | collective-permute-start | bytes 1572872 | tf_op jit(solution)/shard_map/ppermute | solution.py:496
  114.1 3.2 %collective-permute-start.27 = (bf16[2,64,2048]{2,1,0:T(8,128)(2,1)}, bf16[2,64,2048]{2,1,0:T(8,128)(2,1)}, u32[]{:S(2)}, u32[]{:S(2)}) collective-permute-start(bf16[2,64,2048]{2,1,0:T(8,128)(2,1)} %get-tuple-element.104), channel_id=1, source_target_pairs={{0,6},{2,0},{4,2},{6,4},{1,7},{3,1},{5,3},{7,5},{8,14},{10,8},{12,... | collective-permute-start | bytes 1572872 | tf_op jit(solution)/shard_map/ppermute | solution.py:496
  118.2 4.6 %all-to-all-start.2 = ((bf16[8,16,512]{2,1,0:T(8,128)(2,1)}), bf16[8,16,512]{2,1,0:T(8,128)(2,1)S(1)}, u32[]{:S(2)}, u32[]{:S(2)}) async-start(bf16[8,16,512]{2,1,0:T(8,128)(2,1)} %layers.1), calls=%async_computation.2 | async-start | bytes 262144 | tf_op jit(solution)/shard_map/all_to_all | solution.py:508
  122.8 7.2 %collective-permute-done.18.in_ref = bf16[1,2,1,128,2048]{4,3,2,1,0:T(8,128)(2,1)S(1)} collective-permute-done((bf16[1,2,1,128,2048]{4,3,2,1,0:T(8,128)(2,1)}, bf16[1,2,1,128,2048]{4,3,2,1,0:T(8,128)(2,1)S(1)}, u32[]{:S(2)}, u32[]{:S(2)}) %collective-permute-start.18) | collective-permute-done | bytes 1048608 | tf_op jit(solution)/shard_map/ppermute | solution.py:548
  130.0 2.5 %all-to-all-done.2.own_ref = bf16[8,16,512]{2,1,0:T(8,128)(2,1)S(1)} async-done(((bf16[8,16,512]{2,1,0:T(8,128)(2,1)}), bf16[8,16,512]{2,1,0:T(8,128)(2,1)S(1)}, u32[]{:S(2)}, u32[]{:S(2)}) %all-to-all-start.2) | async-done | bytes 131104 | tf_op jit(solution)/shard_map/all_to_all | solution.py:508
  132.9 1.6 collective-permute-start.30
  134.4 1.5 collective-permute-done.26.refs_2_
  136.0 1.8 %relay.1 = (bf16[2,64,2048]{2,1,0:T(8,128)(2,1)S(1)}, bf16[2,64,2048]{2,1,0:T(8,128)(2,1)S(1)}) custom-call(bf16[2,64,2048]{2,1,0:T(8,128)(2,1)} %get-tuple-element.94.sum_p, bf16[2,64,2048]{2,1,0:T(8,128)(2,1)} %get-tuple-element.95.sum_m, bf16[2,64,2048]{2,1,0:T(8,128)(2,1)} %collective-permute-done.24.far_p, ...), custom_call_target="tpu_custom_call" | custom-call | tf_op jit(solution)/shard_map/relay/pallas_call | solution.py:327
  139.1 2.0 %collective-permute-start.29 = (bf16[2,64,2048]{2,1,0:T(8,128)(2,1)S(1)}, bf16[2,64,2048]{2,1,0:T(8,128)(2,1)S(1)}, u32[]{:S(2)}, u32[]{:S(2)}) collective-permute-start(bf16[2,64,2048]{2,1,0:T(8,128)(2,1)S(1)} %get-tuple-element.108), channel_id=1, source_target_pairs={{0,6},{2,0},{4,2},{6,4},{1,7},{3,1},{5,3},{7,5},{8,14},{10,8},{12,... | collective-permute-start | bytes 1572872 | tf_op jit(solution)/shard_map/ppermute | solution.py:496
  141.1 1.5 collective-permute-start.33
  143.6 2.5 %collective-permute-start.31 = (bf16[2,16,4096]{2,1,0:T(8,128)(2,1)S(1)}, bf16[2,16,4096]{2,1,0:T(8,128)(2,1)S(1)}, u32[]{:S(2)}, u32[]{:S(2)}) collective-permute-start(bf16[2,16,4096]{2,1,0:T(8,128)(2,1)S(1)} %pad_maximum_fusion.a_ref), channel_id=1, source_target_pairs={{0,192},{64,0},{128,64},{192,128},{1,193},{65,1},{129,65},{193,129... | collective-permute-start | bytes 786440 | tf_op jit(solution)/shard_map/ppermute | solution.py:496
  147.2 3.5 %collective-permute-done.28.refs_0_ = bf16[2,64,2048]{2,1,0:T(8,128)(2,1)S(1)} collective-permute-done((bf16[2,64,2048]{2,1,0:T(8,128)(2,1)S(1)}, bf16[2,64,2048]{2,1,0:T(8,128)(2,1)S(1)}, u32[]{:S(2)}, u32[]{:S(2)}) %collective-permute-start.28) | collective-permute-done | bytes 524320 | tf_op jit(solution)/shard_map/ppermute | solution.py:496
  151.0 2.6 %add.1 = (bf16[128,2048]{1,0:T(8,128)(2,1)}, bf16[128,2048]{1,0:T(8,128)(2,1)}) custom-call(bf16[2,128,2048]{2,1,0:T(8,128)(2,1)} %get-tuple-element.93.own_ref, bf16[2,64,2048]{2,1,0:T(8,128)(2,1)S(1)} %collective-permute-done.28.refs_0_, bf16[2,64,2048]{2,1,0:T(8,128)(2,1)S(1)} %collective-permute-done.29.refs_1_, ...), custom_call_target="tpu_custom_call" | custom-call | tf_op jit(solution)/shard_map/add/pallas_call | solution.py:461
  (66 shorter events, 21.5 us)
Async XLA Ops:
  5.9 31.1 %collective-permute-start.3 = (bf16[2,128,2048]{2,1,0:T(8,128)(2,1)}, bf16[2,128,2048]{2,1,0:T(8,128)(2,1)S(1)}, u32[]{:S(2)}, u32[]{:S(2)}) collective-permute-start(bf16[2,128,2048]{2,1,0:T(8,128)(2,1)} %get-tuple-element.76.refs_0_), channel_id=1, source_target_pairs={{0,6},{2,0},{4,2},{6,4},{1,7},{3,1},{5,3},{7,5},{8,14},{10,8},{12,... | collective-permute-start | bytes 3145736 | tf_op jit(solution)/shard_map/ppermute | solution.py:496
  8.6 28.3 %collective-permute-start.2 = (bf16[2,128,2048]{2,1,0:T(8,128)(2,1)}, bf16[2,128,2048]{2,1,0:T(8,128)(2,1)S(1)}, u32[]{:S(2)}, u32[]{:S(2)}) collective-permute-start(bf16[2,128,2048]{2,1,0:T(8,128)(2,1)} %get-tuple-element.76.refs_0_), channel_id=1, source_target_pairs={{0,2},{2,4},{4,6},{6,0},{1,3},{3,5},{5,7},{7,1},{8,10},{10,12},{12... | collective-permute-start | bytes 3145736 | tf_op jit(solution)/shard_map/ppermute | solution.py:496
  8.6 28.3 %collective-permute-start.4 = (bf16[48,4096]{1,0:T(8,128)(2,1)}, bf16[48,4096]{1,0:T(8,128)(2,1)}, u32[]{:S(2)}, u32[]{:S(2)}) collective-permute-start(bf16[48,4096]{1,0:T(8,128)(2,1)} %get-tuple-element.60.refs_4_), channel_id=1, source_target_pairs={{0,1},{1,0},{2,3},{3,2},{4,5},{5,4},{6,7},{7,6},{8,9},{9,8},{10,11... | collective-permute-start | bytes 1179656 | tf_op jit(solution)/shard_map/ppermute | solution.py:500
  8.6 28.3 %collective-permute-start.1 = (bf16[48,4096]{1,0:T(8,128)(2,1)}, bf16[48,4096]{1,0:T(8,128)(2,1)}, u32[]{:S(2)}, u32[]{:S(2)}) collective-permute-start(bf16[48,4096]{1,0:T(8,128)(2,1)} %get-tuple-element.60.refs_4_), channel_id=1, source_target_pairs={{0,24},{8,0},{16,8},{24,16},{1,25},{9,1},{17,9},{25,17},{2,26},{10... | collective-permute-start | bytes 1179656 | tf_op jit(solution)/shard_map/ppermute | solution.py:496
  14.9 22.0 %collective-permute-start = (bf16[48,4096]{1,0:T(8,128)(2,1)}, bf16[48,4096]{1,0:T(8,128)(2,1)}, u32[]{:S(2)}, u32[]{:S(2)}) collective-permute-start(bf16[48,4096]{1,0:T(8,128)(2,1)} %get-tuple-element.60.refs_4_), channel_id=1, source_target_pairs={{0,8},{8,16},{16,24},{24,0},{1,9},{9,17},{17,25},{25,1},{2,10},{10... | collective-permute-start | bytes 1179656 | tf_op jit(solution)/shard_map/ppermute | solution.py:496
  17.0 19.9 %all-to-all-start = ((bf16[8,96,128]{2,1,0:T(8,128)(2,1)}), bf16[8,96,128]{2,1,0:T(8,128)(2,1)S(1)}, u32[]{:S(2)}, u32[]{:S(2)}) async-start(bf16[8,96,128]{2,1,0:T(8,128)(2,1)} %memory.1), calls=%async_computation | async-start | bytes 393216 | tf_op jit(solution)/shard_map/all_to_all | solution.py:508
  37.0 26.2 %collective-permute-start.9 = (bf16[2,128,2048]{2,1,0:T(8,128)(2,1)S(1)}, bf16[2,128,2048]{2,1,0:T(8,128)(2,1)S(1)}, u32[]{:S(2)}, u32[]{:S(2)}) collective-permute-start(bf16[2,128,2048]{2,1,0:T(8,128)(2,1)S(1)} %copy-done), channel_id=1, source_target_pairs={{0,4},{2,6},{4,0},{6,2},{1,5},{3,7},{5,1},{7,3},{8,12},{10,14},{12... | collective-permute-start | bytes 3145736 | tf_op jit(solution)/shard_map/ppermute | solution.py:496
  39.3 14.5 %collective-permute-start.5 = (bf16[48,4096]{1,0:T(8,128)(2,1)}, bf16[48,4096]{1,0:T(8,128)(2,1)S(1)}, u32[]{:S(2)}, u32[]{:S(2)}) collective-permute-start(bf16[48,4096]{1,0:T(8,128)(2,1)} %collective-permute-done.refs_5_), channel_id=1, source_target_pairs={{0,8},{8,16},{16,24},{24,0},{1,9},{9,17},{17,25},{25,1},{2,10},{10... | collective-permute-start | bytes 1179656 | tf_op jit(solution)/shard_map/ppermute | solution.py:496
  45.5 9.6 %collective-permute-start.6 = (bf16[48,4096]{1,0:T(8,128)(2,1)}, bf16[48,4096]{1,0:T(8,128)(2,1)S(1)}, u32[]{:S(2)}, u32[]{:S(2)}) collective-permute-start(bf16[48,4096]{1,0:T(8,128)(2,1)} %get-tuple-element.71.refs_4_), channel_id=1, source_target_pairs={{0,24},{8,0},{16,8},{24,16},{1,25},{9,1},{17,9},{25,17},{2,26},{10... | collective-permute-start | bytes 1179656 | tf_op jit(solution)/shard_map/ppermute | solution.py:496
  45.5 10.8 %collective-permute-start.11 = (bf16[48,4096]{1,0:T(8,128)(2,1)}, bf16[48,4096]{1,0:T(8,128)(2,1)S(1)}, u32[]{:S(2)}, u32[]{:S(2)}) collective-permute-start(bf16[48,4096]{1,0:T(8,128)(2,1)} %collective-permute-done.1.refs_6_), channel_id=1, source_target_pairs={{0,1},{1,0},{2,3},{3,2},{4,5},{5,4},{6,7},{7,6},{8,9},{9,8},{10,11... | collective-permute-start | bytes 1179656 | tf_op jit(solution)/shard_map/ppermute | solution.py:500
  45.5 13.7 %collective-permute-start.10 = (bf16[48,4096]{1,0:T(8,128)(2,1)}, bf16[48,4096]{1,0:T(8,128)(2,1)S(1)}, u32[]{:S(2)}, u32[]{:S(2)}) collective-permute-start(bf16[48,4096]{1,0:T(8,128)(2,1)} %collective-permute-done.refs_5_), channel_id=1, source_target_pairs={{0,1},{1,0},{2,3},{3,2},{4,5},{5,4},{6,7},{7,6},{8,9},{9,8},{10,11... | collective-permute-start | bytes 1179656 | tf_op jit(solution)/shard_map/ppermute | solution.py:500
  55.1 19.3 %collective-permute-start.7 = (bf16[48,4096]{1,0:T(8,128)(2,1)}, bf16[48,4096]{1,0:T(8,128)(2,1)S(1)}, u32[]{:S(2)}, u32[]{:S(2)}) collective-permute-start(bf16[48,4096]{1,0:T(8,128)(2,1)} %get-tuple-element.71.refs_4_), channel_id=1, source_target_pairs={{0,8},{8,16},{16,24},{24,0},{1,9},{9,17},{17,25},{25,1},{2,10},{10... | collective-permute-start | bytes 1179656 | tf_op jit(solution)/shard_map/ppermute | solution.py:496
  56.3 18.1 %collective-permute-start.8 = (bf16[48,4096]{1,0:T(8,128)(2,1)S(1)}, bf16[48,4096]{1,0:T(8,128)(2,1)S(1)}, u32[]{:S(2)}, u32[]{:S(2)}) collective-permute-start(bf16[48,4096]{1,0:T(8,128)(2,1)S(1)} %collective-permute-done.6.refs_6_), channel_id=1, source_target_pairs={{0,24},{8,0},{16,8},{24,16},{1,25},{9,1},{17,9},{25,17},{2,26},{10... | collective-permute-start | bytes 1179656 | tf_op jit(solution)/shard_map/ppermute | solution.py:496
  59.2 10.7 %collective-permute-start.15 = (bf16[8,2,48,128]{3,2,1,0:T(8,128)(2,1)S(1)}, bf16[8,2,48,128]{3,2,1,0:T(8,128)(2,1)S(1)}, u32[]{:S(2)}, u32[]{:S(2)}) collective-permute-start(bf16[8,2,48,128]{3,2,1,0:T(8,128)(2,1)S(1)} %bitcast.13), channel_id=1, source_target_pairs={{0,64},{64,128},{128,192},{192,0},{1,65},{65,129},{129,193},{193,1... | collective-permute-start | bytes 589832 | tf_op jit(solution)/shard_map/ppermute | solution.py:496
  60.8 9.3 %collective-permute-start.14 = (bf16[8,2,48,128]{3,2,1,0:T(8,128)(2,1)S(1)}, bf16[8,2,48,128]{3,2,1,0:T(8,128)(2,1)S(1)}, u32[]{:S(2)}, u32[]{:S(2)}) collective-permute-start(bf16[8,2,48,128]{3,2,1,0:T(8,128)(2,1)S(1)} %bitcast.14), channel_id=1, source_target_pairs={{0,128},{64,192},{128,0},{192,64},{1,129},{65,193},{129,1},{193,65... | collective-permute-start | bytes 589832 | tf_op jit(solution)/shard_map/ppermute | solution.py:496
  63.2 9.7 %collective-permute-start.13 = (bf16[8,2,48,128]{3,2,1,0:T(8,128)(2,1)S(1)}, bf16[8,2,48,128]{3,2,1,0:T(8,128)(2,1)S(1)}, u32[]{:S(2)}, u32[]{:S(2)}) collective-permute-start(bf16[8,2,48,128]{3,2,1,0:T(8,128)(2,1)S(1)} %bitcast.15), channel_id=1, source_target_pairs={{0,192},{64,0},{128,64},{192,128},{1,193},{65,1},{129,65},{193,129... | collective-permute-start | bytes 589832 | tf_op jit(solution)/shard_map/ppermute | solution.py:496
  82.4 34.9 %all-to-all-start.1 = ((bf16[8,2,48,512]{3,2,1,0:T(8,128)(2,1)}), bf16[8,2,48,512]{3,2,1,0:T(8,128)(2,1)S(1)}, u32[]{:S(2)}, u32[]{:S(2)}) async-start(bf16[8,2,48,512]{3,2,1,0:T(8,128)(2,1)} %get-tuple-element.89), calls=%async_computation.1 | async-start | bytes 1572864 | tf_op jit(solution)/shard_map/all_to_all | solution.py:508
  95.2 34.7 %collective-permute-start.18 = (bf16[1,2,1,128,2048]{4,3,2,1,0:T(8,128)(2,1)}, bf16[1,2,1,128,2048]{4,3,2,1,0:T(8,128)(2,1)S(1)}, u32[]{:S(2)}, u32[]{:S(2)}) collective-permute-start(bf16[1,2,1,128,2048]{4,3,2,1,0:T(8,128)(2,1)} %get-tuple-element.85), channel_id=1, source_target_pairs={{32,0},{64,32},{96,64},{128,96},{160,128},{192,160},{224,192},{33,... | collective-permute-start | bytes 3145736 | tf_op jit(solution)/shard_map/ppermute | solution.py:548
  98.6 12.0 %collective-permute-start.23 = (f32[8,512]{1,0:T(8,128)S(1)}, f32[8,512]{1,0:T(8,128)S(1)}, u32[]{:S(2)}, u32[]{:S(2)}) collective-permute-start(f32[8,512]{1,0:T(8,128)S(1)} %get-tuple-element.100.gain0_ref), channel_id=1, source_target_pairs={{0,6},{2,0},{4,2},{6,4},{1,7},{3,1},{5,3},{7,5},{8,14},{10,8},{12,... | collective-permute-start | bytes 49160 | tf_op jit(solution)/shard_map/ppermute | solution.py:496
  100.1 10.6 %collective-permute-start.22 = (f32[8,512]{1,0:T(8,128)S(1)}, f32[8,512]{1,0:T(8,128)S(1)}, u32[]{:S(2)}, u32[]{:S(2)}) collective-permute-start(f32[8,512]{1,0:T(8,128)S(1)} %get-tuple-element.100.gain0_ref), channel_id=1, source_target_pairs={{0,4},{2,6},{4,0},{6,2},{1,5},{3,7},{5,1},{7,3},{8,12},{10,14},{12... | collective-permute-start | bytes 49160 | tf_op jit(solution)/shard_map/ppermute | solution.py:496
  102.5 8.1 %collective-permute-start.21 = (f32[8,512]{1,0:T(8,128)S(1)}, f32[8,512]{1,0:T(8,128)S(1)}, u32[]{:S(2)}, u32[]{:S(2)}) collective-permute-start(f32[8,512]{1,0:T(8,128)S(1)} %get-tuple-element.100.gain0_ref), channel_id=1, source_target_pairs={{0,2},{2,4},{4,6},{6,0},{1,3},{3,5},{5,7},{7,1},{8,10},{10,12},{12... | collective-permute-start | bytes 49160 | tf_op jit(solution)/shard_map/ppermute | solution.py:496
  110.7 23.8 %collective-permute-start.24 = (bf16[2,64,2048]{2,1,0:T(8,128)(2,1)}, bf16[2,64,2048]{2,1,0:T(8,128)(2,1)}, u32[]{:S(2)}, u32[]{:S(2)}) collective-permute-start(bf16[2,64,2048]{2,1,0:T(8,128)(2,1)} %get-tuple-element.101), channel_id=1, source_target_pairs={{0,2},{2,4},{4,6},{6,0},{1,3},{3,5},{5,7},{7,1},{8,10},{10,12},{12... | collective-permute-start | bytes 1572872 | tf_op jit(solution)/shard_map/ppermute | solution.py:496
  111.7 22.7 %collective-permute-start.25 = (bf16[2,64,2048]{2,1,0:T(8,128)(2,1)}, bf16[2,64,2048]{2,1,0:T(8,128)(2,1)}, u32[]{:S(2)}, u32[]{:S(2)}) collective-permute-start(bf16[2,64,2048]{2,1,0:T(8,128)(2,1)} %get-tuple-element.102), channel_id=1, source_target_pairs={{0,6},{2,0},{4,2},{6,4},{1,7},{3,1},{5,3},{7,5},{8,14},{10,8},{12,... | collective-permute-start | bytes 1572872 | tf_op jit(solution)/shard_map/ppermute | solution.py:496
  114.1 21.9 %collective-permute-start.26 = (bf16[2,64,2048]{2,1,0:T(8,128)(2,1)}, bf16[2,64,2048]{2,1,0:T(8,128)(2,1)S(1)}, u32[]{:S(2)}, u32[]{:S(2)}) collective-permute-start(bf16[2,64,2048]{2,1,0:T(8,128)(2,1)} %get-tuple-element.103), channel_id=1, source_target_pairs={{0,2},{2,4},{4,6},{6,0},{1,3},{3,5},{5,7},{7,1},{8,10},{10,12},{12... | collective-permute-start | bytes 1572872 | tf_op jit(solution)/shard_map/ppermute | solution.py:496
  114.1 21.9 %collective-permute-start.27 = (bf16[2,64,2048]{2,1,0:T(8,128)(2,1)}, bf16[2,64,2048]{2,1,0:T(8,128)(2,1)}, u32[]{:S(2)}, u32[]{:S(2)}) collective-permute-start(bf16[2,64,2048]{2,1,0:T(8,128)(2,1)} %get-tuple-element.104), channel_id=1, source_target_pairs={{0,6},{2,0},{4,2},{6,4},{1,7},{3,1},{5,3},{7,5},{8,14},{10,8},{12,... | collective-permute-start | bytes 1572872 | tf_op jit(solution)/shard_map/ppermute | solution.py:496
  118.2 14.2 %all-to-all-start.2 = ((bf16[8,16,512]{2,1,0:T(8,128)(2,1)}), bf16[8,16,512]{2,1,0:T(8,128)(2,1)S(1)}, u32[]{:S(2)}, u32[]{:S(2)}) async-start(bf16[8,16,512]{2,1,0:T(8,128)(2,1)} %layers.1), calls=%async_computation.2 | async-start | bytes 262144 | tf_op jit(solution)/shard_map/all_to_all | solution.py:508
  132.9 8.2 %collective-permute-start.30 = (bf16[16,4096]{1,0:T(8,128)(2,1)S(1)}, bf16[16,4096]{1,0:T(8,128)(2,1)S(1)}, u32[]{:S(2)}, u32[]{:S(2)}) collective-permute-start(bf16[16,4096]{1,0:T(8,128)(2,1)S(1)} %encoder.1), channel_id=1, source_target_pairs={{0,32},{32,0},{1,33},{33,1},{2,34},{34,2},{3,35},{35,3},{4,36},{36... | collective-permute-start | bytes 393224 | tf_op jit(solution)/shard_map/ppermute | solution.py:563
  137.8 13.0 %collective-permute-start.28 = (bf16[2,64,2048]{2,1,0:T(8,128)(2,1)S(1)}, bf16[2,64,2048]{2,1,0:T(8,128)(2,1)S(1)}, u32[]{:S(2)}, u32[]{:S(2)}) collective-permute-start(bf16[2,64,2048]{2,1,0:T(8,128)(2,1)S(1)} %get-tuple-element.107), channel_id=1, source_target_pairs={{0,2},{2,4},{4,6},{6,0},{1,3},{3,5},{5,7},{7,1},{8,10},{10,12},{12... | collective-permute-start | bytes 1572872 | tf_op jit(solution)/shard_map/ppermute | solution.py:496
  139.1 12.0 %collective-permute-start.29 = (bf16[2,64,2048]{2,1,0:T(8,128)(2,1)S(1)}, bf16[2,64,2048]{2,1,0:T(8,128)(2,1)S(1)}, u32[]{:S(2)}, u32[]{:S(2)}) collective-permute-start(bf16[2,64,2048]{2,1,0:T(8,128)(2,1)S(1)} %get-tuple-element.108), channel_id=1, source_target_pairs={{0,6},{2,0},{4,2},{6,4},{1,7},{3,1},{5,3},{7,5},{8,14},{10,8},{12,... | collective-permute-start | bytes 1572872 | tf_op jit(solution)/shard_map/ppermute | solution.py:496
  141.1 12.5 %collective-permute-start.33 = (bf16[2,16,4096]{2,1,0:T(8,128)(2,1)S(1)}, bf16[2,16,4096]{2,1,0:T(8,128)(2,1)S(1)}, u32[]{:S(2)}, u32[]{:S(2)}) collective-permute-start(bf16[2,16,4096]{2,1,0:T(8,128)(2,1)S(1)} %pad_maximum_fusion.a_ref), channel_id=1, source_target_pairs={{0,64},{64,128},{128,192},{192,0},{1,65},{65,129},{129,193},{193,1... | collective-permute-start | bytes 786440 | tf_op jit(solution)/shard_map/ppermute | solution.py:496
  142.6 11.0 %collective-permute-start.32 = (bf16[2,16,4096]{2,1,0:T(8,128)(2,1)S(1)}, bf16[2,16,4096]{2,1,0:T(8,128)(2,1)S(1)}, u32[]{:S(2)}, u32[]{:S(2)}) collective-permute-start(bf16[2,16,4096]{2,1,0:T(8,128)(2,1)S(1)} %pad_maximum_fusion.a_ref), channel_id=1, source_target_pairs={{0,128},{64,192},{128,0},{192,64},{1,129},{65,193},{129,1},{193,65... | collective-permute-start | bytes 786440 | tf_op jit(solution)/shard_map/ppermute | solution.py:496
  143.6 10.8 %collective-permute-start.31 = (bf16[2,16,4096]{2,1,0:T(8,128)(2,1)S(1)}, bf16[2,16,4096]{2,1,0:T(8,128)(2,1)S(1)}, u32[]{:S(2)}, u32[]{:S(2)}) collective-permute-start(bf16[2,16,4096]{2,1,0:T(8,128)(2,1)S(1)} %pad_maximum_fusion.a_ref), channel_id=1, source_target_pairs={{0,192},{64,0},{128,64},{192,128},{1,193},{65,1},{129,65},{193,129... | collective-permute-start | bytes 786440 | tf_op jit(solution)/shard_map/ppermute | solution.py:496
  (10 other events, 144.7 us)

commit v4 on v3

--- a/solution.py
+++ b/solution.py
@@ -521,15 +521,19 @@
     blocks = memory_blocks(after(hidden, own0), gain)
     quarter = exchange(blocks, ZC).reshape(8, batches, source_n, 128)
     local, own1 = heads(after(queries, blocks), keys, values, head_grad, 1, local)
-    minus0, plus0, weight_m, weight_p, own1, own0_s, quarter = lax.optimization_barrier(
-        (minus0, plus0, weight_m, weight_p, own1, own0_s, quarter)
+    minus0, plus0, own1, own0_s, quarter = lax.optimization_barrier(
+        (minus0, plus0, own1, own0_s, quarter)
     )
+    weight_m, weight_p = lax.optimization_barrier((weight_m, weight_p, minus0))[:2]
 
     far0 = shift(minus0, "zhi", 1)
     plus1 = shift(own1, "zhi", -1)
     weight_2 = shift(after(stacked, weight_m), "x", 2)
+    minus0, plus0 = lax.optimization_barrier((minus0, plus0, weight_m, weight_p))[:2]
     minus0_s, plus0_s, own1_s = swap(minus0), swap(plus0), swap(own1)
-    far0, plus1, quarter = lax.optimization_barrier((far0, plus1, quarter))
+    far0, plus1, quarter, minus0_s, plus0_s = lax.optimization_barrier(
+        (far0, plus1, quarter, minus0_s, plus0_s)
+    )
 
     minus1 = shift(after(own1, far0), "zhi", 1)
     far1 = shift(plus1, "zhi", -1)

time: 156 us -> 156 us (level)
  no operation moved by 1% of the time
where the time goes in v4:
time: 156 us
  starting transfers between devices  74.2 us (48%)
  waiting for transfers between devices  39.9 us (26%)
  Pallas kernels  39.8 us (26%)
    ppermute x24, starting transfers between devices, shift(): return lax.ppermute(value, axis, [(i, (i + step) % 4) for i in range(4)])  44.9 us
    all_to_all x3, starting transfers between devices, exchange(): return lax.all_to_all(value, axes, split_axis=0, concat_axis=0, tiled=True)  22.8 us
    ppermute x24, waiting for transfers between devices, shift(): return lax.ppermute(value, axis, [(i, (i + step) % 4) for i in range(4)])  18.5 us
    all_to_all x3, waiting for transfers between devices, exchange(): return lax.all_to_all(value, axes, split_axis=0, concat_axis=0, tiled=True)  12.5 us
    pallas_call x2, Pallas kernels, return_blocks(): pl.pallas_call(functools.partial(return_kernel, m), in_specs=[HBM] * 12 +...  10.4 us
    pallas_call x2, Pallas kernels, heads(): pl.pallas_call(functools.partial(heads_kernel, m == 0), grid=(1,), in_spe...  9.77 us
    pallas_call x1, Pallas kernels, weight_blocks(): pl.pallas_call(weight_kernel, in_specs=[PIN] * 3, out_specs=[PIN] * 3 + [...  8.06 us
    ppermute x1, waiting for transfers between devices, body(): lax.ppermute(after(local, minus1_s, far1_s), SEC, [(s, s - 1) for s in ra...  7.17 us
  transfers between devices with their start and end apart: 37, of which 14 were waited for; matrix products, arithmetic and copies ran while one was open for 0% of the time, Pallas kernels for 18%

profile of v4, /device:TPU:8, one launch (start us, length us, event | category | flops | bytes accessed | tf_op | source)
XLA Modules:
  0.0 155.8 jit_solution(10099651147230379787)
XLA Ops:
  0.6 5.2 %heads.2 = (bf16[1,2,1,128,2048]{4,3,2,1,0:T(8,128)(2,1)}, bf16[48,4096]{1,0:T(8,128)(2,1)}, bf16[2,128,2048]{2,1,0:T(8,128)(2,1)}) custom-call(bf16[1,2,1,128,2048]{4,3,2,1,0:T(8,128)(2,1)} %q_ref.2, bf16[1,2,1,48,2048]{4,3,2,1,0:T(8,128)(2,1)} %k_ref.3, bf16[1,2,1,48,2048]{4,3,2,1,0:T(8,128)(2,1)} %v_ref.3, bf16[1,2,1,128,2048]{4,3,2,1,0:T(8,128)(2,1)} %g_ref.3, ...), custom_call_target="tpu_custom_call" | custom-call | bytes 41943040 | tf_op jit(solution)/shard_map/heads/pallas_call | solution.py:106
  5.9 2.8 %collective-permute-start.6 = (bf16[2,128,2048]{2,1,0:T(8,128)(2,1)}, bf16[2,128,2048]{2,1,0:T(8,128)(2,1)S(1)}, u32[]{:S(2)}, u32[]{:S(2)}) collective-permute-start(bf16[2,128,2048]{2,1,0:T(8,128)(2,1)} %get-tuple-element.83.refs_0_), channel_id=1, source_target_pairs={{0,6},{2,0},{4,2},{6,4},{1,7},{3,1},{5,3},{7,5},{8,14},{10,8},{12,... | collective-permute-start | bytes 3145736 | tf_op jit(solution)/shard_map/ppermute | solution.py:496
  8.6 6.3 %collective-permute-start.1 = (bf16[48,4096]{1,0:T(8,128)(2,1)}, bf16[48,4096]{1,0:T(8,128)(2,1)}, u32[]{:S(2)}, u32[]{:S(2)}) collective-permute-start(bf16[48,4096]{1,0:T(8,128)(2,1)} %get-tuple-element.64.refs_4_), channel_id=1, source_target_pairs={{0,24},{8,0},{16,8},{24,16},{1,25},{9,1},{17,9},{25,17},{2,26},{10... | collective-permute-start | bytes 1179656 | tf_op jit(solution)/shard_map/ppermute | solution.py:496
  14.9 2.1 %memory.1 = bf16[8,96,128]{2,1,0:T(8,128)(2,1)} custom-call(bf16[96,4096]{1,0:T(8,128)(2,1)} %bitcast.11, f32[1,4096]{1,0:T(1,128)} %bitcast.18), custom_call_target="tpu_custom_call" | custom-call | tf_op jit(solution)/shard_map/memory/pallas_call | solution.py:135
  17.0 5.4 %all-to-all-start = ((bf16[8,96,128]{2,1,0:T(8,128)(2,1)}), bf16[8,96,128]{2,1,0:T(8,128)(2,1)S(1)}, u32[]{:S(2)}, u32[]{:S(2)}) async-start(bf16[8,96,128]{2,1,0:T(8,128)(2,1)} %memory.1), calls=%async_computation | async-start | bytes 393216 | tf_op jit(solution)/shard_map/all_to_all | solution.py:508
  22.4 4.6 %heads.3 = (bf16[1,2,1,128,2048]{4,3,2,1,0:T(8,128)(2,1)}, bf16[48,4096]{1,0:T(8,128)(2,1)}) custom-call(bf16[1,2,1,128,2048]{4,3,2,1,0:T(8,128)(2,1)} %q_ref.2, bf16[1,2,1,48,2048]{4,3,2,1,0:T(8,128)(2,1)} %k_ref.3, bf16[1,2,1,48,2048]{4,3,2,1,0:T(8,128)(2,1)} %v_ref.3, bf16[1,2,1,128,2048]{4,3,2,1,0:T(8,128)(2,1)} %g_ref.3, ...), custom_call_target="tpu_custom_call", output_to_operand_aliasing={{0}: (4, {})} | custom-call | bytes 41943040 | tf_op jit(solution)/shard_map/heads/pallas_call | solution.py:106
  26.9 9.9 %all-to-all-done = bf16[8,96,128]{2,1,0:T(8,128)(2,1)S(1)} async-done(((bf16[8,96,128]{2,1,0:T(8,128)(2,1)}), bf16[8,96,128]{2,1,0:T(8,128)(2,1)S(1)}, u32[]{:S(2)}, u32[]{:S(2)}) %all-to-all-start) | async-done | bytes 196640 | tf_op jit(solution)/shard_map/all_to_all | solution.py:508
  37.0 2.4 %collective-permute-start.11 = (bf16[2,128,2048]{2,1,0:T(8,128)(2,1)S(1)}, bf16[2,128,2048]{2,1,0:T(8,128)(2,1)S(1)}, u32[]{:S(2)}, u32[]{:S(2)}) collective-permute-start(bf16[2,128,2048]{2,1,0:T(8,128)(2,1)S(1)} %copy-done), channel_id=1, source_target_pairs={{0,4},{2,6},{4,0},{6,2},{1,5},{3,7},{5,1},{7,3},{8,12},{10,14},{12... | collective-permute-start | bytes 3145736 | tf_op jit(solution)/shard_map/ppermute | solution.py:496
  39.3 6.2 %collective-permute-start.3 = (bf16[48,4096]{1,0:T(8,128)(2,1)}, bf16[48,4096]{1,0:T(8,128)(2,1)S(1)}, u32[]{:S(2)}, u32[]{:S(2)}) collective-permute-start(bf16[48,4096]{1,0:T(8,128)(2,1)} %collective-permute-done.refs_5_), channel_id=1, source_target_pairs={{0,8},{8,16},{16,24},{24,0},{1,9},{9,17},{17,25},{25,1},{2,10},{10... | collective-permute-start | bytes 1179656 | tf_op jit(solution)/shard_map/ppermute | solution.py:496
  46.0 7.8 %collective-permute-done.3.refs_7_ = bf16[48,4096]{1,0:T(8,128)(2,1)S(1)} collective-permute-done((bf16[48,4096]{1,0:T(8,128)(2,1)}, bf16[48,4096]{1,0:T(8,128)(2,1)S(1)}, u32[]{:S(2)}, u32[]{:S(2)}) %collective-permute-start.3) | collective-permute-done | bytes 393248 | tf_op jit(solution)/shard_map/ppermute | solution.py:496
  56.6 2.9 %collective-permute-start.10 = (bf16[48,4096]{1,0:T(8,128)(2,1)S(1)}, bf16[48,4096]{1,0:T(8,128)(2,1)S(1)}, u32[]{:S(2)}, u32[]{:S(2)}) collective-permute-start(bf16[48,4096]{1,0:T(8,128)(2,1)S(1)} %collective-permute-done.4.refs_6_), channel_id=1, source_target_pairs={{0,24},{8,0},{16,8},{24,16},{1,25},{9,1},{17,9},{25,17},{2,26},{10... | collective-permute-start | bytes 1179656 | tf_op jit(solution)/shard_map/ppermute | solution.py:496
  59.5 1.6 %collective-permute-start.15 = (bf16[8,2,48,128]{3,2,1,0:T(8,128)(2,1)S(1)}, bf16[8,2,48,128]{3,2,1,0:T(8,128)(2,1)S(1)}, u32[]{:S(2)}, u32[]{:S(2)}) collective-permute-start(bf16[8,2,48,128]{3,2,1,0:T(8,128)(2,1)S(1)} %bitcast.13), channel_id=1, source_target_pairs={{0,64},{64,128},{128,192},{192,0},{1,65},{65,129},{129,193},{193,1... | collective-permute-start | bytes 589832 | tf_op jit(solution)/shard_map/ppermute | solution.py:496
  65.5 4.8 %returned.2 = (bf16[8,2,48,512]{3,2,1,0:T(8,128)(2,1)}, bf16[384,512]{1,0:T(8,128)(2,1)}, bf16[2,8,48,2048]{3,2,1,0:T(8,128)(2,1)}) custom-call(bf16[2,128,2048]{2,1,0:T(8,128)(2,1)S(1)} %copy-done, bf16[2,128,2048]{2,1,0:T(8,128)(2,1)S(1)} %collective-permute-done.6.refs_1_, bf16[2,128,2048]{2,1,0:T(8,128)(2,1)S(1)} %collective-permute-done.11.refs_2_, ...), custom_call_target="tpu_custom_call" | custom-call | tf_op jit(solution)/shard_map/returned/pallas_call | solution.py:260
  70.8 2.1 %collective-permute-done.13.refs_1_ = bf16[8,2,48,128]{3,2,1,0:T(8,128)(2,1)S(1)} collective-permute-done((bf16[8,2,48,128]{3,2,1,0:T(8,128)(2,1)S(1)}, bf16[8,2,48,128]{3,2,1,0:T(8,128)(2,1)S(1)}, u32[]{:S(2)}, u32[]{:S(2)}) %collective-permute-start.13) | collective-permute-done | bytes 196640 | tf_op jit(solution)/shard_map/ppermute | solution.py:496
  76.8 5.6 %returned.3 = (bf16[8,2,48,512]{3,2,1,0:T(8,128)(2,1)}, f32[8,512]{1,0:T(8,128)S(1)}, bf16[2,8,48,2048]{3,2,1,0:T(8,128)(2,1)}) custom-call(bf16[2,128,2048]{2,1,0:T(8,128)(2,1)S(1)} %copy-done, bf16[2,128,2048]{2,1,0:T(8,128)(2,1)S(1)} %collective-permute-done.6.refs_1_, ...), custom_call_target="tpu_custom_call", output_to_operand_aliasing={{0}: (14, {})} | custom-call | tf_op jit(solution)/shard_map/returned/pallas_call | solution.py:260
  82.4 12.9 %all-to-all-start.1 = ((bf16[8,2,48,512]{3,2,1,0:T(8,128)(2,1)}), bf16[8,2,48,512]{3,2,1,0:T(8,128)(2,1)S(1)}, u32[]{:S(2)}, u32[]{:S(2)}) async-start(bf16[8,2,48,512]{3,2,1,0:T(8,128)(2,1)} %get-tuple-element.97), calls=%async_computation.1 | async-start | bytes 1572864 | tf_op jit(solution)/shard_map/all_to_all | solution.py:508
  95.2 3.4 %collective-permute-start.18 = (bf16[1,2,1,128,2048]{4,3,2,1,0:T(8,128)(2,1)}, bf16[1,2,1,128,2048]{4,3,2,1,0:T(8,128)(2,1)S(1)}, u32[]{:S(2)}, u32[]{:S(2)}) collective-permute-start(bf16[1,2,1,128,2048]{4,3,2,1,0:T(8,128)(2,1)} %get-tuple-element.93), channel_id=1, source_target_pairs={{32,0},{64,32},{96,64},{128,96},{160,128},{192,160},{224,192},{33,... | collective-permute-start | bytes 3145736 | tf_op jit(solution)/shard_map/ppermute | solution.py:552
  100.1 2.5 %collective-permute-start.22 = (f32[8,512]{1,0:T(8,128)S(1)}, f32[8,512]{1,0:T(8,128)S(1)}, u32[]{:S(2)}, u32[]{:S(2)}) collective-permute-start(f32[8,512]{1,0:T(8,128)S(1)} %get-tuple-element.108.gain0_ref), channel_id=1, source_target_pairs={{0,4},{2,6},{4,0},{6,2},{1,5},{3,7},{5,1},{7,3},{8,12},{10,14},{12... | collective-permute-start | bytes 49160 | tf_op jit(solution)/shard_map/ppermute | solution.py:496
  102.6 8.1 %weights.1 = (bf16[2,128,2048]{2,1,0:T(8,128)(2,1)}, bf16[2,64,2048]{2,1,0:T(8,128)(2,1)}, bf16[2,64,2048]{2,1,0:T(8,128)(2,1)}, bf16[2,64,2048]{2,1,0:T(8,128)(...) custom-call(bf16[512,768]{1,0:T(8,128)(2,1)} %get-tuple-element.98.flip_ref, ...), custom_call_target="tpu_custom_call" | custom-call | tf_op jit(solution)/shard_map/weights/pallas_call | solution.py:301
  111.7 2.3 %collective-permute-start.25 = (bf16[2,64,2048]{2,1,0:T(8,128)(2,1)}, bf16[2,64,2048]{2,1,0:T(8,128)(2,1)}, u32[]{:S(2)}, u32[]{:S(2)}) collective-permute-start(bf16[2,64,2048]{2,1,0:T(8,128)(2,1)} %get-tuple-element.110), channel_id=1, source_target_pairs={{0,6},{2,0},{4,2},{6,4},{1,7},{3,1},{5,3},{7,5},{8,14},{10,8},{12,... | collective-permute-start | bytes 1572872 | tf_op jit(solution)/shard_map/ppermute | solution.py:496
  114.1 3.2 %collective-permute-start.27 = (bf16[2,64,2048]{2,1,0:T(8,128)(2,1)}, bf16[2,64,2048]{2,1,0:T(8,128)(2,1)}, u32[]{:S(2)}, u32[]{:S(2)}) collective-permute-start(bf16[2,64,2048]{2,1,0:T(8,128)(2,1)} %get-tuple-element.112), channel_id=1, source_target_pairs={{0,6},{2,0},{4,2},{6,4},{1,7},{3,1},{5,3},{7,5},{8,14},{10,8},{12,... | collective-permute-start | bytes 1572872 | tf_op jit(solution)/shard_map/ppermute | solution.py:496
  118.2 4.6 %all-to-all-start.2 = ((bf16[8,16,512]{2,1,0:T(8,128)(2,1)}), bf16[8,16,512]{2,1,0:T(8,128)(2,1)S(1)}, u32[]{:S(2)}, u32[]{:S(2)}) async-start(bf16[8,16,512]{2,1,0:T(8,128)(2,1)} %layers.1), calls=%async_computation.2 | async-start | bytes 262144 | tf_op jit(solution)/shard_map/all_to_all | solution.py:508
  122.8 7.2 %collective-permute-done.18.in_ref = bf16[1,2,1,128,2048]{4,3,2,1,0:T(8,128)(2,1)S(1)} collective-permute-done((bf16[1,2,1,128,2048]{4,3,2,1,0:T(8,128)(2,1)}, bf16[1,2,1,128,2048]{4,3,2,1,0:T(8,128)(2,1)S(1)}, u32[]{:S(2)}, u32[]{:S(2)}) %collective-permute-start.18) | collective-permute-done | bytes 1048608 | tf_op jit(solution)/shard_map/ppermute | solution.py:552
  130.0 2.5 %all-to-all-done.2.own_ref = bf16[8,16,512]{2,1,0:T(8,128)(2,1)S(1)} async-done(((bf16[8,16,512]{2,1,0:T(8,128)(2,1)}), bf16[8,16,512]{2,1,0:T(8,128)(2,1)S(1)}, u32[]{:S(2)}, u32[]{:S(2)}) %all-to-all-start.2) | async-done | bytes 131104 | tf_op jit(solution)/shard_map/all_to_all | solution.py:508
  132.9 1.6 collective-permute-start.30
  134.4 1.5 collective-permute-done.26.refs_2_
  136.0 1.8 %relay.1 = (bf16[2,64,2048]{2,1,0:T(8,128)(2,1)S(1)}, bf16[2,64,2048]{2,1,0:T(8,128)(2,1)S(1)}) custom-call(bf16[2,64,2048]{2,1,0:T(8,128)(2,1)} %get-tuple-element.102.sum_p, bf16[2,64,2048]{2,1,0:T(8,128)(2,1)} %get-tuple-element.103.sum_m, bf16[2,64,2048]{2,1,0:T(8,128)(2,1)} %collective-permute-done.24.far_p, ...), custom_call_target="tpu_custom_call" | custom-call | tf_op jit(solution)/shard_map/relay/pallas_call | solution.py:327
  139.1 2.0 %collective-permute-start.29 = (bf16[2,64,2048]{2,1,0:T(8,128)(2,1)S(1)}, bf16[2,64,2048]{2,1,0:T(8,128)(2,1)S(1)}, u32[]{:S(2)}, u32[]{:S(2)}) collective-permute-start(bf16[2,64,2048]{2,1,0:T(8,128)(2,1)S(1)} %get-tuple-element.116), channel_id=1, source_target_pairs={{0,6},{2,0},{4,2},{6,4},{1,7},{3,1},{5,3},{7,5},{8,14},{10,8},{12,... | collective-permute-start | bytes 1572872 | tf_op jit(solution)/shard_map/ppermute | solution.py:496
  141.1 1.5 collective-permute-start.33
  143.6 2.5 %collective-permute-start.31 = (bf16[2,16,4096]{2,1,0:T(8,128)(2,1)S(1)}, bf16[2,16,4096]{2,1,0:T(8,128)(2,1)S(1)}, u32[]{:S(2)}, u32[]{:S(2)}) collective-permute-start(bf16[2,16,4096]{2,1,0:T(8,128)(2,1)S(1)} %pad_maximum_fusion.a_ref), channel_id=1, source_target_pairs={{0,192},{64,0},{128,64},{192,128},{1,193},{65,1},{129,65},{193,129... | collective-permute-start | bytes 786440 | tf_op jit(solution)/shard_map/ppermute | solution.py:496
  147.2 3.5 %collective-permute-done.28.refs_0_ = bf16[2,64,2048]{2,1,0:T(8,128)(2,1)S(1)} collective-permute-done((bf16[2,64,2048]{2,1,0:T(8,128)(2,1)S(1)}, bf16[2,64,2048]{2,1,0:T(8,128)(2,1)S(1)}, u32[]{:S(2)}, u32[]{:S(2)}) %collective-permute-start.28) | collective-permute-done | bytes 524320 | tf_op jit(solution)/shard_map/ppermute | solution.py:496
  151.0 2.6 %add.1 = (bf16[128,2048]{1,0:T(8,128)(2,1)}, bf16[128,2048]{1,0:T(8,128)(2,1)}) custom-call(bf16[2,128,2048]{2,1,0:T(8,128)(2,1)} %get-tuple-element.101.own_ref, bf16[2,64,2048]{2,1,0:T(8,128)(2,1)S(1)} %collective-permute-done.28.refs_0_, bf16[2,64,2048]{2,1,0:T(8,128)(2,1)S(1)} %collective-permute-done.29.refs_1_, ...), custom_call_target="tpu_custom_call" | custom-call | tf_op jit(solution)/shard_map/add/pallas_call | solution.py:461
  (66 shorter events, 21.8 us)
Async XLA Ops:
  5.9 31.1 %collective-permute-start.6 = (bf16[2,128,2048]{2,1,0:T(8,128)(2,1)}, bf16[2,128,2048]{2,1,0:T(8,128)(2,1)S(1)}, u32[]{:S(2)}, u32[]{:S(2)}) collective-permute-start(bf16[2,128,2048]{2,1,0:T(8,128)(2,1)} %get-tuple-element.83.refs_0_), channel_id=1, source_target_pairs={{0,6},{2,0},{4,2},{6,4},{1,7},{3,1},{5,3},{7,5},{8,14},{10,8},{12,... | collective-permute-start | bytes 3145736 | tf_op jit(solution)/shard_map/ppermute | solution.py:496
  8.6 28.3 %collective-permute-start.5 = (bf16[2,128,2048]{2,1,0:T(8,128)(2,1)}, bf16[2,128,2048]{2,1,0:T(8,128)(2,1)S(1)}, u32[]{:S(2)}, u32[]{:S(2)}) collective-permute-start(bf16[2,128,2048]{2,1,0:T(8,128)(2,1)} %get-tuple-element.83.refs_0_), channel_id=1, source_target_pairs={{0,2},{2,4},{4,6},{6,0},{1,3},{3,5},{5,7},{7,1},{8,10},{10,12},{12... | collective-permute-start | bytes 3145736 | tf_op jit(solution)/shard_map/ppermute | solution.py:496
  8.6 28.3 %collective-permute-start.2 = (bf16[48,4096]{1,0:T(8,128)(2,1)}, bf16[48,4096]{1,0:T(8,128)(2,1)}, u32[]{:S(2)}, u32[]{:S(2)}) collective-permute-start(bf16[48,4096]{1,0:T(8,128)(2,1)} %get-tuple-element.64.refs_4_), channel_id=1, source_target_pairs={{0,1},{1,0},{2,3},{3,2},{4,5},{5,4},{6,7},{7,6},{8,9},{9,8},{10,11... | collective-permute-start | bytes 1179656 | tf_op jit(solution)/shard_map/ppermute | solution.py:500
  8.6 28.3 %collective-permute-start.1 = (bf16[48,4096]{1,0:T(8,128)(2,1)}, bf16[48,4096]{1,0:T(8,128)(2,1)}, u32[]{:S(2)}, u32[]{:S(2)}) collective-permute-start(bf16[48,4096]{1,0:T(8,128)(2,1)} %get-tuple-element.64.refs_4_), channel_id=1, source_target_pairs={{0,24},{8,0},{16,8},{24,16},{1,25},{9,1},{17,9},{25,17},{2,26},{10... | collective-permute-start | bytes 1179656 | tf_op jit(solution)/shard_map/ppermute | solution.py:496
  14.9 22.0 %collective-permute-start = (bf16[48,4096]{1,0:T(8,128)(2,1)}, bf16[48,4096]{1,0:T(8,128)(2,1)}, u32[]{:S(2)}, u32[]{:S(2)}) collective-permute-start(bf16[48,4096]{1,0:T(8,128)(2,1)} %get-tuple-element.64.refs_4_), channel_id=1, source_target_pairs={{0,8},{8,16},{16,24},{24,0},{1,9},{9,17},{17,25},{25,1},{2,10},{10... | collective-permute-start | bytes 1179656 | tf_op jit(solution)/shard_map/ppermute | solution.py:496
  17.0 19.9 %all-to-all-start = ((bf16[8,96,128]{2,1,0:T(8,128)(2,1)}), bf16[8,96,128]{2,1,0:T(8,128)(2,1)S(1)}, u32[]{:S(2)}, u32[]{:S(2)}) async-start(bf16[8,96,128]{2,1,0:T(8,128)(2,1)} %memory.1), calls=%async_computation | async-start | bytes 393216 | tf_op jit(solution)/shard_map/all_to_all | solution.py:508
  37.0 26.2 %collective-permute-start.11 = (bf16[2,128,2048]{2,1,0:T(8,128)(2,1)S(1)}, bf16[2,128,2048]{2,1,0:T(8,128)(2,1)S(1)}, u32[]{:S(2)}, u32[]{:S(2)}) collective-permute-start(bf16[2,128,2048]{2,1,0:T(8,128)(2,1)S(1)} %copy-done), channel_id=1, source_target_pairs={{0,4},{2,6},{4,0},{6,2},{1,5},{3,7},{5,1},{7,3},{8,12},{10,14},{12... | collective-permute-start | bytes 3145736 | tf_op jit(solution)/shard_map/ppermute | solution.py:496
  39.3 14.5 %collective-permute-start.3 = (bf16[48,4096]{1,0:T(8,128)(2,1)}, bf16[48,4096]{1,0:T(8,128)(2,1)S(1)}, u32[]{:S(2)}, u32[]{:S(2)}) collective-permute-start(bf16[48,4096]{1,0:T(8,128)(2,1)} %collective-permute-done.refs_5_), channel_id=1, source_target_pairs={{0,8},{8,16},{16,24},{24,0},{1,9},{9,17},{17,25},{25,1},{2,10},{10... | collective-permute-start | bytes 1179656 | tf_op jit(solution)/shard_map/ppermute | solution.py:496
  45.5 9.6 %collective-permute-start.4 = (bf16[48,4096]{1,0:T(8,128)(2,1)}, bf16[48,4096]{1,0:T(8,128)(2,1)S(1)}, u32[]{:S(2)}, u32[]{:S(2)}) collective-permute-start(bf16[48,4096]{1,0:T(8,128)(2,1)} %get-tuple-element.80.refs_4_), channel_id=1, source_target_pairs={{0,24},{8,0},{16,8},{24,16},{1,25},{9,1},{17,9},{25,17},{2,26},{10... | collective-permute-start | bytes 1179656 | tf_op jit(solution)/shard_map/ppermute | solution.py:496
  45.5 9.6 %collective-permute-start.7 = (bf16[48,4096]{1,0:T(8,128)(2,1)}, bf16[48,4096]{1,0:T(8,128)(2,1)S(1)}, u32[]{:S(2)}, u32[]{:S(2)}) collective-permute-start(bf16[48,4096]{1,0:T(8,128)(2,1)} %collective-permute-done.refs_5_), channel_id=1, source_target_pairs={{0,1},{1,0},{2,3},{3,2},{4,5},{5,4},{6,7},{7,6},{8,9},{9,8},{10,11... | collective-permute-start | bytes 1179656 | tf_op jit(solution)/shard_map/ppermute | solution.py:500
  45.5 9.6 %collective-permute-start.8 = (bf16[48,4096]{1,0:T(8,128)(2,1)}, bf16[48,4096]{1,0:T(8,128)(2,1)S(1)}, u32[]{:S(2)}, u32[]{:S(2)}) collective-permute-start(bf16[48,4096]{1,0:T(8,128)(2,1)} %collective-permute-done.1.refs_6_), channel_id=1, source_target_pairs={{0,1},{1,0},{2,3},{3,2},{4,5},{5,4},{6,7},{7,6},{8,9},{9,8},{10,11... | collective-permute-start | bytes 1179656 | tf_op jit(solution)/shard_map/ppermute | solution.py:500
  55.1 19.3 %collective-permute-start.9 = (bf16[48,4096]{1,0:T(8,128)(2,1)}, bf16[48,4096]{1,0:T(8,128)(2,1)S(1)}, u32[]{:S(2)}, u32[]{:S(2)}) collective-permute-start(bf16[48,4096]{1,0:T(8,128)(2,1)} %get-tuple-element.80.refs_4_), channel_id=1, source_target_pairs={{0,8},{8,16},{16,24},{24,0},{1,9},{9,17},{17,25},{25,1},{2,10},{10... | collective-permute-start | bytes 1179656 | tf_op jit(solution)/shard_map/ppermute | solution.py:496
  56.6 17.8 %collective-permute-start.10 = (bf16[48,4096]{1,0:T(8,128)(2,1)S(1)}, bf16[48,4096]{1,0:T(8,128)(2,1)S(1)}, u32[]{:S(2)}, u32[]{:S(2)}) collective-permute-start(bf16[48,4096]{1,0:T(8,128)(2,1)S(1)} %collective-permute-done.4.refs_6_), channel_id=1, source_target_pairs={{0,24},{8,0},{16,8},{24,16},{1,25},{9,1},{17,9},{25,17},{2,26},{10... | collective-permute-start | bytes 1179656 | tf_op jit(solution)/shard_map/ppermute | solution.py:496
  59.5 10.7 %collective-permute-start.15 = (bf16[8,2,48,128]{3,2,1,0:T(8,128)(2,1)S(1)}, bf16[8,2,48,128]{3,2,1,0:T(8,128)(2,1)S(1)}, u32[]{:S(2)}, u32[]{:S(2)}) collective-permute-start(bf16[8,2,48,128]{3,2,1,0:T(8,128)(2,1)S(1)} %bitcast.13), channel_id=1, source_target_pairs={{0,64},{64,128},{128,192},{192,0},{1,65},{65,129},{129,193},{193,1... | collective-permute-start | bytes 589832 | tf_op jit(solution)/shard_map/ppermute | solution.py:496
  61.1 9.3 %collective-permute-start.14 = (bf16[8,2,48,128]{3,2,1,0:T(8,128)(2,1)S(1)}, bf16[8,2,48,128]{3,2,1,0:T(8,128)(2,1)S(1)}, u32[]{:S(2)}, u32[]{:S(2)}) collective-permute-start(bf16[8,2,48,128]{3,2,1,0:T(8,128)(2,1)S(1)} %bitcast.14), channel_id=1, source_target_pairs={{0,128},{64,192},{128,0},{192,64},{1,129},{65,193},{129,1},{193,65... | collective-permute-start | bytes 589832 | tf_op jit(solution)/shard_map/ppermute | solution.py:496
  63.2 9.7 %collective-permute-start.13 = (bf16[8,2,48,128]{3,2,1,0:T(8,128)(2,1)S(1)}, bf16[8,2,48,128]{3,2,1,0:T(8,128)(2,1)S(1)}, u32[]{:S(2)}, u32[]{:S(2)}) collective-permute-start(bf16[8,2,48,128]{3,2,1,0:T(8,128)(2,1)S(1)} %bitcast.15), channel_id=1, source_target_pairs={{0,192},{64,0},{128,64},{192,128},{1,193},{65,1},{129,65},{193,129... | collective-permute-start | bytes 589832 | tf_op jit(solution)/shard_map/ppermute | solution.py:496
  82.4 34.9 %all-to-all-start.1 = ((bf16[8,2,48,512]{3,2,1,0:T(8,128)(2,1)}), bf16[8,2,48,512]{3,2,1,0:T(8,128)(2,1)S(1)}, u32[]{:S(2)}, u32[]{:S(2)}) async-start(bf16[8,2,48,512]{3,2,1,0:T(8,128)(2,1)} %get-tuple-element.97), calls=%async_computation.1 | async-start | bytes 1572864 | tf_op jit(solution)/shard_map/all_to_all | solution.py:508
  95.2 34.7 %collective-permute-start.18 = (bf16[1,2,1,128,2048]{4,3,2,1,0:T(8,128)(2,1)}, bf16[1,2,1,128,2048]{4,3,2,1,0:T(8,128)(2,1)S(1)}, u32[]{:S(2)}, u32[]{:S(2)}) collective-permute-start(bf16[1,2,1,128,2048]{4,3,2,1,0:T(8,128)(2,1)} %get-tuple-element.93), channel_id=1, source_target_pairs={{32,0},{64,32},{96,64},{128,96},{160,128},{192,160},{224,192},{33,... | collective-permute-start | bytes 3145736 | tf_op jit(solution)/shard_map/ppermute | solution.py:552
  98.6 12.0 %collective-permute-start.23 = (f32[8,512]{1,0:T(8,128)S(1)}, f32[8,512]{1,0:T(8,128)S(1)}, u32[]{:S(2)}, u32[]{:S(2)}) collective-permute-start(f32[8,512]{1,0:T(8,128)S(1)} %get-tuple-element.108.gain0_ref), channel_id=1, source_target_pairs={{0,6},{2,0},{4,2},{6,4},{1,7},{3,1},{5,3},{7,5},{8,14},{10,8},{12,... | collective-permute-start | bytes 49160 | tf_op jit(solution)/shard_map/ppermute | solution.py:496
  100.1 10.6 %collective-permute-start.22 = (f32[8,512]{1,0:T(8,128)S(1)}, f32[8,512]{1,0:T(8,128)S(1)}, u32[]{:S(2)}, u32[]{:S(2)}) collective-permute-start(f32[8,512]{1,0:T(8,128)S(1)} %get-tuple-element.108.gain0_ref), channel_id=1, source_target_pairs={{0,4},{2,6},{4,0},{6,2},{1,5},{3,7},{5,1},{7,3},{8,12},{10,14},{12... | collective-permute-start | bytes 49160 | tf_op jit(solution)/shard_map/ppermute | solution.py:496
  102.5 8.1 %collective-permute-start.21 = (f32[8,512]{1,0:T(8,128)S(1)}, f32[8,512]{1,0:T(8,128)S(1)}, u32[]{:S(2)}, u32[]{:S(2)}) collective-permute-start(f32[8,512]{1,0:T(8,128)S(1)} %get-tuple-element.108.gain0_ref), channel_id=1, source_target_pairs={{0,2},{2,4},{4,6},{6,0},{1,3},{3,5},{5,7},{7,1},{8,10},{10,12},{12... | collective-permute-start | bytes 49160 | tf_op jit(solution)/shard_map/ppermute | solution.py:496
  110.7 23.8 %collective-permute-start.24 = (bf16[2,64,2048]{2,1,0:T(8,128)(2,1)}, bf16[2,64,2048]{2,1,0:T(8,128)(2,1)}, u32[]{:S(2)}, u32[]{:S(2)}) collective-permute-start(bf16[2,64,2048]{2,1,0:T(8,128)(2,1)} %get-tuple-element.109), channel_id=1, source_target_pairs={{0,2},{2,4},{4,6},{6,0},{1,3},{3,5},{5,7},{7,1},{8,10},{10,12},{12... | collective-permute-start | bytes 1572872 | tf_op jit(solution)/shard_map/ppermute | solution.py:496
  111.7 22.7 %collective-permute-start.25 = (bf16[2,64,2048]{2,1,0:T(8,128)(2,1)}, bf16[2,64,2048]{2,1,0:T(8,128)(2,1)}, u32[]{:S(2)}, u32[]{:S(2)}) collective-permute-start(bf16[2,64,2048]{2,1,0:T(8,128)(2,1)} %get-tuple-element.110), channel_id=1, source_target_pairs={{0,6},{2,0},{4,2},{6,4},{1,7},{3,1},{5,3},{7,5},{8,14},{10,8},{12,... | collective-permute-start | bytes 1572872 | tf_op jit(solution)/shard_map/ppermute | solution.py:496
  114.1 21.9 %collective-permute-start.26 = (bf16[2,64,2048]{2,1,0:T(8,128)(2,1)}, bf16[2,64,2048]{2,1,0:T(8,128)(2,1)S(1)}, u32[]{:S(2)}, u32[]{:S(2)}) collective-permute-start(bf16[2,64,2048]{2,1,0:T(8,128)(2,1)} %get-tuple-element.111), channel_id=1, source_target_pairs={{0,2},{2,4},{4,6},{6,0},{1,3},{3,5},{5,7},{7,1},{8,10},{10,12},{12... | collective-permute-start | bytes 1572872 | tf_op jit(solution)/shard_map/ppermute | solution.py:496
  114.1 21.9 %collective-permute-start.27 = (bf16[2,64,2048]{2,1,0:T(8,128)(2,1)}, bf16[2,64,2048]{2,1,0:T(8,128)(2,1)}, u32[]{:S(2)}, u32[]{:S(2)}) collective-permute-start(bf16[2,64,2048]{2,1,0:T(8,128)(2,1)} %get-tuple-element.112), channel_id=1, source_target_pairs={{0,6},{2,0},{4,2},{6,4},{1,7},{3,1},{5,3},{7,5},{8,14},{10,8},{12,... | collective-permute-start | bytes 1572872 | tf_op jit(solution)/shard_map/ppermute | solution.py:496
  118.2 14.2 %all-to-all-start.2 = ((bf16[8,16,512]{2,1,0:T(8,128)(2,1)}), bf16[8,16,512]{2,1,0:T(8,128)(2,1)S(1)}, u32[]{:S(2)}, u32[]{:S(2)}) async-start(bf16[8,16,512]{2,1,0:T(8,128)(2,1)} %layers.1), calls=%async_computation.2 | async-start | bytes 262144 | tf_op jit(solution)/shard_map/all_to_all | solution.py:508
  132.9 8.2 %collective-permute-start.30 = (bf16[16,4096]{1,0:T(8,128)(2,1)S(1)}, bf16[16,4096]{1,0:T(8,128)(2,1)S(1)}, u32[]{:S(2)}, u32[]{:S(2)}) collective-permute-start(bf16[16,4096]{1,0:T(8,128)(2,1)S(1)} %encoder.1), channel_id=1, source_target_pairs={{0,32},{32,0},{1,33},{33,1},{2,34},{34,2},{3,35},{35,3},{4,36},{36... | collective-permute-start | bytes 393224 | tf_op jit(solution)/shard_map/ppermute | solution.py:567
  137.8 13.0 %collective-permute-start.28 = (bf16[2,64,2048]{2,1,0:T(8,128)(2,1)S(1)}, bf16[2,64,2048]{2,1,0:T(8,128)(2,1)S(1)}, u32[]{:S(2)}, u32[]{:S(2)}) collective-permute-start(bf16[2,64,2048]{2,1,0:T(8,128)(2,1)S(1)} %get-tuple-element.115), channel_id=1, source_target_pairs={{0,2},{2,4},{4,6},{6,0},{1,3},{3,5},{5,7},{7,1},{8,10},{10,12},{12... | collective-permute-start | bytes 1572872 | tf_op jit(solution)/shard_map/ppermute | solution.py:496
  139.1 12.0 %collective-permute-start.29 = (bf16[2,64,2048]{2,1,0:T(8,128)(2,1)S(1)}, bf16[2,64,2048]{2,1,0:T(8,128)(2,1)S(1)}, u32[]{:S(2)}, u32[]{:S(2)}) collective-permute-start(bf16[2,64,2048]{2,1,0:T(8,128)(2,1)S(1)} %get-tuple-element.116), channel_id=1, source_target_pairs={{0,6},{2,0},{4,2},{6,4},{1,7},{3,1},{5,3},{7,5},{8,14},{10,8},{12,... | collective-permute-start | bytes 1572872 | tf_op jit(solution)/shard_map/ppermute | solution.py:496
  141.1 12.5 %collective-permute-start.33 = (bf16[2,16,4096]{2,1,0:T(8,128)(2,1)S(1)}, bf16[2,16,4096]{2,1,0:T(8,128)(2,1)S(1)}, u32[]{:S(2)}, u32[]{:S(2)}) collective-permute-start(bf16[2,16,4096]{2,1,0:T(8,128)(2,1)S(1)} %pad_maximum_fusion.a_ref), channel_id=1, source_target_pairs={{0,64},{64,128},{128,192},{192,0},{1,65},{65,129},{129,193},{193,1... | collective-permute-start | bytes 786440 | tf_op jit(solution)/shard_map/ppermute | solution.py:496
  142.6 11.0 %collective-permute-start.32 = (bf16[2,16,4096]{2,1,0:T(8,128)(2,1)S(1)}, bf16[2,16,4096]{2,1,0:T(8,128)(2,1)S(1)}, u32[]{:S(2)}, u32[]{:S(2)}) collective-permute-start(bf16[2,16,4096]{2,1,0:T(8,128)(2,1)S(1)} %pad_maximum_fusion.a_ref), channel_id=1, source_target_pairs={{0,128},{64,192},{128,0},{192,64},{1,129},{65,193},{129,1},{193,65... | collective-permute-start | bytes 786440 | tf_op jit(solution)/shard_map/ppermute | solution.py:496
  143.6 10.8 %collective-permute-start.31 = (bf16[2,16,4096]{2,1,0:T(8,128)(2,1)S(1)}, bf16[2,16,4096]{2,1,0:T(8,128)(2,1)S(1)}, u32[]{:S(2)}, u32[]{:S(2)}) collective-permute-start(bf16[2,16,4096]{2,1,0:T(8,128)(2,1)S(1)} %pad_maximum_fusion.a_ref), channel_id=1, source_target_pairs={{0,192},{64,0},{128,64},{192,128},{1,193},{65,1},{129,65},{193,129... | collective-permute-start | bytes 786440 | tf_op jit(solution)/shard_map/ppermute | solution.py:496
  (10 other events, 144.7 us)
